TPU v7x, 1024 devices: a whole 8x8x8 slice. The times are simulated.
1024 devices in a mesh: grp: 16 (over z, core), dev: 64 (over y, x).
Axes of the slice: x: 8, y: 8, z: 8, core: 2. Of those that a mesh axis runs over, the one named last changes fastest.
Arguments:
- atm_state: float32 [16, 64, 128, 1024], P('grp', 'dev'), may hold values from -6 to 6
- atm_nbrs: int32 [16, 64, 4, 1024], P('grp', 'dev'), may hold values from 0 to 1279
- atm_send: int32 [16, 64, 256], P('grp', 'dev'), may hold values from 0 to 1023
- atm_mix: float32 [16, 64, 1024], P('grp', 'dev'), may hold values from 0.2 to 0.6
- flux_weight: float32 [24, 128], replicated, may hold values from -0.5 to 0.5
- margin_counts: int32 [16, 64, 1024], P('grp', 'dev'), may hold values from 1 to 4, 1536 in all within a row
- margin_weight: float32 [16, 64, 1536], P('grp', 'dev'), may hold values from 0.05 to 1
- block_owner: int32 [16, 64, 12, 1], P('grp', 'dev'), may hold values from 0 to 7, as said below
- recv_cols: int32 [16, 64, 8, 4, 128], P('grp', 'dev'), may hold values from 0 to 2047
- ocn_state: float32 [16, 64, 80, 2048], P('grp', 'dev'), may hold values from -6 to 6
- ocn_nbrs: int32 [16, 64, 6, 2048], P('grp', 'dev'), may hold values from 0 to 2303
- ocn_send: int32 [16, 64, 256], P('grp', 'dev'), may hold values from 0 to 2047
- ocn_mix: float32 [16, 64, 2048], P('grp', 'dev'), may hold values from 0.1 to 0.4
- force_weight: float32 [80, 24], replicated, may hold values from -1.25 to 1.25
- ret_weight: float32 [12, 80], replicated, may hold values from -0.625 to 0.625
Outputs:
- atm_next: float32 [16, 64, 128, 1024], P('grp', 'dev')
- ocn_next: float32 [16, 64, 80, 2048], P('grp', 'dev')
- atm_remapped: float32 [16, 64, 12, 1024], P('grp', 'dev')
Inputs may be any that keep to these rules, and one draw needn't show every extreme that they name: `margin_counts`: the 1024 counts of one partition sum to 1536, and one of them equals 4. `block_owner`: no partition sends more than 4 of its 12 blocks to one ocean group, and every partition sends exactly 4 blocks to one of them.
All inputs are finite; a program needn't handle non-finite values.
Results may differ from a plain program's by a relative error of at most 0.0029.
Values may be sent and summed in bfloat16 or wider, within the bound.
No kernel may reach another device: no remote copies, remote signals or barrier semaphores. Data moves between devices by JAX's collectives and lax.ppermute only.
A program may use at most 32 MiB of HBM per device.

v0:
```python
import jax
import jax.numpy as jnp
from jax import lax
from jax.sharding import PartitionSpec as P

EXACT_DOT = lax.Precision.HIGHEST


def extended_2(shard, sides, width):
    for axis, dim in sides:
        peers, length = (lax.axis_size(axis), shard.shape[dim])
        up = [(i, (i + 1) % peers) for i in range(peers)]
        down = [(j, i) for i, j in up]
        last = lax.slice_in_dim(shard, length - width, length, axis=dim)
        leading = lax.slice_in_dim(shard, 0, width, axis=dim)
        before = lax.ppermute(last, axis, up)
        after = lax.ppermute(leading, axis, down)
        shard = jnp.concatenate([before, shard, after], axis=dim)
    return shard


def stencil(state, pool, neighbours, mixing):
    total = jnp.take(pool, neighbours[0], axis=1)
    for which in range(1, neighbours.shape[0]):
        total = total + jnp.take(pool, neighbours[which], axis=1)
    return state + mixing[None, :] * (total / neighbours.shape[0] - state)


def block_slots(owner):
    order = jnp.arange(owner.shape[0], dtype=jnp.int32)
    earlier = (owner[None, :] == owner[:, None]) & (order[None, :] < order[:, None])
    return jnp.sum(earlier.astype(jnp.int32), axis=1)


def with_rims(state, extended, half):
    return jnp.concatenate([state, extended[:, :half], extended[:, 3 * half :]], axis=1)


def on_device(
    atm_state,
    atm_nbrs,
    atm_send,
    atm_mix,
    flux_weight,
    margin_counts,
    margin_weight,
    block_owner,
    recv_cols,
    ocn_state,
    ocn_nbrs,
    ocn_send,
    ocn_mix,
    force_weight,
    ret_weight,
):
    atmosphere = atm_state[0, 0]
    ocean = ocn_state[0, 0]
    half = atm_send.shape[2] // 2
    levels_air = atmosphere.shape[0]
    groups = lax.axis_size("grp")
    atm_groups = recv_cols.shape[2]
    group = lax.axis_index("grp")
    air_here = group < atm_groups
    air_packed = jnp.take(atmosphere, atm_send[0, 0], axis=1)
    sea_packed = jnp.take(ocean, ocn_send[0, 0], axis=1)
    both_ext = extended_2(
        jnp.concatenate([air_packed, sea_packed], axis=0).astype(jnp.bfloat16), (("dev", 1),), half
    ).astype(jnp.float32)
    air_ext = both_ext[:levels_air]
    sea_ext = both_ext[levels_air:]
    atm_next = lax.cond(
        air_here,
        lambda: stencil(
            atmosphere, with_rims(atmosphere, air_ext, half), atm_nbrs[0, 0], atm_mix[0, 0]
        ),
        lambda: atmosphere,
    )
    ocn_base = lax.cond(
        air_here,
        lambda: ocean,
        lambda: stencil(ocean, with_rims(ocean, sea_ext, half), ocn_nbrs[0, 0], ocn_mix[0, 0]),
    )
    capacity = recv_cols.shape[3]
    block = recv_cols.shape[4]
    columns = atmosphere.shape[1]
    row_count = margin_weight.shape[2]
    blocks_here = block_owner.shape[2]
    fields = flux_weight.shape[0]
    ret_fields = ret_weight.shape[0]
    cells = ocean.shape[1]
    column = jnp.repeat(
        jnp.arange(columns, dtype=jnp.int32), margin_counts[0, 0], total_repeat_length=row_count
    )
    weights = margin_weight[0, 0]
    fluxes = jnp.dot(flux_weight, atm_next, precision=EXACT_DOT)
    row_values = (jnp.take(fluxes, column, axis=1) * weights[None, :]).astype(jnp.bfloat16)
    outgoing = row_values.reshape(fields, blocks_here, block).transpose(1, 0, 2)
    owner = block_owner[0, 0, :, 0]
    slot = block_slots(owner)
    cell_index = recv_cols[0, 0].reshape(-1)
    returned = jnp.dot(ret_weight, ocean, precision=EXACT_DOT).astype(jnp.bfloat16)
    looked = (
        jnp.take(returned, cell_index, axis=1)
        .reshape(ret_fields, atm_groups, capacity, block)
        .transpose(1, 2, 0, 3)
    )
    upward = (
        jnp.zeros((groups, capacity, fields, block), jnp.bfloat16)
        .at[atm_groups + owner, slot]
        .set(outgoing)
    )
    padded = jnp.pad(looked, ((0, 0), (0, 0), (0, fields - ret_fields), (0, 0)))
    combined = jnp.concatenate([padded, upward[atm_groups:]], axis=0)
    arrived = lax.all_to_all(combined, "grp", split_axis=0, concat_axis=0, tiled=True)
    from_air = arrived[:atm_groups]
    from_owners = arrived[atm_groups:, :, :ret_fields]
    sea_side = (group >= atm_groups).astype(jnp.float32)
    air_side = 1.0 - sea_side
    incoming = from_air.transpose(2, 0, 1, 3).reshape(fields, -1).astype(jnp.float32)
    cell_flux = jnp.zeros((fields, cells), jnp.float32).at[:, cell_index].add(incoming)
    forcing = jnp.dot(force_weight, cell_flux, precision=EXACT_DOT)
    ocn_next = ocn_base + sea_side * forcing
    mine = (
        from_owners[owner, slot]
        .transpose(1, 0, 2)
        .reshape(ret_fields, row_count)
        .astype(jnp.float32)
    )
    weighted = (
        jnp.zeros((ret_fields, columns), jnp.float32).at[:, column].add(mine * weights[None, :])
    )
    weight_sum = jnp.zeros((columns,), jnp.float32).at[column].add(weights)
    remapped = air_side * (weighted / weight_sum[None, :])
    return (atm_next[None, None], ocn_next[None, None], remapped[None, None])


def solution(mesh):
    in_specs = (
        P("grp", "dev", None, None),
        P("grp", "dev", None, None),
        P("grp", "dev", None),
        P("grp", "dev", None),
        P(),
        P("grp", "dev", None),
        P("grp", "dev", None),
        P("grp", "dev", None, None),
        P("grp", "dev", None, None, None),
        P("grp", "dev", None, None),
        P("grp", "dev", None, None),
        P("grp", "dev", None),
        P("grp", "dev", None),
        P(),
        P(),
    )
    out_specs = (
        P("grp", "dev", None, None),
        P("grp", "dev", None, None),
        P("grp", "dev", None, None),
    )
    return jax.shard_map(
        on_device, mesh=mesh, in_specs=in_specs, out_specs=out_specs, check_vma=False
    )
```

profile of v0, /device:TPU:513, one launch (start us, length us, event | category | flops | bytes accessed | tf_op | source)
XLA Modules:
  0.0 181.4 jit_solution(10166330802363438879)
XLA Ops:
  0.7 1.3 copy.46
  3.8 0.7 gather_fusion.10
  4.6 0.7 gather_fusion.11
  6.1 8.2 %collective-permute-start.1 = (bf16[208,128]{0,1:T(8,128)(2,1)}, bf16[208,128]{0,1:T(8,128)(2,1)S(1)}, u32[]{:S(2)}, u32[]{:S(2)}) collective-permute-start(bf16[208,128]{0,1:T(8,128)(2,1)} %get-tuple-element.114), channel_id=1, source_target_pairs={{1,0},{2,1},{3,2},{4,3},{5,4},{6,5},{7,6},{8,7},{9,8},{10,9},{11,1... | collective-permute-start | bytes 159752 | tf_op jit(solution)/shard_map/ppermute | solution.py:17
  14.3 1.9 %collective-permute-start = (bf16[208,128]{0,1:T(8,128)(2,1)}, bf16[208,128]{0,1:T(8,128)(2,1)}, u32[]{:S(2)}, u32[]{:S(2)}) collective-permute-start(bf16[208,128]{0,1:T(8,128)(2,1)} %get-tuple-element.113), channel_id=1, source_target_pairs={{0,1},{1,2},{2,3},{3,4},{4,5},{5,6},{6,7},{7,8},{8,9},{9,10},{10,1... | collective-permute-start | bytes 159752 | tf_op jit(solution)/shard_map/ppermute | solution.py:16
  17.1 12.1 %gather_fusion.12 = bf16[4096,12]{1,0:T(8,128)(2,1)S(1)} fusion(bf16[12,2048]{0,1:T(8,128)(2,1)S(1)} %copy.50, s32[4096]{0:T(1024)S(1)} %broadcast_clamp_fusion), kind=kCustom, calls=%fused_computation.12 | custom fusion | bytes 212992 | tf_op jit(solution)/shard_map/jit(_take)/gather | solution.py:103
  30.5 0.7 pad_add_fusion
  31.8 7.6 %scatter_custom_fusion = s32[1536]{0:T(1024)S(1)} fusion(s32[1024]{0:T(1024)S(1)} %bitcast.214, s32[1024]{0:T(1024)S(1)} %broadcast.361, s32[]{:T(128)} %constant.146.clone.1), kind=kCustom, calls=%fused_computation.126 | custom fusion | flops 1024 | bytes 6148 | tf_op jit(solution)/shard_map/scatter-add | solution.py:91
  40.1 5.9 %gather_fusion.13 = s32[1536]{0:T(1024)S(1)} fusion(s32[1024]{0:T(1024)S(1)} %iota.10, s32[2048]{0:T(1024)S(1)} %pad_clamp_fusion.1), kind=kCustom, calls=%fused_computation.13 | custom fusion | bytes 18432 | tf_op jit(solution)/shard_map/jit(_take)/gather | solution.py:91
  46.8 1.7 maximum_convert_fusion
  49.9 2.6 %gather_fusion.14 = f32[1536,24]{1,0:T(8,128)S(1)} fusion(f32[24,1024]{0,1:T(8,128)S(1)} %copy.52, s32[2048]{0:T(1024)S(1)} %pad_clamp_fusion), kind=kCustom, calls=%fused_computation.14 | custom fusion | bytes 301056 | tf_op jit(solution)/shard_map/jit(_take)/gather | solution.py:96
  52.8 1.1 scatter_fusion
  54.0 0.8 fusion.25
  54.8 22.9 %all-to-all-start = ((bf16[16,4,24,128]{3,2,1,0:T(8,128)(2,1)}), bf16[16,4,24,128]{3,2,1,0:T(8,128)(2,1)}, u32[]{:S(2)}, u32[]{:S(2)}) async-start(bf16[16,4,24,128]{3,2,1,0:T(8,128)(2,1)} %fusion.25), calls=%async_computation | async-start | bytes 786432 | tf_op jit(solution)/shard_map/all_to_all | solution.py:114
  77.7 11.1 %scatter_custom_fusion.4 = f32[1024]{0:T(1024)S(1)} fusion(s32[1536]{0:T(1024)S(1)} %fusion.33, f32[1536]{0:T(1024)S(1)} %reduce.6, f32[]{:T(128)} %constant.152.clone.1), kind=kCustom, calls=%fused_computation.133 | custom fusion | flops 1536 | bytes 4100 | tf_op jit(solution)/shard_map/scatter-add | solution.py:132
  88.9 1.0 copy.48
  89.9 51.4 %conditional.3 = (f32[80,2048]{1,0:T(8,128)S(1)}) conditional(s32[]{:T(128)} %convert_element_type.41, (f32[1,1,2048]{2,1,0:T(1,128)S(1)}, f32[208,512]{0,1:T(8,128)}, f32[80,2048]{0,1:T(8,128)S(1)}, s32[1,1,6,2048]{3,1,2,0:T(1,128)S(1)}) %tuple.74, f32[80,2048]{0,1:T(8,128)S(1)} %bitcast.171), branch_computations={%region_2.5_spmd, %region_3.6_spmd} | conditional | flops 2949120 | bytes 16482312 | solution.py:78
  89.9 0.9 fusion.47
  90.9 5.5 %gather_fusion.9 = f32[2048,80]{1,0:T(8,128)S(1)} fusion(f32[80,2304]{0,1:T(8,128)S(1)} %pad_maximum_fusion.1, s32[2048]{0:T(1024)S(1)} %fusion.17), kind=kCustom, calls=%fused_computation.9.clone | custom fusion | bytes 1318912 | tf_op jit(solution)/shard_map/cond/branch_0_fun/jit(_take)/gather | solution.py:25
  96.4 7.6 %gather_fusion.8 = f32[2048,80]{1,0:T(8,128)} fusion(f32[80,2304]{0,1:T(8,128)S(1)} %pad_maximum_fusion.1, s32[2048]{0:T(1024)S(1)} %fusion.16), kind=kCustom, calls=%fused_computation.8.clone | custom fusion | bytes 1318912 | tf_op jit(solution)/shard_map/cond/branch_0_fun/jit(_take)/gather | solution.py:25
  104.0 7.6 %gather_fusion.7 = f32[2048,80]{1,0:T(8,128)} fusion(f32[80,2304]{0,1:T(8,128)S(1)} %pad_maximum_fusion.1, s32[2048]{0:T(1024)S(1)} %fusion.15), kind=kCustom, calls=%fused_computation.7.clone | custom fusion | bytes 1318912 | tf_op jit(solution)/shard_map/cond/branch_0_fun/jit(_take)/gather | solution.py:25
  111.6 7.6 %gather_fusion.6 = f32[2048,80]{1,0:T(8,128)} fusion(f32[80,2304]{0,1:T(8,128)S(1)} %pad_maximum_fusion.1, s32[2048]{0:T(1024)S(1)} %fusion.14), kind=kCustom, calls=%fused_computation.6.clone | custom fusion | bytes 1318912 | tf_op jit(solution)/shard_map/cond/branch_0_fun/jit(_take)/gather | solution.py:25
  119.1 7.5 %gather_fusion.5 = f32[2048,80]{1,0:T(8,128)} fusion(f32[80,2304]{0,1:T(8,128)S(1)} %pad_maximum_fusion.1, s32[2048]{0:T(1024)S(1)} %fusion.13), kind=kCustom, calls=%fused_computation.5.clone | custom fusion | bytes 1318912 | tf_op jit(solution)/shard_map/cond/branch_0_fun/jit(_take)/gather | solution.py:25
  126.7 7.6 %gather_fusion.4 = f32[2048,80]{1,0:T(8,128)} fusion(f32[80,2304]{0,1:T(8,128)S(1)} %pad_maximum_fusion.1, s32[2048]{0:T(1024)S(1)} %fusion.12), kind=kCustom, calls=%fused_computation.1.clone | custom fusion | bytes 1318912 | tf_op jit(solution)/shard_map/cond/branch_0_fun/jit(_take)/gather | solution.py:23
  134.3 6.4 %fusion.11 = f32[80,2048]{0,1:T(8,128)S(1)} fusion(f32[80,2048]{0,1:T(8,128)S(1)} %get-tuple-element.50, f32[2048,80]{1,0:T(8,128)S(1)} %gather_fusion.9, f32[2048,80]{1,0:T(8,128)} %gather_fusion.8, f32[2048,80]{1,0:T(8,128)} %gather_fusion.7, f32[2048,80]{1,0:T(8,128)} %gather_fusion.6, f32[2048,80]{1,0:T(8,128)} %gather_fusion.5, ...), kind=kLoop, calls=%fused_computation.46 | loop fusion | flops 2457600 | bytes 5263360 | tf_op jit(solution)/shard_map/cond/branch_0_fun/add | solution.py:26
  141.3 1.0 convert_bitcast_fusion
  142.5 2.0 %copy.55 = f32[4096,24]{1,0:T(8,128)} copy(f32[4096,24]{0,1:T(8,128)S(1)} %bitcast.176) | data formatting | bytes 786432 | tf_op jit(solution)/shard_map/convert_element_type | solution.py:119
  144.5 22.9 %scatter_custom_fusion.2 = f32[24,2048]{0,1:T(8,128)S(1)} fusion(s32[4096]{0:T(1024)S(1)} %bitcast.197, f32[4096,24]{1,0:T(8,128)} %copy.55, f32[]{:T(128)} %constant.152.clone.1), kind=kCustom, calls=%fused_computation.79 | custom fusion | flops 98304 | bytes 197120 | tf_op jit(solution)/shard_map/scatter-add | solution.py:120
  167.4 0.9 slice.173
  169.4 8.9 %scatter_custom_fusion.3 = f32[12,1024]{0,1:T(8,128)S(1)} fusion(s32[1536]{0:T(1024)S(1)} %fusion.33, f32[1536,12]{1,0:T(8,128)S(1)} %copy.58, f32[]{:T(128)} %constant.152.clone.1), kind=kCustom, calls=%fused_computation.84 | custom fusion | flops 18432 | bytes 49156 | tf_op jit(solution)/shard_map/scatter-add | solution.py:130
  178.5 0.8 copy.59
  179.3 2.1 %fusion.20 = f32[1,1,80,2048]{3,2,1,0:T(8,128)} fusion(f32[80,2048]{1,0:T(8,128)S(1)} %get-tuple-element.86, f32[24,2048]{0,1:T(8,128)S(1)} %scatter_custom_fusion.2, f32[80,24]{0,1:T(8,128)S(1)} %copy-done, f32[]{:T(128)S(6)} %convert_element_type.43), kind=kOutput, calls=%fused_computation.72 | convolution fusion | flops 47513600 | bytes 1515012 | tf_op jit(solution)/shard_map/dot_general | solution.py:121
  (99 shorter events, 10.4 us)
Async XLA Ops:
  0.6 178.7 %copy-start = (f32[80,24]{0,1:T(8,128)S(1)}, f32[80,24]{0,1:T(8,128)}, u32[]{:S(2)}) copy-start(f32[80,24]{0,1:T(8,128)} %param.38) | copy-start | bytes 23044
  0.6 2.7 %copy-start.1 = (f32[1,1,80,2048]{3,2,1,0:T(8,128)S(1)}, f32[1,1,80,2048]{3,2,1,0:T(8,128)}, u32[]{:S(2)}) copy-start(f32[1,1,80,2048]{3,2,1,0:T(8,128)} %param.34) | copy-start | bytes 1966084
  0.7 3.0 %copy-start.12 = (s32[1,1,256]{2,1,0:T(1,128)S(1)}, s32[1,1,256]{2,1,0:T(1,128)}, u32[]{:S(2)}) copy-start(s32[1,1,256]{2,1,0:T(1,128)} %param.36) | copy-start | bytes 3076
  3.4 12.9 %copy-start.2 = (s32[1,1,8,4,128]{4,3,2,1,0:T(4,128)S(1)}, s32[1,1,8,4,128]{4,3,2,1,0:T(4,128)}, u32[]{:S(2)}) copy-start(s32[1,1,8,4,128]{4,3,2,1,0:T(4,128)} %param.33) | copy-start | bytes 49156
  3.7 12.6 %copy-start.6 = (f32[12,80]{1,0:T(8,128)S(1)}, f32[12,80]{1,0:T(8,128)}, u32[]{:S(2)}) copy-start(f32[12,80]{1,0:T(8,128)} %param.39) | copy-start | bytes 11524
  6.1 40.6 %collective-permute-start.1 = (bf16[208,128]{0,1:T(8,128)(2,1)}, bf16[208,128]{0,1:T(8,128)(2,1)S(1)}, u32[]{:S(2)}, u32[]{:S(2)}) collective-permute-start(bf16[208,128]{0,1:T(8,128)(2,1)} %get-tuple-element.114), channel_id=1, source_target_pairs={{1,0},{2,1},{3,2},{4,3},{5,4},{6,5},{7,6},{8,7},{9,8},{10,9},{11,1... | collective-permute-start | bytes 159752 | tf_op jit(solution)/shard_map/ppermute | solution.py:17
  14.3 32.4 %collective-permute-start = (bf16[208,128]{0,1:T(8,128)(2,1)}, bf16[208,128]{0,1:T(8,128)(2,1)}, u32[]{:S(2)}, u32[]{:S(2)}) collective-permute-start(bf16[208,128]{0,1:T(8,128)(2,1)} %get-tuple-element.113), channel_id=1, source_target_pairs={{0,1},{1,2},{2,3},{3,4},{4,5},{5,6},{6,7},{7,8},{8,9},{9,10},{10,1... | collective-permute-start | bytes 159752 | tf_op jit(solution)/shard_map/ppermute | solution.py:16
  17.1 12.6 %copy-start.13 = (s32[1,1,12,1]{2,3,1,0:T(1,128)S(1)}, s32[1,1,12,1]{2,3,1,0:T(1,128)}, u32[]{:S(2)}) copy-start(s32[1,1,12,1]{2,3,1,0:T(1,128)} %param.32) | copy-start | bytes 148
  17.1 12.8 %copy-start.11 = (s32[1,1,1024]{2,1,0:T(1,128)S(1)}, s32[1,1,1024]{2,1,0:T(1,128)}, u32[]{:S(2)}) copy-start(s32[1,1,1024]{2,1,0:T(1,128)} %param.30) | copy-start | bytes 12292
  40.1 6.6 %copy-start.9 = (f32[1,1,1536]{2,1,0:T(1,128)S(1)}, f32[1,1,1536]{2,1,0:T(1,128)}, u32[]{:S(2)}) copy-start(f32[1,1,1536]{2,1,0:T(1,128)} %param.31) | copy-start | bytes 18436
  40.1 8.4 %copy-start.4 = (s32[1,1,4,1024]{3,2,1,0:T(4,128)S(1)}, s32[1,1,4,1024]{3,2,1,0:T(4,128)}, u32[]{:S(2)}) copy-start(s32[1,1,4,1024]{3,2,1,0:T(4,128)} %param.26) | copy-start | bytes 49156
  48.4 0.7 copy-start.5
  49.9 2.8 %copy-start.7 = (pred[12,128]{1,0:T(8,128)(4,1)S(1)}, pred[12,128]{1,0:T(8,128)(4,1)}, u32[]{:S(2)}) copy-start(pred[12,128]{1,0:T(8,128)(4,1)} %compare_and_fusion.11) | copy-start | bytes 4612
  53.9 35.9 %copy-start.3 = (s32[1,1,6,2048]{3,1,2,0:T(1,128)S(1)}, s32[1,1,6,2048]{3,1,2,0:T(1,128)}, u32[]{:S(2)}) copy-start(s32[1,1,6,2048]{3,1,2,0:T(1,128)} %param.35) | copy-start | bytes 147460
  54.0 35.9 %copy-start.8 = (f32[1,1,2048]{2,1,0:T(1,128)S(1)}, f32[1,1,2048]{2,1,0:T(1,128)}, u32[]{:S(2)}) copy-start(f32[1,1,2048]{2,1,0:T(1,128)} %param.37) | copy-start | bytes 24580
  54.8 86.5 %all-to-all-start = ((bf16[16,4,24,128]{3,2,1,0:T(8,128)(2,1)}), bf16[16,4,24,128]{3,2,1,0:T(8,128)(2,1)}, u32[]{:S(2)}, u32[]{:S(2)}) async-start(bf16[16,4,24,128]{3,2,1,0:T(8,128)(2,1)} %fusion.25), calls=%async_computation | async-start | bytes 786432 | tf_op jit(solution)/shard_map/all_to_all | solution.py:114
where the time goes:
time: 182 us; the launch traced here: 181 us
  local copies, waits for them, and re-layouts  78.2 us (43%)
  other arithmetic  65.6 us (36%)
  starting transfers between devices  33 us (18%)
  matrix products  3.12 us (2%)
    gather x5, local copies, waits for them, and re-layouts, stencil(): total = total + jnp.take(pool, neighbours[which], axis=1)  35.7 us
    all_to_all x1, starting transfers between devices, on_device(): lax.all_to_all(combined, 'grp', split_axis=0, concat_axis=0, tiled=True)  22.9 us
    scatter-add x1, other arithmetic, on_device(): jnp.zeros((fields, cells), jnp.float32).at[:, cell_index].add(incoming)  22.9 us
    gather x2, local copies, waits for them, and re-layouts, on_device(): jnp.take(returned, cell_index, axis=1)  12.6 us
    scatter-add x1, other arithmetic, on_device(): weight_sum = jnp.zeros((columns,), jnp.float32).at[column].add(weights)  11.1 us
    scatter-add x1, other arithmetic, on_device(): jnp.zeros((ret_fields, columns), jnp.float32).at[:, column]  8.87 us
    ppermute x1, starting transfers between devices, extended_2(): after = lax.ppermute(leading, axis, down)  8.19 us
    scatter-add x1, other arithmetic, on_device(): jnp.repeat(jnp.arange(columns, dtype=jnp.int32), margin_counts[0, 0], tot...  7.62 us
  transfers between devices with their start and end apart: 3, of which 0 were waited for; matrix products, arithmetic and copies ran while one was open for 52% of the time, Pallas kernels for 0%

commit v1 on v0

v1 whole, which is shorter than its diff:
```python
import functools

import jax
import jax.numpy as jnp
from jax import lax
from jax.experimental import pallas as pl
from jax.experimental.pallas import tpu as pltpu
from jax.sharding import PartitionSpec as P

F32 = jnp.float32
BF16 = jnp.bfloat16
I32 = jnp.int32
TILE = 256
NT = (((1,), (1,)), ((), ()))


def dot(a, b):
    return jnp.dot(a, b, preferred_element_type=F32)


def dot_nt(a, b):
    return lax.dot_general(a, b, NT, preferred_element_type=F32)


def split(x):
    hi = x.astype(BF16)
    lo = (x - hi.astype(F32)).astype(BF16)
    return hi, lo


def exact(w, x):
    wh, wl = split(w)
    xh, xl = split(x)
    return dot(wh, xh) + (dot(wl, xh) + dot(wh, xl))


def row_iota(rows, cols):
    return lax.broadcasted_iota(I32, (rows, cols), 0)


def one_hot(rows_bf, index_row):
    return jnp.where(rows_bf == index_row, jnp.ones((), BF16), jnp.zeros((), BF16))


def pack_kernel(atm_groups, air_ref, air_send, sea_ref, sea_send, down, up, air, sea, sem):
    here = lax.axis_index("grp") < atm_groups
    half = down.shape[1]
    rows = row_iota(TILE, 2 * half).astype(F32).astype(BF16)

    def packed(state, send):
        index = send[...]
        total = None
        for base in range(0, state.shape[1], TILE):
            mark = one_hot(rows, (index - base).astype(F32).astype(BF16))
            part = dot(state[:, base : base + TILE].astype(BF16), mark)
            total = part if total is None else total + part
        levels = state.shape[0]
        out = total.astype(BF16)
        down[0:levels, :] = out[:, :half]
        up[0:levels, :] = out[:, half:]

    @pl.when(here)
    def _():
        copy = pltpu.make_async_copy(air_ref, air, sem)
        copy.start()
        copy.wait()
        packed(air, air_send)

    @pl.when(jnp.logical_not(here))
    def _():
        copy = pltpu.make_async_copy(sea_ref, sea, sem)
        copy.start()
        copy.wait()
        packed(sea, sea_send)


def stencil_chunk(pool, nbrs, at, rows, width):
    picks = [n[:, pl.ds(at, width)] for n in nbrs]
    total = None
    for base in range(0, pool.shape[1], TILE):
        marks = None
        for pick in picks:
            mark = one_hot(rows, (pick - base).astype(F32).astype(BF16))
            marks = mark if marks is None else marks + mark
        part = dot(pool[:, base : base + TILE], marks)
        total = part if total is None else total + part
    return total


def fill_ends(counts, ends):
    blocks, lanes = counts.shape
    given = counts[...].astype(F32).astype(BF16)
    upto = jnp.where(
        row_iota(lanes, lanes) <= lax.broadcasted_iota(I32, (lanes, lanes), 1), 1.0, 0.0
    ).astype(BF16)
    within = dot(given, upto)
    whole = dot(given, jnp.ones((lanes, lanes), BF16))
    before = jnp.zeros((1, lanes), F32)
    for j in range(blocks):
        ends[j : j + 1, :] = (within[j : j + 1] + before).astype(I32)
        before = before + whole[j : j + 1]


def fill_spread(counts, ends, spread):
    fill_ends(counts, ends)
    rows, _ = spread.shape
    blocks, lanes = counts.shape
    order = row_iota(rows, lanes)
    for j in range(blocks):
        end = ends[j : j + 1, :]
        begin = end - counts[j : j + 1, :]
        inside = (order >= begin) & (order < end)
        spread[:, j * lanes : (j + 1) * lanes] = jnp.where(inside, 1.0, 0.0).astype(BF16)


def slots_of(owner, seen, visit):
    for o in range(seen.shape[0]):
        seen[o] = 0
    for b in range(owner.shape[1]):
        o = owner[0, b]
        k = seen[o]
        seen[o] = k + 1
        visit(b, o, k)


def mid_kernel(
    atm_groups,
    air_ref, air_nbrs, air_mix, flux_weight, counts, weights, owner, recv,
    sea_ref, sea_nbrs, sea_mix, ret_weight, low, high,
    air_out, base_out, send_out,
    air, sea, air_pool, sea_pool, spread, ends, returned, seen, sem, out_sem,
):
    here = lax.axis_index("grp") < atm_groups
    rows = row_iota(TILE, TILE).astype(F32).astype(BF16)
    half = low.shape[1]

    def pooled(state, pool):
        levels, own = state.shape
        pool[:, :own] = state[...].astype(BF16)
        pool[:, own : own + half] = low[0:levels, :]
        pool[:, own + half :] = high[0:levels, :]

    @pl.when(here)
    def _():
        copy = pltpu.make_async_copy(air_ref, air, sem)
        copy.start()
        fill_spread(counts, ends, spread)
        send_out[...] = jnp.zeros(send_out.shape, BF16)
        copy.wait()
        pooled(air, air_pool)
        columns = air.shape[1]
        amount = air_nbrs.shape[0]
        nbrs = [air_nbrs.at[k : k + 1, :] for k in range(amount)]
        parts = []
        for at in range(0, columns, TILE):
            total = stencil_chunk(air_pool, nbrs, at, rows, TILE)
            own = air[:, at : at + TILE]
            new = own + air_mix[:, at : at + TILE] * (total * (1.0 / amount) - own)
            air[:, at : at + TILE] = new
            parts.append(exact(flux_weight[...], new))
        out_copy = pltpu.make_async_copy(air, air_out, out_sem)
        out_copy.start()
        hi, lo = split(jnp.concatenate(parts, axis=1))
        fields = hi.shape[0]
        block = send_out.shape[3]

        def visit(b, o, k):
            mark = spread[b * block : (b + 1) * block, :]
            value = dot_nt(hi, mark) + dot_nt(lo, mark)
            value = value * weights[:, b * block : (b + 1) * block]
            send_out[atm_groups + o, k] = value.astype(BF16)

        slots_of(owner, seen, visit)
        out_copy.wait()

    @pl.when(jnp.logical_not(here))
    def _():
        keep = pltpu.make_async_copy(air_ref, air_out, out_sem)
        keep.start()
        copy = pltpu.make_async_copy(sea_ref, sea, sem)
        copy.start()
        copy.wait()
        pooled(sea, sea_pool)
        cells = sea.shape[1]
        fields = ret_weight.shape[0]
        his = cells // TILE
        pad = returned.shape[0] // his
        for h in range(his):
            chunk = exact(ret_weight[...], sea[:, h * TILE : (h + 1) * TILE])
            chunk = jnp.concatenate([chunk, jnp.zeros((pad - fields, TILE), F32)], axis=0)
            returned[h * pad : (h + 1) * pad, :] = chunk.astype(BF16)
        senders, slots, block = recv.shape
        for s in range(senders):
            index = jnp.concatenate([recv[s, k : k + 1, :] for k in range(slots)], axis=1)
            top = index // TILE
            rest = (index - top * TILE).astype(F32).astype(BF16)
            row_b = row_iota(TILE, slots * block).astype(F32).astype(BF16)
            found = dot(returned[...], one_hot(row_b, rest))
            look = jnp.zeros((pad, slots * block), F32)
            for h in range(his):
                look = jnp.where(top == h, found[h * pad : (h + 1) * pad], look)
            look = jnp.concatenate(
                [look, jnp.zeros((send_out.shape[2] - pad, slots * block), F32)], axis=0
            ).astype(BF16)
            for k in range(slots):
                send_out[s, k] = look[:, k * block : (k + 1) * block]
        amount = sea_nbrs.shape[0]
        nbrs = [sea_nbrs.at[k] for k in range(amount)]

        def step(i, carry):
            at = pl.multiple_of(i * TILE, TILE)
            total = stencil_chunk(sea_pool, nbrs, at, rows, TILE)
            own = sea[:, pl.ds(at, TILE)]
            base_out[:, pl.ds(at, TILE)] = own + sea_mix[:, pl.ds(at, TILE)] * (
                total * (1.0 / amount) - own
            )
            return carry

        lax.fori_loop(0, his, step, 0)
        keep.wait()


def post_kernel(
    atm_groups,
    arrived, counts, weights, owner, recv, sea_ref, base, force_weight,
    sea_out, mapped_out,
    sea, spread, ends, mine, seen, sem,
):
    here = lax.axis_index("grp") < atm_groups

    @pl.when(here)
    def _():
        keep = pltpu.make_async_copy(sea_ref, sea_out, sem)
        keep.start()
        fill_spread(counts, ends, spread)
        fields = mapped_out.shape[0]
        block = arrived.shape[3]

        def visit(b, o, k):
            mine[:, b * block : (b + 1) * block] = arrived[atm_groups + o, k].astype(F32)

        slots_of(owner, seen, visit)
        w = weights[...]
        scaled = mine[0:16, :] * w
        order = row_iota(16, scaled.shape[1])
        scaled = jnp.where(order < fields, scaled, jnp.where(order == fields, w, 0.0))
        hi, lo = split(scaled)
        both = dot(hi, spread[...]) + dot(lo, spread[...])
        mapped_out[...] = both[0:fields] / both[fields : fields + 1]
        keep.wait()

    @pl.when(jnp.logical_not(here))
    def _():
        mapped_out[...] = jnp.zeros(mapped_out.shape, F32)
        senders, slots, block = recv.shape
        fields = arrived.shape[2]
        his = sea.shape[1] // TILE
        flux = jnp.zeros((his * fields, TILE), F32)
        row_b = row_iota(TILE, slots * block).astype(F32).astype(BF16)
        for s in range(senders):
            index = jnp.concatenate([recv[s, k : k + 1, :] for k in range(slots)], axis=1)
            top = index // TILE
            rest = (index - top * TILE).astype(F32).astype(BF16)
            got = jnp.concatenate([arrived[s, k].astype(F32) for k in range(slots)], axis=1)
            parts = [jnp.where(top == h, got, 0.0) for h in range(his)]
            apart = jnp.concatenate(parts, axis=0).astype(BF16)
            flux = flux + dot_nt(apart, one_hot(row_b, rest))
        for h in range(his):
            forcing = exact(force_weight[...], flux[h * fields : (h + 1) * fields])
            at = slice(h * TILE, (h + 1) * TILE)
            sea[:, at] = base[:, at] + forcing
        out = pltpu.make_async_copy(sea, sea_out, sem)
        out.start()
        out.wait()


def vmem():
    return pl.BlockSpec(memory_space=pltpu.VMEM)


def smem():
    return pl.BlockSpec(memory_space=pltpu.SMEM)


def anywhere():
    return pl.BlockSpec(memory_space=pl.ANY)


def on_device(
    atm_state, atm_nbrs, atm_send, atm_mix, flux_weight, margin_counts, margin_weight,
    block_owner, recv_cols, ocn_state, ocn_nbrs, ocn_send, ocn_mix, force_weight, ret_weight,
):
    levels_air, columns = atm_state.shape[2:]
    levels_sea, cells = ocn_state.shape[2:]
    pair = atm_send.shape[2]
    half = pair // 2
    amount_air = atm_nbrs.shape[2]
    amount_sea = ocn_nbrs.shape[2]
    atm_groups, capacity, block = recv_cols.shape[2:]
    row_count = margin_weight.shape[2]
    blocks_here = block_owner.shape[2]
    fields = flux_weight.shape[0]
    ret_fields = ret_weight.shape[0]
    groups = lax.axis_size("grp")
    peers = lax.axis_size("dev")

    air = atm_state.reshape(levels_air, columns)
    sea = ocn_state.reshape(levels_sea, cells)
    counts = margin_counts.reshape(columns // 128, 128)
    weights = margin_weight.reshape(1, row_count)
    owner = block_owner.reshape(1, blocks_here)
    recv = recv_cols.reshape(atm_groups, capacity, block)

    most = max(levels_air, levels_sea)
    params = pltpu.CompilerParams(vmem_limit_bytes=32 * 2**20)
    down, up = pl.pallas_call(
        functools.partial(pack_kernel, atm_groups),
        out_shape=[jax.ShapeDtypeStruct((most, half), BF16)] * 2,
        in_specs=[anywhere(), vmem(), anywhere(), vmem()],
        out_specs=[vmem(), vmem()],
        scratch_shapes=[
            pltpu.VMEM((levels_air, columns), F32),
            pltpu.VMEM((levels_sea, cells), F32),
            pltpu.SemaphoreType.DMA,
        ],
        compiler_params=params,
        name="pack",
    )(air, atm_send.reshape(1, pair), sea, ocn_send.reshape(1, pair))
    higher = [(i, (i + 1) % peers) for i in range(peers)]
    lower = [(j, i) for i, j in higher]
    low = lax.ppermute(up, "dev", higher)
    high = lax.ppermute(down, "dev", lower)

    air_next, base, outgoing = pl.pallas_call(
        functools.partial(mid_kernel, atm_groups),
        out_shape=[
            jax.ShapeDtypeStruct((levels_air, columns), F32),
            jax.ShapeDtypeStruct((levels_sea, cells), F32),
            jax.ShapeDtypeStruct((groups, capacity, fields, block), BF16),
        ],
        in_specs=[
            anywhere(), vmem(), vmem(), vmem(), vmem(), vmem(), smem(), vmem(),
            anywhere(), vmem(), vmem(), vmem(), vmem(), vmem(),
        ],
        out_specs=[anywhere(), vmem(), vmem()],
        scratch_shapes=[
            pltpu.VMEM((levels_air, columns), F32),
            pltpu.VMEM((levels_sea, cells), F32),
            pltpu.VMEM((levels_air, columns + pair), BF16),
            pltpu.VMEM((levels_sea, cells + pair), BF16),
            pltpu.VMEM((row_count, columns), BF16),
            pltpu.VMEM((columns // 128, 128), I32),
            pltpu.VMEM((16 * (cells // TILE), TILE), BF16),
            pltpu.SMEM((groups - atm_groups,), I32),
            pltpu.SemaphoreType.DMA,
            pltpu.SemaphoreType.DMA,
        ],
        compiler_params=params,
        name="mid",
    )(
        air, atm_nbrs.reshape(amount_air, columns), atm_mix.reshape(1, columns), flux_weight,
        counts, weights, owner, recv,
        sea, ocn_nbrs.reshape(amount_sea, 1, cells), ocn_mix.reshape(1, cells), ret_weight,
        low, high,
    )
    arrived = lax.all_to_all(outgoing, "grp", split_axis=0, concat_axis=0, tiled=True)
    sea_next, mapped = pl.pallas_call(
        functools.partial(post_kernel, atm_groups),
        out_shape=[
            jax.ShapeDtypeStruct((levels_sea, cells), F32),
            jax.ShapeDtypeStruct((ret_fields, columns), F32),
        ],
        in_specs=[
            vmem(), vmem(), vmem(), smem(), vmem(), anywhere(), vmem(), vmem(),
        ],
        out_specs=[anywhere(), vmem()],
        scratch_shapes=[
            pltpu.VMEM((levels_sea, cells), F32),
            pltpu.VMEM((row_count, columns), BF16),
            pltpu.VMEM((columns // 128, 128), I32),
            pltpu.VMEM((fields, row_count), F32),
            pltpu.SMEM((groups - atm_groups,), I32),
            pltpu.SemaphoreType.DMA,
        ],
        compiler_params=params,
        name="post",
    )(arrived, counts, weights, owner, recv, sea, base, force_weight)
    return (air_next[None, None], sea_next[None, None], mapped[None, None])


def solution(mesh):
    whole = P("grp", "dev")
    specs = [whole] * 15
    for replicated in (4, 13, 14):
        specs[replicated] = P()
    return jax.shard_map(
        on_device,
        mesh=mesh,
        in_specs=tuple(specs),
        out_specs=(whole, whole, whole),
        check_vma=False,
    )
```

time: 182 us -> 63.9 us (0.35)
  the two profiles are of different devices: /device:TPU:513 before, /device:TPU:63 now
where the time goes in v1:
time: 63.9 us; the launch traced here: 63.5 us
  starting transfers between devices  26.6 us (42%)
  waiting for transfers between devices  20.5 us (32%)
  Pallas kernels  11.4 us (18%)
  local copies, waits for them, and re-layouts  4.19 us (7%)
  between operations  0.83 us (1%)
    all_to_all x1, starting transfers between devices, on_device(): lax.all_to_all(outgoing, 'grp', split_axis=0, concat_axis=0, tiled=True)  20.3 us
    all_to_all x1, waiting for transfers between devices, on_device(): lax.all_to_all(outgoing, 'grp', split_axis=0, concat_axis=0, tiled=True)  14.5 us
    pallas_call x1, Pallas kernels, on_device(): pl.pallas_call(functools.partial(mid_kernel, atm_groups), out_shape=[jax....  7.93 us
    ppermute x1, waiting for transfers between devices, on_device(): high = lax.ppermute(down, 'dev', lower)  6.04 us
    ppermute x1, starting transfers between devices, on_device(): low = lax.ppermute(up, 'dev', higher)  4.33 us
    unnamed x34, local copies, waits for them, and re-layouts  4.19 us
    pallas_call x1, Pallas kernels, on_device(): pl.pallas_call(functools.partial(post_kernel, atm_groups), out_shape=[jax...  3.17 us
    ppermute x1, starting transfers between devices, on_device(): high = lax.ppermute(down, 'dev', lower)  1.92 us
  transfers between devices with their start and end apart: 3, of which 2 were waited for; matrix products, arithmetic and copies ran while one was open for 0% of the time, Pallas kernels for 0%

profile of v1, /device:TPU:63, one launch (start us, length us, event | category | flops | bytes accessed | tf_op | source)
XLA Modules:
  0.0 63.5 jit_solution(5861793954633412416)
XLA Ops:
  0.6 0.0 copy-start.14
  0.6 0.0 copy-start.13
  0.7 0.7 %copy-done.14 = s32[1,1,256]{2,1,0:T(1,128)S(1)} copy-done((s32[1,1,256]{2,1,0:T(1,128)S(1)}, s32[1,1,256]{2,1,0:T(1,128)}, u32[]{:S(2)}) %copy-start.14) | copy-done | bytes 1048
  1.3 0.0 copy-done.13
  1.3 1.1 %copy-done = f32[1,1,80,2048]{3,2,1,0:T(8,128)S(1)} copy-done((f32[1,1,80,2048]{3,2,1,0:T(8,128)S(1)}, f32[1,1,80,2048]{3,2,1,0:T(8,128)}, u32[]{:S(2)}) %copy-start) | copy-done | bytes 655384
  2.4 1.0 %copy-done.2 = f32[1,1,128,1024]{3,2,1,0:T(8,128)S(1)} copy-done((f32[1,1,128,1024]{3,2,1,0:T(8,128)S(1)}, f32[1,1,128,1024]{3,2,1,0:T(8,128)}, u32[]{:S(2)}) %copy-start.2) | copy-done | bytes 524312
  3.5 0.0 copy-start.7
  3.5 0.0 copy-start.8
  3.5 0.0 copy-start.9
  3.5 0.0 copy-start.10
  3.5 0.3 pack.1
  3.8 0.0 copy-start.3
  3.8 4.3 %collective-permute-start = (bf16[128,128]{1,0:T(8,128)(2,1)S(1)}, bf16[128,128]{1,0:T(8,128)(2,1)S(1)}, u32[]{:S(2)}, u32[]{:S(2)}) collective-permute-start(bf16[128,128]{1,0:T(8,128)(2,1)S(1)} %get-tuple-element.10), channel_id=1, source_target_pairs={{0,1},{1,2},{2,3},{3,4},{4,5},{5,6},{6,7},{7,8},{8,9},{9,10},{10,1... | collective-permute-start | bytes 98312 | tf_op jit(solution)/shard_map/ppermute | solution.py:331
  8.2 1.9 %collective-permute-start.1 = (bf16[128,128]{1,0:T(8,128)(2,1)S(1)}, bf16[128,128]{1,0:T(8,128)(2,1)S(1)}, u32[]{:S(2)}, u32[]{:S(2)}) collective-permute-start(bf16[128,128]{1,0:T(8,128)(2,1)S(1)} %get-tuple-element.11), channel_id=1, source_target_pairs={{1,0},{2,1},{3,2},{4,3},{5,4},{6,5},{7,6},{8,7},{9,8},{10,9},{11,1... | collective-permute-start | bytes 98312 | tf_op jit(solution)/shard_map/ppermute | solution.py:332
  10.1 0.0 collective-permute-done.low
  10.1 6.0 %collective-permute-done.1.high = bf16[128,128]{1,0:T(8,128)(2,1)S(1)} collective-permute-done((bf16[128,128]{1,0:T(8,128)(2,1)S(1)}, bf16[128,128]{1,0:T(8,128)(2,1)S(1)}, u32[]{:S(2)}, u32[]{:S(2)}) %collective-permute-start.1) | collective-permute-done | bytes 32800 | tf_op jit(solution)/shard_map/ppermute | solution.py:332
  16.2 0.0 copy-done.4
  16.2 0.0 copy-done.6
  16.2 0.0 copy-done.7
  16.2 0.0 copy-done.8
  16.2 0.0 copy-done.9
  16.2 0.0 copy-done.10
  16.2 0.0 copy-done.11
  16.2 0.0 copy-done.3
  16.2 0.6 copy-done.12
  16.8 7.9 %mid.1 = (f32[128,1024]{1,0:T(8,128)}, f32[80,2048]{1,0:T(8,128)S(1)}, bf16[16,4,24,128]{3,2,1,0:T(8,128)(2,1)}) custom-call(f32[128,1024]{1,0:T(8,128)S(1)} %bitcast.19, s32[4,1024]{1,0:T(4,128)S(1)} %bitcast.26, f32[1,1024]{1,0:T(1,128)S(1)} %bitcast.30, f32[24,128]{1,0:T(8,128)S(1)} %copy-done.8, s32[8,128]{1,0:T(8,128)S(1)} %bitcast.27, ...), custom_call_target="tpu_custom_call" | custom-call | tf_op jit(solution)/shard_map/mid/pallas_call | solution.py:334
  24.8 0.0 copy-start.15
  24.8 20.3 %all-to-all-start = ((bf16[16,4,24,128]{3,2,1,0:T(8,128)(2,1)}), bf16[16,4,24,128]{3,2,1,0:T(8,128)(2,1)S(1)}, u32[]{:S(2)}, u32[]{:S(2)}) async-start(bf16[16,4,24,128]{3,2,1,0:T(8,128)(2,1)} %get-tuple-element.13), calls=%async_computation | async-start | bytes 786432 | tf_op jit(solution)/shard_map/all_to_all | solution.py:366
  45.1 0.1 copy.18.force_weight
  45.2 14.5 %all-to-all-done.arrived = bf16[16,4,24,128]{3,2,1,0:T(8,128)(2,1)S(1)} async-done(((bf16[16,4,24,128]{3,2,1,0:T(8,128)(2,1)}), bf16[16,4,24,128]{3,2,1,0:T(8,128)(2,1)S(1)}, u32[]{:S(2)}, u32[]{:S(2)}) %all-to-all-start) | async-done | bytes 393248 | tf_op jit(solution)/shard_map/all_to_all | solution.py:366
  59.6 3.2 %post.1 = (f32[80,2048]{1,0:T(8,128)}, f32[12,1024]{1,0:T(8,128)S(1)}) custom-call(bf16[16,4,24,128]{3,2,1,0:T(8,128)(2,1)S(1)} %all-to-all-done.arrived, s32[8,128]{1,0:T(8,128)S(1)} %bitcast.28, f32[1,1536]{1,0:T(1,128)S(1)} %bitcast.25, s32[1,12]{1,0:T(1,128)S(1)} %bitcast.32, s32[8,4,128]{2,1,0:T(4,128)S(1)} %bitcast.21, f32[80,2048]{1,0:T(8,128)S(1)} %bitcast.17, ...), custom_call_target="tpu_custom_call" | custom-call | tf_op jit(solution)/shard_map/post/pallas_call | solution.py:367
  62.8 0.7 %copy.19 = f32[1,1,12,1024]{3,1,2,0:T(1,128)} copy(f32[1,1,12,1024]{3,2,1,0:T(8,128)S(1)} %bitcast.22) | data formatting | bytes 98304
  (11 shorter events, 0.0 us)
Async XLA Ops:
  0.6 0.7 %copy-start.14 = (s32[1,1,256]{2,1,0:T(1,128)S(1)}, s32[1,1,256]{2,1,0:T(1,128)}, u32[]{:S(2)}) copy-start(s32[1,1,256]{2,1,0:T(1,128)} %param.26) | copy-start | bytes 3076
  0.6 0.7 %copy-start.13 = (s32[1,1,256]{2,1,0:T(1,128)S(1)}, s32[1,1,256]{2,1,0:T(1,128)}, u32[]{:S(2)}) copy-start(s32[1,1,256]{2,1,0:T(1,128)} %param.17) | copy-start | bytes 3076
  1.3 1.1 %copy-start = (f32[1,1,80,2048]{3,2,1,0:T(8,128)S(1)}, f32[1,1,80,2048]{3,2,1,0:T(8,128)}, u32[]{:S(2)}) copy-start(f32[1,1,80,2048]{3,2,1,0:T(8,128)} %param.24) | copy-start | bytes 1966084
  2.4 1.0 %copy-start.2 = (f32[1,1,128,1024]{3,2,1,0:T(8,128)S(1)}, f32[1,1,128,1024]{3,2,1,0:T(8,128)}, u32[]{:S(2)}) copy-start(f32[1,1,128,1024]{3,2,1,0:T(8,128)} %param.15) | copy-start | bytes 1572868
  3.5 12.7 %copy-start.1 = (f32[1,1,80,2048]{3,2,1,0:T(8,128)S(1)}, f32[1,1,80,2048]{3,2,1,0:T(8,128)}, u32[]{:S(2)}) copy-start(f32[1,1,80,2048]{3,2,1,0:T(8,128)} %param.24) | copy-start | bytes 1966084
  3.5 12.7 %copy-start.4 = (s32[1,1,6,2048]{3,1,2,0:T(1,128)S(1)}, s32[1,1,6,2048]{3,1,2,0:T(1,128)}, u32[]{:S(2)}) copy-start(s32[1,1,6,2048]{3,1,2,0:T(1,128)} %param.25) | copy-start | bytes 147460
  3.5 12.7 %copy-start.5 = (f32[1,1,1536]{2,1,0:T(1,128)S(1)}, f32[1,1,1536]{2,1,0:T(1,128)}, u32[]{:S(2)}) copy-start(f32[1,1,1536]{2,1,0:T(1,128)} %param.21) | copy-start | bytes 18436
  3.5 12.7 %copy-start.6 = (s32[1,1,4,1024]{3,2,1,0:T(4,128)S(1)}, s32[1,1,4,1024]{3,2,1,0:T(4,128)}, u32[]{:S(2)}) copy-start(s32[1,1,4,1024]{3,2,1,0:T(4,128)} %param.16) | copy-start | bytes 49156
  3.5 12.7 %copy-start.7 = (s32[1,1,1024]{2,1,0:T(1,128)S(1)}, s32[1,1,1024]{2,1,0:T(1,128)}, u32[]{:S(2)}) copy-start(s32[1,1,1024]{2,1,0:T(1,128)} %param.20) | copy-start | bytes 12292
  3.5 12.7 %copy-start.8 = (f32[24,128]{1,0:T(8,128)S(1)}, f32[24,128]{1,0:T(8,128)}, u32[]{:S(2)}) copy-start(f32[24,128]{1,0:T(8,128)} %flux_weight.1) | copy-start | bytes 36868
  3.5 12.7 %copy-start.9 = (f32[1,1,2048]{2,1,0:T(1,128)S(1)}, f32[1,1,2048]{2,1,0:T(1,128)}, u32[]{:S(2)}) copy-start(f32[1,1,2048]{2,1,0:T(1,128)} %param.27) | copy-start | bytes 24580
  3.5 12.7 %copy-start.10 = (f32[12,80]{1,0:T(8,128)S(1)}, f32[12,80]{1,0:T(8,128)}, u32[]{:S(2)}) copy-start(f32[12,80]{1,0:T(8,128)} %ret_weight.1) | copy-start | bytes 11524
  3.5 12.7 %copy-start.11 = (f32[1,1,1024]{2,1,0:T(1,128)S(1)}, f32[1,1,1024]{2,1,0:T(1,128)}, u32[]{:S(2)}) copy-start(f32[1,1,1024]{2,1,0:T(1,128)} %param.18) | copy-start | bytes 12292
  3.8 12.4 %copy-start.3 = (s32[1,1,8,4,128]{4,3,2,1,0:T(4,128)S(1)}, s32[1,1,8,4,128]{4,3,2,1,0:T(4,128)}, u32[]{:S(2)}) copy-start(s32[1,1,8,4,128]{4,3,2,1,0:T(4,128)} %param.23) | copy-start | bytes 49156
  3.8 6.3 %collective-permute-start = (bf16[128,128]{1,0:T(8,128)(2,1)S(1)}, bf16[128,128]{1,0:T(8,128)(2,1)S(1)}, u32[]{:S(2)}, u32[]{:S(2)}) collective-permute-start(bf16[128,128]{1,0:T(8,128)(2,1)S(1)} %get-tuple-element.10), channel_id=1, source_target_pairs={{0,1},{1,2},{2,3},{3,4},{4,5},{5,6},{6,7},{7,8},{8,9},{9,10},{10,1... | collective-permute-start | bytes 98312 | tf_op jit(solution)/shard_map/ppermute | solution.py:331
  8.2 8.0 %collective-permute-start.1 = (bf16[128,128]{1,0:T(8,128)(2,1)S(1)}, bf16[128,128]{1,0:T(8,128)(2,1)S(1)}, u32[]{:S(2)}, u32[]{:S(2)}) collective-permute-start(bf16[128,128]{1,0:T(8,128)(2,1)S(1)} %get-tuple-element.11), channel_id=1, source_target_pairs={{1,0},{2,1},{3,2},{4,3},{5,4},{6,5},{7,6},{8,7},{9,8},{10,9},{11,1... | collective-permute-start | bytes 98312 | tf_op jit(solution)/shard_map/ppermute | solution.py:332
  16.2 0.7 %copy-start.12 = (s32[1,1,12,1]{2,3,1,0:T(1,128)S(1)}, s32[1,1,12,1]{2,3,1,0:T(1,128)}, u32[]{:S(2)}) copy-start(s32[1,1,12,1]{2,3,1,0:T(1,128)} %param.22) | copy-start | bytes 148
  24.8 20.3 %copy-start.15 = (f32[80,24]{0,1:T(8,128)S(1)}, f32[80,24]{0,1:T(8,128)}, u32[]{:S(2)}) copy-start(f32[80,24]{0,1:T(8,128)} %param.28) | copy-start | bytes 23044
  24.8 34.9 %all-to-all-start = ((bf16[16,4,24,128]{3,2,1,0:T(8,128)(2,1)}), bf16[16,4,24,128]{3,2,1,0:T(8,128)(2,1)S(1)}, u32[]{:S(2)}, u32[]{:S(2)}) async-start(bf16[16,4,24,128]{3,2,1,0:T(8,128)(2,1)} %get-tuple-element.13), calls=%async_computation | async-start | bytes 786432 | tf_op jit(solution)/shard_map/all_to_all | solution.py:366

commit v2 on v1

v2 whole, which is shorter than its diff:
```python
import functools

import jax
import jax.numpy as jnp
from jax import lax
from jax.experimental import pallas as pl
from jax.experimental.pallas import tpu as pltpu
from jax.sharding import PartitionSpec as P

F32 = jnp.float32
BF16 = jnp.bfloat16
I32 = jnp.int32
TILE = 256
NT = (((1,), (1,)), ((), ()))


def dot(a, b):
    return jnp.dot(a, b, preferred_element_type=F32)


def dot_nt(a, b):
    return lax.dot_general(a, b, NT, preferred_element_type=F32)


def split(x):
    hi = x.astype(BF16)
    lo = (x - hi.astype(F32)).astype(BF16)
    return hi, lo


def exact(w, x):
    wh, wl = split(w)
    xh, xl = split(x)
    return dot(wh, xh) + (dot(wl, xh) + dot(wh, xl))


def row_iota(rows, cols):
    return lax.broadcasted_iota(I32, (rows, cols), 0)


def one_hot(rows_bf, index_row):
    return jnp.where(rows_bf == index_row, jnp.ones((), BF16), jnp.zeros((), BF16))


def cast_row(row):
    return row.astype(F32).astype(BF16)


def row_marks(rows, cols):
    return cast_row(row_iota(rows, cols))


def marks_at(picks, base, rows):
    marks = None
    for pick in picks:
        mark = one_hot(rows, cast_row(pick - base))
        marks = mark if marks is None else marks + mark
    return marks


def pack_into(state, send, down, up):
    half = down.shape[1]
    rows = row_marks(TILE, 2 * half)
    index = send[...]
    total = None
    for base in range(0, state.shape[1], TILE):
        part = dot(state[:, base : base + TILE].astype(BF16), marks_at([index], base, rows))
        total = part if total is None else total + part
    out = total.astype(BF16)
    down[...] = out[:, :half]
    up[...] = out[:, half:]


def fetch(source, target, sem):
    copy = pltpu.make_async_copy(source, target, sem)
    copy.start()
    return copy


def fetch_all(pairs, sems):
    return [fetch(source, target, sems.at[i]) for i, (source, target) in enumerate(pairs)]


def wait_all(copies):
    for copy in copies:
        copy.wait()


def air_pack_kernel(atm_groups, air_ref, send_ref, down, up, air, send, sems):
    @pl.when(lax.axis_index("grp") < atm_groups)
    def _():
        wait_all(fetch_all([(send_ref, send), (air_ref, air)], sems))
        pack_into(air, send, down, up)


def own_sums(pool, nbrs, at, width):
    rows = row_marks(TILE, width)
    picks = [n[:, pl.ds(at, width)] for n in nbrs]
    total = None
    for base in range(0, pool.shape[1], TILE):
        part = dot(pool[:, base : base + TILE], marks_at(picks, base, rows))
        total = part if total is None else total + part
    return total


def rim_marks(nbrs, at, width, own):
    picks = [n[:, pl.ds(at, width)] for n in nbrs]
    return marks_at(picks, own, row_marks(TILE, width))


def fill_ends(counts, ends):
    blocks, lanes = counts.shape
    given = cast_row(counts[...])
    upto = jnp.where(
        row_iota(lanes, lanes) <= lax.broadcasted_iota(I32, (lanes, lanes), 1), 1.0, 0.0
    ).astype(BF16)
    within = dot(given, upto)
    whole = dot(given, jnp.ones((lanes, lanes), BF16))
    before = jnp.zeros((1, lanes), F32)
    for j in range(blocks):
        ends[j : j + 1, :] = (within[j : j + 1] + before).astype(I32)
        before = before + whole[j : j + 1]


def fill_spread(counts, ends, spread):
    fill_ends(counts, ends)
    rows, _ = spread.shape
    blocks, lanes = counts.shape
    order = row_iota(rows, lanes)
    for j in range(blocks):
        end = ends[j : j + 1, :]
        begin = end - counts[j : j + 1, :]
        inside = (order >= begin) & (order < end)
        spread[:, j * lanes : (j + 1) * lanes] = jnp.where(inside, 1.0, 0.0).astype(BF16)


def slots_of(owner, seen, visit):
    for o in range(seen.shape[0]):
        seen[o] = 0
    for b in range(owner.shape[1]):
        o = owner[0, b]
        k = seen[o]
        seen[o] = k + 1
        visit(b, o, k)


def look_up(sea, ret_weight, recv, returned, looked):
    cells = sea.shape[1]
    fields = ret_weight.shape[0]
    his = cells // TILE
    pad = returned.shape[0] // his
    for h in range(his):
        chunk = exact(ret_weight[...], sea[:, h * TILE : (h + 1) * TILE])
        chunk = jnp.concatenate([chunk, jnp.zeros((pad - fields, TILE), F32)], axis=0)
        returned[h * pad : (h + 1) * pad, :] = chunk.astype(BF16)
    senders, slots, block = recv.shape
    for s in range(senders):
        index = jnp.concatenate([recv[s, k : k + 1, :] for k in range(slots)], axis=1)
        top = index // TILE
        rest = cast_row(index - top * TILE)
        found = dot(returned[...], one_hot(row_marks(TILE, slots * block), rest))
        look = jnp.zeros((pad, slots * block), F32)
        for h in range(his):
            look = jnp.where(top == h, found[h * pad : (h + 1) * pad], look)
        look = jnp.concatenate(
            [look, jnp.zeros((looked.shape[2] - pad, slots * block), F32)], axis=0
        ).astype(BF16)
        for k in range(slots):
            looked[s, k] = look[:, k * block : (k + 1) * block]


def air_own_kernel(
    atm_groups,
    after, air_ref, air_nbrs_ref, air_mix_ref, counts_ref,
    sea_ref, sea_send_ref, ret_weight_ref, recv_ref,
    part_ref, marks_ref, spread_ref, payload, air_out, sea_down_ref, sea_up_ref,
    air, air_nbrs, air_mix, counts, part, marks, spread, pool, ends,
    sea, sea_send, ret_weight, recv, returned, looked, down, up, sems, out_sems,
):
    here = lax.axis_index("grp") < atm_groups

    @pl.when(here)
    def _():
        near, many, whole, mixed = fetch_all(
            [(air_nbrs_ref, air_nbrs), (counts_ref, counts), (air_ref, air), (air_mix_ref, air_mix)],
            sems,
        )
        amount, columns = air_nbrs.shape
        nbrs = [air_nbrs.at[k : k + 1, :] for k in range(amount)]
        many.wait()
        fill_spread(counts, ends, spread)
        out_spread = fetch(spread, spread_ref, out_sems.at[0])
        near.wait()
        for at in range(0, columns, TILE):
            marks[:, at : at + TILE] = rim_marks(nbrs, at, TILE, columns)
        out_marks = fetch(marks, marks_ref, out_sems.at[1])
        wait_all([whole, mixed])
        pool[...] = air[...].astype(BF16)
        for at in range(0, columns, TILE):
            mix = air_mix[:, at : at + TILE]
            total = own_sums(pool, nbrs, at, TILE)
            own = air[:, at : at + TILE]
            part[:, at : at + TILE] = own + mix * (total * (1.0 / amount) - own)
        out_part = fetch(part, part_ref, out_sems.at[2])
        wait_all([out_spread, out_marks, out_part])

    @pl.when(jnp.logical_not(here))
    def _():
        keep = fetch(air_ref, air_out, out_sems.at[0])
        listed, *rest = fetch_all(
            [
                (sea_send_ref, sea_send),
                (sea_ref, sea),
                (ret_weight_ref, ret_weight),
                (recv_ref, recv),
            ],
            sems,
        )
        wait_all(rest)
        look_up(sea, ret_weight, recv, returned, looked)
        sent = fetch(looked, payload.at[pl.ds(0, atm_groups)], out_sems.at[1])
        listed.wait()
        pack_into(sea, sea_send, down, up)
        out_down = fetch(down, sea_down_ref, out_sems.at[2])
        out_up = fetch(up, sea_up_ref, out_sems.at[3])
        wait_all([sent, out_down, out_up, keep])


def air_send_kernel(
    atm_groups, amount,
    part_ref, marks_ref, spread_ref, low, high, air_mix_ref, flux_weight_ref, weights_ref,
    owner, sea_down_in, sea_up_in, payload_in, air_in,
    payload, air_out, sea_down, sea_up,
    part, marks, spread, air_mix, flux_weight, weights,
    air, rows_out, seen, sems, out_sems,
):
    @pl.when(lax.axis_index("grp") < atm_groups)
    def _():
        last, spreading, *first = fetch_all(
            [
                (weights_ref, weights),
                (spread_ref, spread),
                (marks_ref, marks),
                (part_ref, part),
                (air_mix_ref, air_mix),
                (flux_weight_ref, flux_weight),
            ],
            sems,
        )
        rows_out[...] = jnp.zeros(rows_out.shape, BF16)
        columns = air.shape[1]
        wait_all(first)
        rim = jnp.concatenate([low[...], high[...]], axis=1)
        parts = []
        for at in range(0, columns, TILE):
            total = dot(rim, marks[:, at : at + TILE])
            new = part[:, at : at + TILE] + air_mix[:, at : at + TILE] * (total * (1.0 / amount))
            air[:, at : at + TILE] = new
            parts.append(exact(flux_weight[...], new))
        stored = fetch(air, air_out, out_sems.at[0])
        hi, lo = split(jnp.concatenate(parts, axis=1))
        block = rows_out.shape[3]
        wait_all([last, spreading])

        def visit(b, o, k):
            mark = spread[b * block : (b + 1) * block, :]
            value = dot_nt(hi, mark) + dot_nt(lo, mark)
            value = value * weights[:, b * block : (b + 1) * block]
            rows_out[o, k] = value.astype(BF16)

        slots_of(owner, seen, visit)
        sent = fetch(rows_out, payload.at[pl.ds(atm_groups, rows_out.shape[0])], out_sems.at[1])
        wait_all([stored, sent])


def sea_own_kernel(
    atm_groups,
    after, sea_ref, sea_nbrs_ref,
    sums_ref, marks_ref, sea_out,
    sea, sea_nbrs, sums, marks, pool, sems, out_sems,
):
    here = lax.axis_index("grp") < atm_groups

    @pl.when(here)
    def _():
        fetch(sea_ref, sea_out, out_sems.at[0]).wait()

    @pl.when(jnp.logical_not(here))
    def _():
        near, whole = fetch_all([(sea_nbrs_ref, sea_nbrs), (sea_ref, sea)], sems)
        amount, _, cells = sea_nbrs.shape
        nbrs = [sea_nbrs.at[k] for k in range(amount)]
        near.wait()
        for at in range(0, cells, TILE):
            marks[:, at : at + TILE] = rim_marks(nbrs, at, TILE, cells)
        out_marks = fetch(marks, marks_ref, out_sems.at[1])
        whole.wait()
        pool[...] = sea[...].astype(BF16)

        def step(i, carry):
            at = pl.multiple_of(i * TILE, TILE)
            sums[:, pl.ds(at, TILE)] = own_sums(pool, nbrs, at, TILE)
            return carry

        lax.fori_loop(0, cells // TILE, step, 0)
        out_sums = fetch(sums, sums_ref, out_sems.at[0])
        wait_all([out_marks, out_sums])


def last_kernel(
    atm_groups, amount,
    arrived, spread_ref, weights_ref, owner,
    recv_ref, sea_ref, sums_ref, marks_ref, low, high, sea_mix_ref, force_weight_ref, sea_in,
    sea_out, mapped_ref,
    spread, weights, mine, mapped, seen,
    recv, sea, sums, marks, sea_mix, force_weight, sems, out_sems,
):
    here = lax.axis_index("grp") < atm_groups
    fields, _, columns = mapped.shape

    @pl.when(here)
    def _():
        given, spreading = fetch_all([(weights_ref, weights), (spread_ref, spread)], sems)
        block = arrived.shape[3]
        given.wait()

        def visit(b, o, k):
            mine[:, b * block : (b + 1) * block] = arrived[atm_groups + o, k].astype(F32)

        slots_of(owner, seen, visit)
        w = weights[...]
        scaled = mine[0:16, :] * w
        order = row_iota(16, scaled.shape[1])
        scaled = jnp.where(order < fields, scaled, jnp.where(order == fields, w, 0.0))
        hi, lo = split(scaled)
        spreading.wait()
        both = dot(hi, spread[...]) + dot(lo, spread[...])
        mean = both[0:fields] / both[fields : fields + 1]
        for f in range(fields):
            mapped[f] = mean[f : f + 1]
        fetch(mapped, mapped_ref, out_sems.at[0]).wait()

    @pl.when(jnp.logical_not(here))
    def _():
        mapped[...] = jnp.zeros(mapped.shape, F32)
        stored = fetch(mapped, mapped_ref, out_sems.at[0])
        cells_in, *rest = fetch_all(
            [
                (recv_ref, recv),
                (sea_ref, sea),
                (sums_ref, sums),
                (marks_ref, marks),
                (sea_mix_ref, sea_mix),
                (force_weight_ref, force_weight),
            ],
            sems,
        )
        senders, slots, block = recv.shape
        rows = arrived.shape[2]
        his = sea.shape[1] // TILE
        flux = jnp.zeros((his * rows, TILE), F32)
        cells_in.wait()
        for s in range(senders):
            index = jnp.concatenate([recv[s, k : k + 1, :] for k in range(slots)], axis=1)
            top = index // TILE
            rest_of = cast_row(index - top * TILE)
            values = jnp.concatenate([arrived[s, k].astype(F32) for k in range(slots)], axis=1)
            parts = [jnp.where(top == h, values, 0.0) for h in range(his)]
            apart = jnp.concatenate(parts, axis=0).astype(BF16)
            flux = flux + dot_nt(apart, one_hot(row_marks(TILE, slots * block), rest_of))
        wait_all(rest)
        rim = jnp.concatenate([low[...], high[...]], axis=1)
        for h in range(his):
            at = slice(h * TILE, (h + 1) * TILE)
            forcing = exact(force_weight[...], flux[h * rows : (h + 1) * rows])
            total = sums[:, at] + dot(rim, marks[:, at])
            own = sea[:, at]
            sea[:, at] = own + sea_mix[:, at] * (total * (1.0 / amount) - own) + forcing
        out = fetch(sea, sea_out, out_sems.at[1])
        wait_all([stored, out])


def vmem():
    return pl.BlockSpec(memory_space=pltpu.VMEM)


def smem():
    return pl.BlockSpec(memory_space=pltpu.SMEM)


def anywhere():
    return pl.BlockSpec(memory_space=pl.ANY)


def in_hbm(x):
    return pltpu.with_memory_space_constraint(x, pltpu.HBM)


def shape(dims, dtype):
    return jax.ShapeDtypeStruct(dims, dtype)


def on_device(
    atm_state, atm_nbrs, atm_send, atm_mix, flux_weight, margin_counts, margin_weight,
    block_owner, recv_cols, ocn_state, ocn_nbrs, ocn_send, ocn_mix, force_weight, ret_weight,
):
    levels_air, columns = atm_state.shape[2:]
    levels_sea, cells = ocn_state.shape[2:]
    pair = atm_send.shape[2]
    half = pair // 2
    amount_air = atm_nbrs.shape[2]
    amount_sea = ocn_nbrs.shape[2]
    atm_groups, capacity, block = recv_cols.shape[2:]
    row_count = margin_weight.shape[2]
    blocks_here = block_owner.shape[2]
    fields = flux_weight.shape[0]
    ret_fields = ret_weight.shape[0]
    groups = lax.axis_size("grp")
    peers = lax.axis_size("dev")

    air = atm_state.reshape(levels_air, columns)
    sea = ocn_state.reshape(levels_sea, cells)
    counts = margin_counts.reshape(columns // 128, 128)
    weights = margin_weight.reshape(1, row_count)
    owner = block_owner.reshape(1, blocks_here)
    recv = recv_cols.reshape(atm_groups, capacity, block)
    air_mix = atm_mix.reshape(1, columns)
    air_shape = shape((levels_air, columns), F32)
    sea_shape = shape((levels_sea, cells), F32)
    air_rim = shape((levels_air, half), BF16)
    sea_rim = shape((levels_sea, half), BF16)
    payload_shape = shape((groups, capacity, fields, block), BF16)
    sent_shape = (capacity, fields, block)
    dma = pltpu.SemaphoreType.DMA

    def scratch(*dims, dtype=F32):
        return pltpu.VMEM(dims, dtype)

    air_scratch = scratch(levels_air, columns)
    sea_scratch = scratch(levels_sea, cells)
    air_marks = scratch(pair, columns, dtype=BF16)
    sea_marks_in = scratch(pair, cells, dtype=BF16)
    spread_in = scratch(row_count, columns, dtype=BF16)
    sea_half = scratch(levels_sea, half, dtype=BF16)
    pair_in = scratch(1, pair, dtype=I32)
    recv_in = scratch(atm_groups, capacity, block, dtype=I32)
    weights_in = scratch(1, row_count)
    air_row = scratch(1, columns)
    params = pltpu.CompilerParams(vmem_limit_bytes=60 * 2**20)

    def shifted(value, first, last, step):
        line = [
            (g * peers + i, g * peers + (i + step) % peers)
            for g in range(first, last)
            for i in range(peers)
        ]
        return in_hbm(lax.ppermute(value, ("grp", "dev"), line))

    down, up = pl.pallas_call(
        functools.partial(air_pack_kernel, atm_groups),
        out_shape=[air_rim] * 2,
        in_specs=[anywhere()] * 2,
        out_specs=[vmem(), vmem()],
        scratch_shapes=[air_scratch, pair_in, dma((2,))],
        compiler_params=params,
        name="air_pack",
    )(air, atm_send.reshape(1, pair))
    low = shifted(up, 0, atm_groups, 1)
    high = shifted(down, 0, atm_groups, -1)

    part, marks, spread, payload, air_pre, sea_down, sea_up = pl.pallas_call(
        functools.partial(air_own_kernel, atm_groups),
        out_shape=[
            air_shape,
            shape((pair, columns), BF16),
            shape((row_count, columns), BF16),
            payload_shape,
            air_shape,
            sea_rim,
            sea_rim,
        ],
        in_specs=[anywhere()] * 9,
        out_specs=[anywhere()] * 7,
        scratch_shapes=[
            air_scratch,
            scratch(amount_air, columns, dtype=I32),
            air_row,
            scratch(columns // 128, 128, dtype=I32),
            air_scratch,
            air_marks,
            spread_in,
            scratch(levels_air, columns, dtype=BF16),
            scratch(columns // 128, 128, dtype=I32),
            sea_scratch,
            pair_in,
            scratch(ret_fields, levels_sea),
            recv_in,
            scratch(16 * (cells // TILE), TILE, dtype=BF16),
            scratch(atm_groups, *sent_shape, dtype=BF16),
            sea_half,
            sea_half,
            dma((4,)),
            dma((4,)),
        ],
        compiler_params=params,
        cost_estimate=pl.CostEstimate(flops=4 * 10**9, bytes_accessed=10**7, transcendentals=0),
        name="air_own",
    )(
        up, air, atm_nbrs.reshape(amount_air, columns), air_mix, counts,
        sea, ocn_send.reshape(1, pair), ret_weight, recv,
    )
    payload, air_next, sea_down, sea_up = pl.pallas_call(
        functools.partial(air_send_kernel, atm_groups, amount_air),
        out_shape=[payload_shape, air_shape, sea_rim, sea_rim],
        in_specs=[anywhere()] * 3 + [vmem()] * 2 + [anywhere()] * 3 + [smem()] + [anywhere()] * 4,
        out_specs=[anywhere()] * 4,
        scratch_shapes=[
            air_scratch,
            air_marks,
            spread_in,
            air_row,
            scratch(fields, levels_air),
            weights_in,
            air_scratch,
            scratch(groups - atm_groups, *sent_shape, dtype=BF16),
            pltpu.SMEM((groups - atm_groups,), I32),
            dma((6,)),
            dma((2,)),
        ],
        input_output_aliases={11: 0, 12: 1, 9: 2, 10: 3},
        compiler_params=params,
        name="air_send",
    )(
        part, marks, spread, low, high, air_mix, flux_weight, weights, owner,
        sea_down, sea_up, payload, air_pre,
    )
    arrived = in_hbm(lax.all_to_all(payload, "grp", split_axis=0, concat_axis=0, tiled=True))
    sea_low = shifted(sea_up, atm_groups, groups, 1)
    sea_high = shifted(sea_down, atm_groups, groups, -1)

    sums, sea_marks, sea_pre = pl.pallas_call(
        functools.partial(sea_own_kernel, atm_groups),
        out_shape=[sea_shape, shape((pair, cells), BF16), sea_shape],
        in_specs=[anywhere()] * 3,
        out_specs=[anywhere()] * 3,
        scratch_shapes=[
            sea_scratch,
            scratch(amount_sea, 1, cells, dtype=I32),
            sea_scratch,
            sea_marks_in,
            scratch(levels_sea, cells, dtype=BF16),
            dma((2,)),
            dma((2,)),
        ],
        compiler_params=params,
        cost_estimate=pl.CostEstimate(flops=8 * 10**9, bytes_accessed=10**7, transcendentals=0),
        name="sea_own",
    )(payload, sea, ocn_nbrs.reshape(amount_sea, 1, cells))
    sea_next, mapped = pl.pallas_call(
        functools.partial(last_kernel, atm_groups, amount_sea),
        out_shape=[sea_shape, shape((ret_fields, 1, columns), F32)],
        in_specs=[vmem()] + [anywhere()] * 2 + [smem()] + [anywhere()] * 4 + [vmem()] * 2 + [anywhere()] * 3,
        out_specs=[anywhere()] * 2,
        scratch_shapes=[
            spread_in,
            weights_in,
            scratch(fields, row_count),
            scratch(ret_fields, 1, columns),
            pltpu.SMEM((groups - atm_groups,), I32),
            recv_in,
            sea_scratch,
            sea_scratch,
            sea_marks_in,
            scratch(1, cells),
            scratch(levels_sea, fields),
            dma((6,)),
            dma((2,)),
        ],
        input_output_aliases={12: 0},
        compiler_params=params,
        name="last",
    )(
        arrived, spread, weights, owner,
        recv, sea, sums, sea_marks, sea_low, sea_high, ocn_mix.reshape(1, cells), force_weight,
        sea_pre,
    )
    mapped = mapped.reshape(1, 1, ret_fields, columns)
    return (air_next[None, None], sea_next[None, None], mapped)


def solution(mesh):
    whole = P("grp", "dev")
    specs = [whole] * 15
    for replicated in (4, 13, 14):
        specs[replicated] = P()
    return jax.shard_map(
        on_device,
        mesh=mesh,
        in_specs=tuple(specs),
        out_specs=(whole, whole, whole),
        check_vma=False,
    )
```

time: 63.9 us -> 68.3 us (1.069)
  the two profiles are of different devices: /device:TPU:63 before, /device:TPU:1 now
where the time goes in v2:
time: 68.3 us; the launch traced here: 67.9 us
  Pallas kernels  40.2 us (59%)
  starting transfers between devices  24.9 us (36%)
  local copies, waits for them, and re-layouts  2.08 us (3%)
  between operations  0.77 us (1%)
    pallas_call x1, Pallas kernels, on_device(): pl.pallas_call(functools.partial(sea_own_kernel, atm_groups), out_shape=[...  21 us
    all_to_all x1, starting transfers between devices, on_device(): lax.all_to_all(payload, 'grp', split_axis=0, concat_axis=0, tiled=True)  12.6 us
    ppermute x4, starting transfers between devices, shifted(): return in_hbm(lax.ppermute(value, ('grp', 'dev'), line))  12.3 us
    pallas_call x1, Pallas kernels, on_device(): pl.pallas_call(functools.partial(air_send_kernel, atm_groups, amount_air)...  6.58 us
    pallas_call x1, Pallas kernels, on_device(): pl.pallas_call(functools.partial(air_own_kernel, atm_groups), out_shape=[...  6.06 us
    pallas_call x1, Pallas kernels, on_device(): pl.pallas_call(functools.partial(last_kernel, atm_groups, amount_sea), ou...  4.57 us
    unnamed x13, local copies, waits for them, and re-layouts  2.08 us
    pallas_call x1, Pallas kernels, on_device(): pl.pallas_call(functools.partial(air_pack_kernel, atm_groups), out_shape=...  1.95 us
  transfers between devices with their start and end apart: 5, of which 0 were waited for; matrix products, arithmetic and copies ran while one was open for 1% of the time, Pallas kernels for 40%

profile of v2, /device:TPU:1, one launch (start us, length us, event | category | flops | bytes accessed | tf_op | source)
XLA Modules:
  0.0 67.9 jit_solution(11021957086237227052)
XLA Ops:
  0.6 2.0 %air_pack.1 = (bf16[128,128]{1,0:T(8,128)(2,1)}, bf16[128,128]{1,0:T(8,128)(2,1)}) custom-call(f32[128,1024]{1,0:T(8,128)} %bitcast.22, s32[1,256]{1,0:T(1,128)} %bitcast.33), custom_call_target="tpu_custom_call" | custom-call | tf_op jit(solution)/shard_map/air_pack/pallas_call | solution.py:459
  2.6 9.0 %collective-permute-start.1 = (bf16[128,128]{1,0:T(8,128)(2,1)}, bf16[128,128]{1,0:T(8,128)(2,1)S(1)}, u32[]{:S(2)}, u32[]{:S(2)}) collective-permute-start(bf16[128,128]{1,0:T(8,128)(2,1)} %get-tuple-element.25), channel_id=1, source_target_pairs={{0,63},{1,0},{2,1},{3,2},{4,3},{5,4},{6,5},{7,6},{8,7},{9,8},{10,9... | collective-permute-start | bytes 98312 | tf_op jit(solution)/shard_map/ppermute | solution.py:457
  11.6 1.9 %collective-permute-start = (bf16[128,128]{1,0:T(8,128)(2,1)}, bf16[128,128]{1,0:T(8,128)(2,1)S(1)}, u32[]{:S(2)}, u32[]{:S(2)}) collective-permute-start(bf16[128,128]{1,0:T(8,128)(2,1)} %get-tuple-element.21.after), channel_id=1, source_target_pairs={{0,1},{1,2},{2,3},{3,4},{4,5},{5,6},{6,7},{7,8},{8,9},{9,10},{10,1... | collective-permute-start | bytes 98312 | tf_op jit(solution)/shard_map/ppermute | solution.py:457
  13.6 0.0 copy-start.5
  13.6 6.1 %air_own.1 = (f32[128,1024]{1,0:T(8,128)}, bf16[256,1024]{1,0:T(8,128)(2,1)}, bf16[1536,1024]{1,0:T(8,128)(2,1)}, bf16[16,4,24,128]{3,2,1,0:T(8,128)(2,1)}, f32[...) custom-call(bf16[128,128]{1,0:T(8,128)(2,1)} %get-tuple-element.21.after, f32[128,1024]{1,0:T(8,128)} %bitcast.23, ...), custom_call_target="tpu_custom_call" | custom-call | flops 4000000000 | bytes 10000000 | tf_op jit(solution)/shard_map/air_own/pallas_call | solution.py:471
  19.6 0.0 copy-done.5
  19.6 0.7 %copy.23.force_weight_ref = f32[80,24]{1,0:T(8,128)} copy(f32[80,24]{0,1:T(8,128)S(1)} %copy-done.5) | data formatting | bytes 15360 | tf_op args[13]
  20.3 0.0 collective-permute-done.1.high
  20.4 0.0 copy-start.1
  20.4 0.0 collective-permute-done.low
  20.4 0.0 copy-start.2
  20.4 0.6 copy-done.1
  21.0 0.0 copy-done.2
  21.0 6.6 %air_send.1 = (bf16[16,4,24,128]{3,2,1,0:T(8,128)(2,1)}, f32[128,1024]{1,0:T(8,128)}, bf16[80,128]{1,0:T(8,128)(2,1)}, bf16[80,128]{1,0:T(8,128)(2,1)}) custom-call(f32[128,1024]{1,0:T(8,128)} %get-tuple-element.22.part_ref, ...), custom_call_target="tpu_custom_call", output_to_operand_aliasing={{0}: (11, {}), {1}: (12, {}), {2}: (9, {}), {3}: (10, {})} | custom-call | tf_op jit(solution)/shard_map/air_send/pallas_call | solution.py:512
  27.6 12.6 %all-to-all-start = ((bf16[16,4,24,128]{3,2,1,0:T(8,128)(2,1)}), bf16[16,4,24,128]{3,2,1,0:T(8,128)(2,1)S(1)}, u32[]{:S(2)}, u32[]{:S(2)}) async-start(bf16[16,4,24,128]{3,2,1,0:T(8,128)(2,1)} %get-tuple-element.31.after), calls=%async_computation | async-start | bytes 786432 | tf_op jit(solution)/shard_map/all_to_all | solution.py:537
  40.2 0.7 collective-permute-start.2
  40.8 0.7 collective-permute-start.3
  41.5 21.0 %sea_own.1 = (f32[80,2048]{1,0:T(8,128)}, bf16[256,2048]{1,0:T(8,128)(2,1)}, f32[80,2048]{1,0:T(8,128)}) custom-call(bf16[16,4,24,128]{3,2,1,0:T(8,128)(2,1)} %get-tuple-element.31.after, f32[80,2048]{1,0:T(8,128)} %bitcast.18, s32[6,1,2048]{2,1,0:T(1,128)} %bitcast.34), custom_call_target="tpu_custom_call" | custom-call | flops 8000000000 | bytes 10000000 | tf_op jit(solution)/shard_map/sea_own/pallas_call | solution.py:541
  62.5 0.0 collective-permute-done.2.low
  62.5 0.0 copy-start.3
  62.5 0.0 collective-permute-done.3.high
  62.5 0.0 copy-start.4
  62.6 0.0 all-to-all-done.arrived
  62.6 0.0 copy-start
  62.6 0.5 copy-done.3
  63.1 0.0 copy-done.4
  63.1 0.2 copy-done
  63.3 4.6 %last.1 = (f32[80,2048]{1,0:T(8,128)}, f32[12,1,1024]{2,1,0:T(1,128)}) custom-call(bf16[16,4,24,128]{3,2,1,0:T(8,128)(2,1)} %copy-done, bf16[1536,1024]{1,0:T(8,128)(2,1)} %get-tuple-element.24.spread_ref, f32[1,1536]{1,0:T(1,128)} %bitcast.25, s32[1,12]{1,0:T(1,128)} %bitcast.32, s32[8,4,128]{2,1,0:T(4,128)} %bitcast.27, ...), custom_call_target="tpu_custom_call", output_to_operand_aliasing={{0}: (12, {})} | custom-call | tf_op jit(solution)/shard_map/last/pallas_call | solution.py:559
Async XLA Ops:
  2.6 17.8 %collective-permute-start.1 = (bf16[128,128]{1,0:T(8,128)(2,1)}, bf16[128,128]{1,0:T(8,128)(2,1)S(1)}, u32[]{:S(2)}, u32[]{:S(2)}) collective-permute-start(bf16[128,128]{1,0:T(8,128)(2,1)} %get-tuple-element.25), channel_id=1, source_target_pairs={{0,63},{1,0},{2,1},{3,2},{4,3},{5,4},{6,5},{7,6},{8,7},{9,8},{10,9... | collective-permute-start | bytes 98312 | tf_op jit(solution)/shard_map/ppermute | solution.py:457
  11.6 8.7 %collective-permute-start = (bf16[128,128]{1,0:T(8,128)(2,1)}, bf16[128,128]{1,0:T(8,128)(2,1)S(1)}, u32[]{:S(2)}, u32[]{:S(2)}) collective-permute-start(bf16[128,128]{1,0:T(8,128)(2,1)} %get-tuple-element.21.after), channel_id=1, source_target_pairs={{0,1},{1,2},{2,3},{3,4},{4,5},{5,6},{6,7},{7,8},{8,9},{9,10},{10,1... | collective-permute-start | bytes 98312 | tf_op jit(solution)/shard_map/ppermute | solution.py:457
  13.6 6.1 %copy-start.5 = (f32[80,24]{0,1:T(8,128)S(1)}, f32[80,24]{0,1:T(8,128)}, u32[]{:S(2)}) copy-start(f32[80,24]{0,1:T(8,128)} %param.28) | copy-start | bytes 23044
  20.4 0.6 copy-start.1
  20.4 0.6 copy-start.2
  27.6 35.0 %all-to-all-start = ((bf16[16,4,24,128]{3,2,1,0:T(8,128)(2,1)}), bf16[16,4,24,128]{3,2,1,0:T(8,128)(2,1)S(1)}, u32[]{:S(2)}, u32[]{:S(2)}) async-start(bf16[16,4,24,128]{3,2,1,0:T(8,128)(2,1)} %get-tuple-element.31.after), calls=%async_computation | async-start | bytes 786432 | tf_op jit(solution)/shard_map/all_to_all | solution.py:537
  40.2 22.3 %collective-permute-start.2 = (bf16[80,128]{1,0:T(8,128)(2,1)}, bf16[80,128]{1,0:T(8,128)(2,1)S(1)}, u32[]{:S(2)}, u32[]{:S(2)}) collective-permute-start(bf16[80,128]{1,0:T(8,128)(2,1)} %get-tuple-element.34), channel_id=1, source_target_pairs={{512,513},{513,514},{514,515},{515,516},{516,517},{517,518},{518,5... | collective-permute-start | bytes 61448 | tf_op jit(solution)/shard_map/ppermute | solution.py:457
  40.8 21.7 %collective-permute-start.3 = (bf16[80,128]{1,0:T(8,128)(2,1)}, bf16[80,128]{1,0:T(8,128)(2,1)S(1)}, u32[]{:S(2)}, u32[]{:S(2)}) collective-permute-start(bf16[80,128]{1,0:T(8,128)(2,1)} %get-tuple-element.35), channel_id=1, source_target_pairs={{512,575},{513,512},{514,513},{515,514},{516,515},{517,516},{518,5... | collective-permute-start | bytes 61448 | tf_op jit(solution)/shard_map/ppermute | solution.py:457
  62.5 0.6 copy-start.3
  62.5 0.6 copy-start.4
  62.6 0.8 %copy-start = (bf16[16,4,24,128]{3,2,1,0:T(8,128)(2,1)}, bf16[16,4,24,128]{3,2,1,0:T(8,128)(2,1)S(1)}, u32[]{:S(2)}) copy-start(bf16[16,4,24,128]{3,2,1,0:T(8,128)(2,1)S(1)} %all-to-all-done.arrived) | copy-start | bytes 1179652

commit v3 on v2

--- a/solution.py
+++ b/solution.py
@@ -10,6 +10,7 @@
 F32 = jnp.float32
 BF16 = jnp.bfloat16
 I32 = jnp.int32
+I16 = jnp.int16
 TILE = 256
 NT = (((1,), (1,)), ((), ()))
 
@@ -93,7 +94,7 @@
         pack_into(air, send, down, up)
 
 
-def own_sums(pool, nbrs, at, width):
+def sums_of(pool, nbrs, at, width):
     rows = row_marks(TILE, width)
     picks = [n[:, pl.ds(at, width)] for n in nbrs]
     total = None
@@ -122,16 +123,53 @@
         before = before + whole[j : j + 1]
 
 
-def fill_spread(counts, ends, spread):
-    fill_ends(counts, ends)
-    rows, _ = spread.shape
+def interval(order, begin, end):
+    return jnp.where((order >= begin) & (order < end), jnp.ones((), BF16), jnp.zeros((), BF16))
+
+
+def fill_limits(counts, ends, begins_at, ends_at):
     blocks, lanes = counts.shape
-    order = row_iota(rows, lanes)
+    end = jnp.transpose(ends[...].astype(F32)).astype(I32)
+    begin = jnp.transpose((ends[...] - counts[...]).astype(F32)).astype(I32)
     for j in range(blocks):
-        end = ends[j : j + 1, :]
-        begin = end - counts[j : j + 1, :]
-        inside = (order >= begin) & (order < end)
-        spread[:, j * lanes : (j + 1) * lanes] = jnp.where(inside, 1.0, 0.0).astype(BF16)
+        at = slice(j * lanes, (j + 1) * lanes)
+        ends_at[at, :] = jnp.broadcast_to(end[:, j : j + 1], (lanes, lanes)).astype(I16)
+        begins_at[at, :] = jnp.broadcast_to(begin[:, j : j + 1], (lanes, lanes)).astype(I16)
+
+
+def spread_rows(values, begins_at, ends_at, tile):
+    columns, lanes = ends_at.shape
+    reach = (columns // 2) // TILE
+    lane = lax.broadcasted_iota(I32, (TILE, lanes), 1)
+    total = None
+    for t in range(max(0, tile - reach), min(tile, columns // TILE - 1) + 1):
+        at = slice(t * TILE, (t + 1) * TILE)
+        sides = []
+        for side in range(TILE // lanes):
+            order = (lane + (tile * TILE + side * lanes)).astype(I16)
+            sides.append(interval(order, begins_at[at, :], ends_at[at, :]))
+        part = dot(values[:, at], jnp.concatenate(sides, axis=1))
+        total = part if total is None else total + part
+    return total
+
+
+def gather_rows(values, counts, ends, tile):
+    blocks, lanes = counts.shape
+    reach = (blocks * lanes // 2) // TILE
+    each = TILE // lanes
+    end = jnp.concatenate([ends[tile * each + i : tile * each + i + 1, :] for i in range(each)], axis=1)
+    count = jnp.concatenate(
+        [counts[tile * each + i : tile * each + i + 1, :] for i in range(each)], axis=1
+    )
+    begin = (end - count).astype(I16)
+    end = end.astype(I16)
+    rows = row_iota(TILE, TILE)
+    total = None
+    for t in range(tile, tile + reach + 1):
+        mark = interval((rows + t * TILE).astype(I16), begin, end)
+        part = dot(values[:, t * TILE : (t + 1) * TILE], mark)
+        total = part if total is None else total + part
+    return total
 
 
 def slots_of(owner, seen, visit):
@@ -169,47 +207,75 @@
             looked[s, k] = look[:, k * block : (k + 1) * block]
 
 
-def air_own_kernel(
+def mid_kernel(
     atm_groups,
-    after, air_ref, air_nbrs_ref, air_mix_ref, counts_ref,
+    low, high, air_ref, air_nbrs_ref, air_mix_ref, counts_ref, flux_weight_ref, weights_ref, owner,
     sea_ref, sea_send_ref, ret_weight_ref, recv_ref,
-    part_ref, marks_ref, spread_ref, payload, air_out, sea_down_ref, sea_up_ref,
-    air, air_nbrs, air_mix, counts, part, marks, spread, pool, ends,
-    sea, sea_send, ret_weight, recv, returned, looked, down, up, sems, out_sems,
+    payload, air_out, sea_down_ref, sea_up_ref,
+    air, air_nbrs, air_mix, counts, flux_weight, weights,
+    pool, ends, begins_at, ends_at, values, sent, seen,
+    sea, sea_send, ret_weight, recv, returned, down, up, sems, out_sems,
 ):
     here = lax.axis_index("grp") < atm_groups
+    count_groups = sent.shape[0]
 
     @pl.when(here)
     def _():
-        near, many, whole, mixed = fetch_all(
-            [(air_nbrs_ref, air_nbrs), (counts_ref, counts), (air_ref, air), (air_mix_ref, air_mix)],
+        many, near, whole, mixed, *rest = fetch_all(
+            [
+                (counts_ref, counts),
+                (air_nbrs_ref, air_nbrs),
+                (air_ref, air),
+                (air_mix_ref, air_mix),
+                (flux_weight_ref, flux_weight),
+                (weights_ref, weights),
+            ],
             sems,
         )
+        sent[...] = jnp.zeros(sent.shape, BF16)
+        values[...] = jnp.zeros(values.shape, BF16)
+        many.wait()
+        fill_ends(counts, ends)
+        fill_limits(counts, ends, begins_at, ends_at)
         amount, columns = air_nbrs.shape
+        half = low.shape[1]
+        pool[:, columns : columns + half] = low[...]
+        pool[:, columns + half :] = high[...]
+        wait_all([near, whole, mixed, *rest])
+        pool[:, :columns] = air[...].astype(BF16)
         nbrs = [air_nbrs.at[k : k + 1, :] for k in range(amount)]
-        many.wait()
-        fill_spread(counts, ends, spread)
-        out_spread = fetch(spread, spread_ref, out_sems.at[0])
-        near.wait()
+        fields = flux_weight.shape[0]
         for at in range(0, columns, TILE):
-            marks[:, at : at + TILE] = rim_marks(nbrs, at, TILE, columns)
-        out_marks = fetch(marks, marks_ref, out_sems.at[1])
-        wait_all([whole, mixed])
-        pool[...] = air[...].astype(BF16)
-        for at in range(0, columns, TILE):
-            mix = air_mix[:, at : at + TILE]
-            total = own_sums(pool, nbrs, at, TILE)
+            total = sums_of(pool, nbrs, at, TILE)
             own = air[:, at : at + TILE]
-            part[:, at : at + TILE] = own + mix * (total * (1.0 / amount) - own)
-        out_part = fetch(part, part_ref, out_sems.at[2])
-        wait_all([out_spread, out_marks, out_part])
+            new = own + air_mix[:, at : at + TILE] * (total * (1.0 / amount) - own)
+            air[:, at : at + TILE] = new
+            hi, lo = split(exact(flux_weight[...], new))
+            values[0:fields, at : at + TILE] = hi
+            values[32 : 32 + fields, at : at + TILE] = lo
+        stored = fetch(air, air_out, out_sems.at[0])
+        block = sent.shape[3]
+        each = TILE // block
+        tiles = []
+        for t in range(weights.shape[1] // TILE):
+            both = spread_rows(values, begins_at, ends_at, t)
+            tile = (both[0:fields] + both[32 : 32 + fields]) * weights[:, t * TILE : (t + 1) * TILE]
+            tiles.append(tile.astype(BF16))
+
+        def visit(b, o, k):
+            i = b % each
+            sent[o, k] = tiles[b // each][:, i * block : (i + 1) * block]
+
+        slots_of(owner, seen, visit)
+        done = fetch(sent, payload.at[pl.ds(atm_groups, count_groups)], out_sems.at[1])
+        wait_all([stored, done])
 
     @pl.when(jnp.logical_not(here))
     def _():
-        keep = fetch(air_ref, air_out, out_sems.at[0])
-        listed, *rest = fetch_all(
+        listed, kept, *rest = fetch_all(
             [
                 (sea_send_ref, sea_send),
+                (air_ref, air),
                 (sea_ref, sea),
                 (ret_weight_ref, ret_weight),
                 (recv_ref, recv),
@@ -217,60 +283,15 @@
             sems,
         )
         wait_all(rest)
-        look_up(sea, ret_weight, recv, returned, looked)
-        sent = fetch(looked, payload.at[pl.ds(0, atm_groups)], out_sems.at[1])
+        look_up(sea, ret_weight, recv, returned, sent)
+        done = fetch(sent, payload.at[pl.ds(0, atm_groups)], out_sems.at[1])
+        kept.wait()
+        keep = fetch(air, air_out, out_sems.at[0])
         listed.wait()
         pack_into(sea, sea_send, down, up)
         out_down = fetch(down, sea_down_ref, out_sems.at[2])
         out_up = fetch(up, sea_up_ref, out_sems.at[3])
-        wait_all([sent, out_down, out_up, keep])
-
-
-def air_send_kernel(
-    atm_groups, amount,
-    part_ref, marks_ref, spread_ref, low, high, air_mix_ref, flux_weight_ref, weights_ref,
-    owner, sea_down_in, sea_up_in, payload_in, air_in,
-    payload, air_out, sea_down, sea_up,
-    part, marks, spread, air_mix, flux_weight, weights,
-    air, rows_out, seen, sems, out_sems,
-):
-    @pl.when(lax.axis_index("grp") < atm_groups)
-    def _():
-        last, spreading, *first = fetch_all(
-            [
-                (weights_ref, weights),
-                (spread_ref, spread),
-                (marks_ref, marks),
-                (part_ref, part),
-                (air_mix_ref, air_mix),
-                (flux_weight_ref, flux_weight),
-            ],
-            sems,
-        )
-        rows_out[...] = jnp.zeros(rows_out.shape, BF16)
-        columns = air.shape[1]
-        wait_all(first)
-        rim = jnp.concatenate([low[...], high[...]], axis=1)
-        parts = []
-        for at in range(0, columns, TILE):
-            total = dot(rim, marks[:, at : at + TILE])
-            new = part[:, at : at + TILE] + air_mix[:, at : at + TILE] * (total * (1.0 / amount))
-            air[:, at : at + TILE] = new
-            parts.append(exact(flux_weight[...], new))
-        stored = fetch(air, air_out, out_sems.at[0])
-        hi, lo = split(jnp.concatenate(parts, axis=1))
-        block = rows_out.shape[3]
-        wait_all([last, spreading])
-
-        def visit(b, o, k):
-            mark = spread[b * block : (b + 1) * block, :]
-            value = dot_nt(hi, mark) + dot_nt(lo, mark)
-            value = value * weights[:, b * block : (b + 1) * block]
-            rows_out[o, k] = value.astype(BF16)
-
-        slots_of(owner, seen, visit)
-        sent = fetch(rows_out, payload.at[pl.ds(atm_groups, rows_out.shape[0])], out_sems.at[1])
-        wait_all([stored, sent])
+        wait_all([done, keep, out_down, out_up])
 
 
 def sea_own_kernel(
@@ -283,7 +304,8 @@
 
     @pl.when(here)
     def _():
-        fetch(sea_ref, sea_out, out_sems.at[0]).wait()
+        fetch(sea_ref, sea, sems.at[0]).wait()
+        fetch(sea, sea_out, out_sems.at[0]).wait()
 
     @pl.when(jnp.logical_not(here))
     def _():
@@ -299,7 +321,7 @@
 
         def step(i, carry):
             at = pl.multiple_of(i * TILE, TILE)
-            sums[:, pl.ds(at, TILE)] = own_sums(pool, nbrs, at, TILE)
+            sums[:, pl.ds(at, TILE)] = sums_of(pool, nbrs, at, TILE)
             return carry
 
         lax.fori_loop(0, cells // TILE, step, 0)
@@ -309,10 +331,10 @@
 
 def last_kernel(
     atm_groups, amount,
-    arrived, spread_ref, weights_ref, owner,
+    arrived, counts_ref, weights_ref, owner,
     recv_ref, sea_ref, sums_ref, marks_ref, low, high, sea_mix_ref, force_weight_ref, sea_in,
     sea_out, mapped_ref,
-    spread, weights, mine, mapped, seen,
+    counts, ends, weights, mine, mapped, seen,
     recv, sea, sums, marks, sea_mix, force_weight, sems, out_sems,
 ):
     here = lax.axis_index("grp") < atm_groups
@@ -320,24 +342,28 @@
 
     @pl.when(here)
     def _():
-        given, spreading = fetch_all([(weights_ref, weights), (spread_ref, spread)], sems)
+        many, given = fetch_all([(counts_ref, counts), (weights_ref, weights)], sems)
         block = arrived.shape[3]
-        given.wait()
 
         def visit(b, o, k):
             mine[:, b * block : (b + 1) * block] = arrived[atm_groups + o, k].astype(F32)
 
         slots_of(owner, seen, visit)
+        many.wait()
+        fill_ends(counts, ends)
+        given.wait()
         w = weights[...]
         scaled = mine[0:16, :] * w
         order = row_iota(16, scaled.shape[1])
         scaled = jnp.where(order < fields, scaled, jnp.where(order == fields, w, 0.0))
         hi, lo = split(scaled)
-        spreading.wait()
-        both = dot(hi, spread[...]) + dot(lo, spread[...])
-        mean = both[0:fields] / both[fields : fields + 1]
-        for f in range(fields):
-            mapped[f] = mean[f : f + 1]
+        both_in = jnp.concatenate([hi, lo], axis=0)
+        for t in range(columns // TILE):
+            both = gather_rows(both_in, counts, ends, t)
+            both = both[0:16] + both[16:32]
+            mean = both[0:fields] / both[fields : fields + 1]
+            for f in range(fields):
+                mapped[f, :, t * TILE : (t + 1) * TILE] = mean[f : f + 1]
         fetch(mapped, mapped_ref, out_sems.at[0]).wait()
 
     @pl.when(jnp.logical_not(here))
@@ -370,9 +396,10 @@
             flux = flux + dot_nt(apart, one_hot(row_marks(TILE, slots * block), rest_of))
         wait_all(rest)
         rim = jnp.concatenate([low[...], high[...]], axis=1)
+        spread_weight = jnp.transpose(force_weight[...])
         for h in range(his):
             at = slice(h * TILE, (h + 1) * TILE)
-            forcing = exact(force_weight[...], flux[h * rows : (h + 1) * rows])
+            forcing = exact(spread_weight, flux[h * rows : (h + 1) * rows])
             total = sums[:, at] + dot(rim, marks[:, at])
             own = sea[:, at]
             sea[:, at] = own + sea_mix[:, at] * (total * (1.0 / amount) - own) + forcing
@@ -418,13 +445,13 @@
     groups = lax.axis_size("grp")
     peers = lax.axis_size("dev")
 
-    air = atm_state.reshape(levels_air, columns)
-    sea = ocn_state.reshape(levels_sea, cells)
-    counts = margin_counts.reshape(columns // 128, 128)
-    weights = margin_weight.reshape(1, row_count)
-    owner = block_owner.reshape(1, blocks_here)
-    recv = recv_cols.reshape(atm_groups, capacity, block)
-    air_mix = atm_mix.reshape(1, columns)
+    air = in_hbm(atm_state.reshape(levels_air, columns))
+    sea = in_hbm(ocn_state.reshape(levels_sea, cells))
+    counts = in_hbm(margin_counts.reshape(columns // 128, 128))
+    weights = in_hbm(margin_weight.reshape(1, row_count))
+    owner = in_hbm(block_owner.reshape(1, blocks_here))
+    recv = in_hbm(recv_cols.reshape(atm_groups, capacity, block))
+    air_mix = in_hbm(atm_mix.reshape(1, columns))
     air_shape = shape((levels_air, columns), F32)
     sea_shape = shape((levels_sea, cells), F32)
     air_rim = shape((levels_air, half), BF16)
@@ -438,15 +465,14 @@
 
     air_scratch = scratch(levels_air, columns)
     sea_scratch = scratch(levels_sea, cells)
-    air_marks = scratch(pair, columns, dtype=BF16)
     sea_marks_in = scratch(pair, cells, dtype=BF16)
-    spread_in = scratch(row_count, columns, dtype=BF16)
+    counts_in = scratch(columns // 128, 128, dtype=I32)
     sea_half = scratch(levels_sea, half, dtype=BF16)
     pair_in = scratch(1, pair, dtype=I32)
     recv_in = scratch(atm_groups, capacity, block, dtype=I32)
     weights_in = scratch(1, row_count)
     air_row = scratch(1, columns)
-    params = pltpu.CompilerParams(vmem_limit_bytes=60 * 2**20)
+    params = pltpu.CompilerParams(vmem_limit_bytes=24 * 2**20)
 
     def shifted(value, first, last, step):
         line = [
@@ -454,7 +480,7 @@
             for g in range(first, last)
             for i in range(peers)
         ]
-        return in_hbm(lax.ppermute(value, ("grp", "dev"), line))
+        return lax.ppermute(value, ("grp", "dev"), line)
 
     down, up = pl.pallas_call(
         functools.partial(air_pack_kernel, atm_groups),
@@ -464,77 +490,46 @@
         scratch_shapes=[air_scratch, pair_in, dma((2,))],
         compiler_params=params,
         name="air_pack",
-    )(air, atm_send.reshape(1, pair))
+    )(air, in_hbm(atm_send.reshape(1, pair)))
     low = shifted(up, 0, atm_groups, 1)
     high = shifted(down, 0, atm_groups, -1)
 
-    part, marks, spread, payload, air_pre, sea_down, sea_up = pl.pallas_call(
-        functools.partial(air_own_kernel, atm_groups),
-        out_shape=[
-            air_shape,
-            shape((pair, columns), BF16),
-            shape((row_count, columns), BF16),
-            payload_shape,
-            air_shape,
-            sea_rim,
-            sea_rim,
-        ],
-        in_specs=[anywhere()] * 9,
-        out_specs=[anywhere()] * 7,
+    payload, air_next, sea_down, sea_up = pl.pallas_call(
+        functools.partial(mid_kernel, atm_groups),
+        out_shape=[payload_shape, air_shape, sea_rim, sea_rim],
+        in_specs=[vmem()] * 2 + [anywhere()] * 6 + [smem()] + [anywhere()] * 4,
+        out_specs=[anywhere()] * 4,
         scratch_shapes=[
             air_scratch,
             scratch(amount_air, columns, dtype=I32),
             air_row,
-            scratch(columns // 128, 128, dtype=I32),
-            air_scratch,
-            air_marks,
-            spread_in,
-            scratch(levels_air, columns, dtype=BF16),
-            scratch(columns // 128, 128, dtype=I32),
+            counts_in,
+            scratch(fields, levels_air),
+            weights_in,
+            scratch(levels_air, columns + pair, dtype=BF16),
+            counts_in,
+            scratch(columns, 128, dtype=I16),
+            scratch(columns, 128, dtype=I16),
+            scratch(64, columns, dtype=BF16),
+            scratch(atm_groups, *sent_shape, dtype=BF16),
+            pltpu.SMEM((groups - atm_groups,), I32),
             sea_scratch,
             pair_in,
             scratch(ret_fields, levels_sea),
             recv_in,
             scratch(16 * (cells // TILE), TILE, dtype=BF16),
-            scratch(atm_groups, *sent_shape, dtype=BF16),
             sea_half,
             sea_half,
-            dma((4,)),
+            dma((6,)),
             dma((4,)),
         ],
         compiler_params=params,
-        cost_estimate=pl.CostEstimate(flops=4 * 10**9, bytes_accessed=10**7, transcendentals=0),
-        name="air_own",
+        name="mid",
     )(
-        up, air, atm_nbrs.reshape(amount_air, columns), air_mix, counts,
-        sea, ocn_send.reshape(1, pair), ret_weight, recv,
+        low, high, air, in_hbm(atm_nbrs.reshape(amount_air, columns)), air_mix, counts, in_hbm(flux_weight),
+        weights, owner, sea, in_hbm(ocn_send.reshape(1, pair)), in_hbm(ret_weight), recv,
     )
-    payload, air_next, sea_down, sea_up = pl.pallas_call(
-        functools.partial(air_send_kernel, atm_groups, amount_air),
-        out_shape=[payload_shape, air_shape, sea_rim, sea_rim],
-        in_specs=[anywhere()] * 3 + [vmem()] * 2 + [anywhere()] * 3 + [smem()] + [anywhere()] * 4,
-        out_specs=[anywhere()] * 4,
-        scratch_shapes=[
-            air_scratch,
-            air_marks,
-            spread_in,
-            air_row,
-            scratch(fields, levels_air),
-            weights_in,
-            air_scratch,
-            scratch(groups - atm_groups, *sent_shape, dtype=BF16),
-            pltpu.SMEM((groups - atm_groups,), I32),
-            dma((6,)),
-            dma((2,)),
-        ],
-        input_output_aliases={11: 0, 12: 1, 9: 2, 10: 3},
-        compiler_params=params,
-        name="air_send",
-    )(
-        part, marks, spread, low, high, air_mix, flux_weight, weights, owner,
-        sea_down, sea_up, payload, air_pre,
-    )
-    arrived = in_hbm(lax.all_to_all(payload, "grp", split_axis=0, concat_axis=0, tiled=True))
+    arrived = lax.all_to_all(payload, "grp", split_axis=0, concat_axis=0, tiled=True)
     sea_low = shifted(sea_up, atm_groups, groups, 1)
     sea_high = shifted(sea_down, atm_groups, groups, -1)
 
@@ -555,14 +550,15 @@
         compiler_params=params,
         cost_estimate=pl.CostEstimate(flops=8 * 10**9, bytes_accessed=10**7, transcendentals=0),
         name="sea_own",
-    )(payload, sea, ocn_nbrs.reshape(amount_sea, 1, cells))
+    )(payload, sea, in_hbm(ocn_nbrs.reshape(amount_sea, 1, cells)))
     sea_next, mapped = pl.pallas_call(
         functools.partial(last_kernel, atm_groups, amount_sea),
         out_shape=[sea_shape, shape((ret_fields, 1, columns), F32)],
         in_specs=[vmem()] + [anywhere()] * 2 + [smem()] + [anywhere()] * 4 + [vmem()] * 2 + [anywhere()] * 3,
         out_specs=[anywhere()] * 2,
         scratch_shapes=[
-            spread_in,
+            counts_in,
+            counts_in,
             weights_in,
             scratch(fields, row_count),
             scratch(ret_fields, 1, columns),
@@ -572,7 +568,7 @@
             sea_scratch,
             sea_marks_in,
             scratch(1, cells),
-            scratch(levels_sea, fields),
+            scratch(fields, levels_sea),
             dma((6,)),
             dma((2,)),
         ],
@@ -580,8 +576,8 @@
         compiler_params=params,
         name="last",
     )(
-        arrived, spread, weights, owner,
-        recv, sea, sums, sea_marks, sea_low, sea_high, ocn_mix.reshape(1, cells), force_weight,
+        arrived, counts, weights, owner,
+        recv, sea, sums, sea_marks, sea_low, sea_high, in_hbm(ocn_mix.reshape(1, cells)), in_hbm(force_weight.T),
         sea_pre,
     )
     mapped = mapped.reshape(1, 1, ret_fields, columns)

time: 68.3 us -> 52.6 us (0.77)
  Pallas kernels: 40.2 us -> 10.7 us
  waiting for transfers between devices: 0.01 us -> 12.2 us
  starting transfers between devices: 24.9 us -> 28.6 us
  local copies, waits for them, and re-layouts: 2.08 us -> 0 us
    pallas_call x1, Pallas kernels: 21 us -> 1.97 us  [on_device(): pl.pallas_call(functools.partial(sea_own_kernel, atm_groups), out_shape=[...]
    all_to_all x1, waiting for transfers between devices: 0.01 us -> 11.2 us  [on_device(): lax.all_to_all(payload, 'grp', split_axis=0, concat_axis=0, tiled=True)]
    pallas_call x2 -> x1, Pallas kernels: 12.6 us -> 4.82 us  [on_device(): pl.pallas_call(functools.partial(mid_kernel, atm_groups), out_shape=[payl...]
    all_to_all x1, starting transfers between devices: 12.6 us -> 16.3 us  [on_device(): lax.all_to_all(payload, 'grp', split_axis=0, concat_axis=0, tiled=True)]
    unnamed x13 -> x0, local copies, waits for them, and re-layouts: 2.08 us -> none
    pallas_call x1, Pallas kernels: 4.57 us -> 2.6 us  [on_device(): pl.pallas_call(functools.partial(last_kernel, atm_groups, amount_sea), ou...]
    ppermute x4, waiting for transfers between devices: 0.01 us -> 1 us  [shifted(): return lax.ppermute(value, ('grp', 'dev'), line)]
  transfers between devices with their start and end apart: 5 -> 5, of which waited for: 0 -> 2; matrix products, arithmetic and copies ran while one was open for 1% -> 0% of each run, Pallas kernels for 40% -> 4%
where the time goes in v3:
time: 52.6 us; the launch traced here: 52.2 us
  starting transfers between devices  28.6 us (54%)
  waiting for transfers between devices  12.2 us (23%)
  Pallas kernels  10.7 us (20%)
  between operations  0.71 us (1%)
    all_to_all x1, starting transfers between devices, on_device(): lax.all_to_all(payload, 'grp', split_axis=0, concat_axis=0, tiled=True)  16.3 us
    ppermute x4, starting transfers between devices, shifted(): return lax.ppermute(value, ('grp', 'dev'), line)  12.3 us
    all_to_all x1, waiting for transfers between devices, on_device(): lax.all_to_all(payload, 'grp', split_axis=0, concat_axis=0, tiled=True)  11.2 us
    pallas_call x1, Pallas kernels, on_device(): pl.pallas_call(functools.partial(mid_kernel, atm_groups), out_shape=[payl...  4.82 us
    pallas_call x1, Pallas kernels, on_device(): pl.pallas_call(functools.partial(last_kernel, atm_groups, amount_sea), ou...  2.6 us
    pallas_call x1, Pallas kernels, on_device(): pl.pallas_call(functools.partial(sea_own_kernel, atm_groups), out_shape=[...  1.97 us
    pallas_call x1, Pallas kernels, on_device(): pl.pallas_call(functools.partial(air_pack_kernel, atm_groups), out_shape=...  1.33 us
  transfers between devices with their start and end apart: 5, of which 2 were waited for; matrix products, arithmetic and copies ran while one was open for 0% of the time, Pallas kernels for 4%

profile of v3, /device:TPU:1, one launch (start us, length us, event | category | flops | bytes accessed | tf_op | source)
XLA Modules:
  0.0 52.2 jit_solution(16998298833920852157)
XLA Ops:
  0.6 1.3 %air_pack.1 = (bf16[128,128]{1,0:T(8,128)(2,1)S(1)}, bf16[128,128]{1,0:T(8,128)(2,1)S(1)}) custom-call(f32[128,1024]{1,0:T(8,128)} %bitcast.21, s32[1,256]{1,0:T(1,128)} %bitcast.36), custom_call_target="tpu_custom_call" | custom-call | tf_op jit(solution)/shard_map/air_pack/pallas_call | solution.py:485
  2.0 3.9 %collective-permute-start = (bf16[128,128]{1,0:T(8,128)(2,1)S(1)}, bf16[128,128]{1,0:T(8,128)(2,1)S(1)}, u32[]{:S(2)}, u32[]{:S(2)}) collective-permute-start(bf16[128,128]{1,0:T(8,128)(2,1)S(1)} %get-tuple-element.14), channel_id=1, source_target_pairs={{0,1},{1,2},{2,3},{3,4},{4,5},{5,6},{6,7},{7,8},{8,9},{9,10},{10,1... | collective-permute-start | bytes 98312 | tf_op jit(solution)/shard_map/ppermute | solution.py:483
  5.9 7.0 %collective-permute-start.1 = (bf16[128,128]{1,0:T(8,128)(2,1)S(1)}, bf16[128,128]{1,0:T(8,128)(2,1)S(1)}, u32[]{:S(2)}, u32[]{:S(2)}) collective-permute-start(bf16[128,128]{1,0:T(8,128)(2,1)S(1)} %get-tuple-element.15), channel_id=1, source_target_pairs={{0,63},{1,0},{2,1},{3,2},{4,3},{5,4},{6,5},{7,6},{8,7},{9,8},{10,9... | collective-permute-start | bytes 98312 | tf_op jit(solution)/shard_map/ppermute | solution.py:483
  12.9 0.0 collective-permute-done.low
  12.9 1.0 %collective-permute-done.1.high = bf16[128,128]{1,0:T(8,128)(2,1)S(1)} collective-permute-done((bf16[128,128]{1,0:T(8,128)(2,1)S(1)}, bf16[128,128]{1,0:T(8,128)(2,1)S(1)}, u32[]{:S(2)}, u32[]{:S(2)}) %collective-permute-start.1) | collective-permute-done | bytes 32800 | tf_op jit(solution)/shard_map/ppermute | solution.py:483
  13.9 4.8 %mid.1 = (bf16[16,4,24,128]{3,2,1,0:T(8,128)(2,1)}, f32[128,1024]{1,0:T(8,128)}, bf16[80,128]{1,0:T(8,128)(2,1)S(1)}, bf16[80,128]{1,0:T(8,128)(2,1)S(1)}) custom-call(bf16[128,128]{1,0:T(8,128)(2,1)S(1)} %collective-permute-done.low, bf16[128,128]{1,0:T(8,128)(2,1)S(1)} %collective-permute-done.1.high, f32[128,1024]{1,0:T(8,128)} %bitcast.22, ...), custom_call_target="tpu_custom_call" | custom-call | tf_op jit(solution)/shard_map/mid/pallas_call | solution.py:497
  18.8 16.3 %all-to-all-start = ((bf16[16,4,24,128]{3,2,1,0:T(8,128)(2,1)}), bf16[16,4,24,128]{3,2,1,0:T(8,128)(2,1)S(1)}, u32[]{:S(2)}, u32[]{:S(2)}) async-start(bf16[16,4,24,128]{3,2,1,0:T(8,128)(2,1)} %get-tuple-element.17.after), calls=%async_computation | async-start | bytes 786432 | tf_op jit(solution)/shard_map/all_to_all | solution.py:532
  35.1 0.7 %collective-permute-start.2 = (bf16[80,128]{1,0:T(8,128)(2,1)S(1)}, bf16[80,128]{1,0:T(8,128)(2,1)S(1)}, u32[]{:S(2)}, u32[]{:S(2)}) collective-permute-start(bf16[80,128]{1,0:T(8,128)(2,1)S(1)} %get-tuple-element.20), channel_id=1, source_target_pairs={{512,513},{513,514},{514,515},{515,516},{516,517},{517,518},{518,5... | collective-permute-start | bytes 61448 | tf_op jit(solution)/shard_map/ppermute | solution.py:483
  35.7 0.7 %collective-permute-start.3 = (bf16[80,128]{1,0:T(8,128)(2,1)S(1)}, bf16[80,128]{1,0:T(8,128)(2,1)S(1)}, u32[]{:S(2)}, u32[]{:S(2)}) collective-permute-start(bf16[80,128]{1,0:T(8,128)(2,1)S(1)} %get-tuple-element.21), channel_id=1, source_target_pairs={{512,575},{513,512},{514,513},{515,514},{516,515},{517,516},{518,5... | collective-permute-start | bytes 61448 | tf_op jit(solution)/shard_map/ppermute | solution.py:483
  36.4 2.0 %sea_own.1 = (f32[80,2048]{1,0:T(8,128)S(1)}, bf16[256,2048]{1,0:T(8,128)(2,1)S(1)}, f32[80,2048]{1,0:T(8,128)}) custom-call(bf16[16,4,24,128]{3,2,1,0:T(8,128)(2,1)} %get-tuple-element.17.after, f32[80,2048]{1,0:T(8,128)} %bitcast.19, s32[6,1,2048]{2,1,0:T(1,128)} %bitcast.39), custom_call_target="tpu_custom_call" | custom-call | flops 8000000000 | bytes 10000000 | tf_op jit(solution)/shard_map/sea_own/pallas_call | solution.py:536
  38.4 0.0 collective-permute-done.2.low
  38.4 0.0 collective-permute-done.3.high
  38.4 11.2 %all-to-all-done.arrived = bf16[16,4,24,128]{3,2,1,0:T(8,128)(2,1)S(1)} async-done(((bf16[16,4,24,128]{3,2,1,0:T(8,128)(2,1)}), bf16[16,4,24,128]{3,2,1,0:T(8,128)(2,1)S(1)}, u32[]{:S(2)}, u32[]{:S(2)}) %all-to-all-start) | async-done | bytes 393248 | tf_op jit(solution)/shard_map/all_to_all | solution.py:532
  49.6 2.6 %last.1 = (f32[80,2048]{1,0:T(8,128)}, f32[12,1,1024]{2,1,0:T(1,128)}) custom-call(bf16[16,4,24,128]{3,2,1,0:T(8,128)(2,1)S(1)} %all-to-all-done.arrived, s32[8,128]{1,0:T(8,128)} %bitcast.30, f32[1,1536]{1,0:T(1,128)} %bitcast.27, s32[1,12]{1,0:T(1,128)} %bitcast.35, s32[8,4,128]{2,1,0:T(4,128)} %bitcast.25, ...), custom_call_target="tpu_custom_call", output_to_operand_aliasing={{0}: (12, {})} | custom-call | tf_op jit(solution)/shard_map/last/pallas_call | solution.py:554
Async XLA Ops:
  2.0 11.0 %collective-permute-start = (bf16[128,128]{1,0:T(8,128)(2,1)S(1)}, bf16[128,128]{1,0:T(8,128)(2,1)S(1)}, u32[]{:S(2)}, u32[]{:S(2)}) collective-permute-start(bf16[128,128]{1,0:T(8,128)(2,1)S(1)} %get-tuple-element.14), channel_id=1, source_target_pairs={{0,1},{1,2},{2,3},{3,4},{4,5},{5,6},{6,7},{7,8},{8,9},{9,10},{10,1... | collective-permute-start | bytes 98312 | tf_op jit(solution)/shard_map/ppermute | solution.py:483
  5.9 8.0 %collective-permute-start.1 = (bf16[128,128]{1,0:T(8,128)(2,1)S(1)}, bf16[128,128]{1,0:T(8,128)(2,1)S(1)}, u32[]{:S(2)}, u32[]{:S(2)}) collective-permute-start(bf16[128,128]{1,0:T(8,128)(2,1)S(1)} %get-tuple-element.15), channel_id=1, source_target_pairs={{0,63},{1,0},{2,1},{3,2},{4,3},{5,4},{6,5},{7,6},{8,7},{9,8},{10,9... | collective-permute-start | bytes 98312 | tf_op jit(solution)/shard_map/ppermute | solution.py:483
  18.8 30.8 %all-to-all-start = ((bf16[16,4,24,128]{3,2,1,0:T(8,128)(2,1)}), bf16[16,4,24,128]{3,2,1,0:T(8,128)(2,1)S(1)}, u32[]{:S(2)}, u32[]{:S(2)}) async-start(bf16[16,4,24,128]{3,2,1,0:T(8,128)(2,1)} %get-tuple-element.17.after), calls=%async_computation | async-start | bytes 786432 | tf_op jit(solution)/shard_map/all_to_all | solution.py:532
  35.1 3.3 %collective-permute-start.2 = (bf16[80,128]{1,0:T(8,128)(2,1)S(1)}, bf16[80,128]{1,0:T(8,128)(2,1)S(1)}, u32[]{:S(2)}, u32[]{:S(2)}) collective-permute-start(bf16[80,128]{1,0:T(8,128)(2,1)S(1)} %get-tuple-element.20), channel_id=1, source_target_pairs={{512,513},{513,514},{514,515},{515,516},{516,517},{517,518},{518,5... | collective-permute-start | bytes 61448 | tf_op jit(solution)/shard_map/ppermute | solution.py:483
  35.7 2.7 %collective-permute-start.3 = (bf16[80,128]{1,0:T(8,128)(2,1)S(1)}, bf16[80,128]{1,0:T(8,128)(2,1)S(1)}, u32[]{:S(2)}, u32[]{:S(2)}) collective-permute-start(bf16[80,128]{1,0:T(8,128)(2,1)S(1)} %get-tuple-element.21), channel_id=1, source_target_pairs={{512,575},{513,512},{514,513},{515,514},{516,515},{517,516},{518,5... | collective-permute-start | bytes 61448 | tf_op jit(solution)/shard_map/ppermute | solution.py:483

commit v4 on v3

--- a/solution.py
+++ b/solution.py
@@ -59,17 +59,31 @@
     return marks
 
 
-def pack_into(state, send, down, up):
-    half = down.shape[1]
+def is_even():
+    return lax.rem(lax.axis_index("dev"), 2) == 0
+
+
+def pack_into(state, send, first, second):
+    half = first.shape[1]
     rows = row_marks(TILE, 2 * half)
     index = send[...]
     total = None
     for base in range(0, state.shape[1], TILE):
         part = dot(state[:, base : base + TILE].astype(BF16), marks_at([index], base, rows))
         total = part if total is None else total + part
-    out = total.astype(BF16)
-    down[...] = out[:, :half]
-    up[...] = out[:, half:]
+    down = total[:, :half]
+    up = total[:, half:]
+    even = is_even()
+    first[...] = jnp.where(even, down, up).astype(BF16)
+    second[...] = jnp.where(even, up, down).astype(BF16)
+
+
+def rims(first, second):
+    even = is_even()
+    one = first[...].astype(F32)
+    two = second[...].astype(F32)
+    both = jnp.concatenate([jnp.where(even, one, two), jnp.where(even, two, one)], axis=1)
+    return both.astype(BF16)
 
 
 def fetch(source, target, sem):
@@ -207,13 +221,35 @@
             looked[s, k] = look[:, k * block : (k + 1) * block]
 
 
+def air_own_kernel(
+    atm_groups, after, air_ref, air_nbrs_ref, air_mix_ref, part, marks, air, air_nbrs, air_mix, pool, sems
+):
+    @pl.when(lax.axis_index("grp") < atm_groups)
+    def _():
+        near, *rest = fetch_all(
+            [(air_nbrs_ref, air_nbrs), (air_ref, air), (air_mix_ref, air_mix)], sems
+        )
+        amount, columns = air_nbrs.shape
+        nbrs = [air_nbrs.at[k : k + 1, :] for k in range(amount)]
+        near.wait()
+        for at in range(0, columns, TILE):
+            marks[:, at : at + TILE] = rim_marks(nbrs, at, TILE, columns)
+        wait_all(rest)
+        pool[...] = air[...].astype(BF16)
+        for at in range(0, columns, TILE):
+            total = sums_of(pool, nbrs, at, TILE)
+            own = air[:, at : at + TILE]
+            mix = air_mix[:, at : at + TILE]
+            part[:, at : at + TILE] = own + mix * (total * (1.0 / amount) - own)
+
+
 def mid_kernel(
-    atm_groups,
-    low, high, air_ref, air_nbrs_ref, air_mix_ref, counts_ref, flux_weight_ref, weights_ref, owner,
+    atm_groups, amount,
+    first, second, part, marks, air_ref, air_mix_ref, counts_ref, flux_weight_ref, weights_ref, owner,
     sea_ref, sea_send_ref, ret_weight_ref, recv_ref,
     payload, air_out, sea_down_ref, sea_up_ref,
-    air, air_nbrs, air_mix, counts, flux_weight, weights,
-    pool, ends, begins_at, ends_at, values, sent, seen,
+    air, air_mix, counts, flux_weight, weights,
+    ends, begins_at, ends_at, values, sent, seen,
     sea, sea_send, ret_weight, recv, returned, down, up, sems, out_sems,
 ):
     here = lax.axis_index("grp") < atm_groups
@@ -221,11 +257,9 @@
 
     @pl.when(here)
     def _():
-        many, near, whole, mixed, *rest = fetch_all(
+        many, *rest = fetch_all(
             [
                 (counts_ref, counts),
-                (air_nbrs_ref, air_nbrs),
-                (air_ref, air),
                 (air_mix_ref, air_mix),
                 (flux_weight_ref, flux_weight),
                 (weights_ref, weights),
@@ -234,21 +268,16 @@
         )
         sent[...] = jnp.zeros(sent.shape, BF16)
         values[...] = jnp.zeros(values.shape, BF16)
+        rim = rims(first, second)
         many.wait()
         fill_ends(counts, ends)
         fill_limits(counts, ends, begins_at, ends_at)
-        amount, columns = air_nbrs.shape
-        half = low.shape[1]
-        pool[:, columns : columns + half] = low[...]
-        pool[:, columns + half :] = high[...]
-        wait_all([near, whole, mixed, *rest])
-        pool[:, :columns] = air[...].astype(BF16)
-        nbrs = [air_nbrs.at[k : k + 1, :] for k in range(amount)]
+        wait_all(rest)
+        columns = air.shape[1]
         fields = flux_weight.shape[0]
         for at in range(0, columns, TILE):
-            total = sums_of(pool, nbrs, at, TILE)
-            own = air[:, at : at + TILE]
-            new = own + air_mix[:, at : at + TILE] * (total * (1.0 / amount) - own)
+            total = dot(rim, marks[:, at : at + TILE])
+            new = part[:, at : at + TILE] + air_mix[:, at : at + TILE] * (total * (1.0 / amount))
             air[:, at : at + TILE] = new
             hi, lo = split(exact(flux_weight[...], new))
             values[0:fields, at : at + TILE] = hi
@@ -332,7 +361,7 @@
 def last_kernel(
     atm_groups, amount,
     arrived, counts_ref, weights_ref, owner,
-    recv_ref, sea_ref, sums_ref, marks_ref, low, high, sea_mix_ref, force_weight_ref, sea_in,
+    recv_ref, sea_ref, sums_ref, marks_ref, first, second, sea_mix_ref, force_weight_ref, sea_in,
     sea_out, mapped_ref,
     counts, ends, weights, mine, mapped, seen,
     recv, sea, sums, marks, sea_mix, force_weight, sems, out_sems,
@@ -395,7 +424,7 @@
             apart = jnp.concatenate(parts, axis=0).astype(BF16)
             flux = flux + dot_nt(apart, one_hot(row_marks(TILE, slots * block), rest_of))
         wait_all(rest)
-        rim = jnp.concatenate([low[...], high[...]], axis=1)
+        rim = rims(first, second)
         spread_weight = jnp.transpose(force_weight[...])
         for h in range(his):
             at = slice(h * TILE, (h + 1) * TILE)
@@ -474,15 +503,15 @@
     air_row = scratch(1, columns)
     params = pltpu.CompilerParams(vmem_limit_bytes=24 * 2**20)
 
-    def shifted(value, first, last, step):
-        line = [
-            (g * peers + i, g * peers + (i + step) % peers)
+    def swapped(value, first, last, odd):
+        pairs = [
+            (g * peers + i, g * peers + (((i - odd) ^ 1) + odd) % peers)
             for g in range(first, last)
             for i in range(peers)
         ]
-        return lax.ppermute(value, ("grp", "dev"), line)
-
-    down, up = pl.pallas_call(
+        return lax.ppermute(value, ("grp", "dev"), pairs)
+
+    to_first, to_second = pl.pallas_call(
         functools.partial(air_pack_kernel, atm_groups),
         out_shape=[air_rim] * 2,
         in_specs=[anywhere()] * 2,
@@ -491,22 +520,36 @@
         compiler_params=params,
         name="air_pack",
     )(air, in_hbm(atm_send.reshape(1, pair)))
-    low = shifted(up, 0, atm_groups, 1)
-    high = shifted(down, 0, atm_groups, -1)
-
-    payload, air_next, sea_down, sea_up = pl.pallas_call(
-        functools.partial(mid_kernel, atm_groups),
-        out_shape=[payload_shape, air_shape, sea_rim, sea_rim],
-        in_specs=[vmem()] * 2 + [anywhere()] * 6 + [smem()] + [anywhere()] * 4,
-        out_specs=[anywhere()] * 4,
+    first = swapped(to_first, 0, atm_groups, 1)
+    second = swapped(to_second, 0, atm_groups, 0)
+
+    part, marks = pl.pallas_call(
+        functools.partial(air_own_kernel, atm_groups),
+        out_shape=[air_shape, shape((pair, columns), BF16)],
+        in_specs=[anywhere()] * 4,
+        out_specs=[vmem()] * 2,
         scratch_shapes=[
             air_scratch,
             scratch(amount_air, columns, dtype=I32),
             air_row,
+            scratch(levels_air, columns, dtype=BF16),
+            dma((3,)),
+        ],
+        compiler_params=params,
+        cost_estimate=pl.CostEstimate(flops=4 * 10**9, bytes_accessed=10**7, transcendentals=0),
+        name="air_own",
+    )(to_second, air, in_hbm(atm_nbrs.reshape(amount_air, columns)), air_mix)
+    payload, air_next, sea_to_first, sea_to_second = pl.pallas_call(
+        functools.partial(mid_kernel, atm_groups, amount_air),
+        out_shape=[payload_shape, air_shape, sea_rim, sea_rim],
+        in_specs=[vmem()] * 4 + [anywhere()] * 5 + [smem()] + [anywhere()] * 4,
+        out_specs=[anywhere()] * 4,
+        scratch_shapes=[
+            air_scratch,
+            air_row,
             counts_in,
             scratch(fields, levels_air),
             weights_in,
-            scratch(levels_air, columns + pair, dtype=BF16),
             counts_in,
             scratch(columns, 128, dtype=I16),
             scratch(columns, 128, dtype=I16),
@@ -520,18 +563,18 @@
             scratch(16 * (cells // TILE), TILE, dtype=BF16),
             sea_half,
             sea_half,
-            dma((6,)),
+            dma((5,)),
             dma((4,)),
         ],
         compiler_params=params,
         name="mid",
     )(
-        low, high, air, in_hbm(atm_nbrs.reshape(amount_air, columns)), air_mix, counts, in_hbm(flux_weight),
+        first, second, part, marks, air, air_mix, counts, in_hbm(flux_weight),
         weights, owner, sea, in_hbm(ocn_send.reshape(1, pair)), in_hbm(ret_weight), recv,
     )
     arrived = lax.all_to_all(payload, "grp", split_axis=0, concat_axis=0, tiled=True)
-    sea_low = shifted(sea_up, atm_groups, groups, 1)
-    sea_high = shifted(sea_down, atm_groups, groups, -1)
+    sea_first = swapped(sea_to_first, atm_groups, groups, 1)
+    sea_second = swapped(sea_to_second, atm_groups, groups, 0)
 
     sums, sea_marks, sea_pre = pl.pallas_call(
         functools.partial(sea_own_kernel, atm_groups),
@@ -577,7 +620,7 @@
         name="last",
     )(
         arrived, counts, weights, owner,
-        recv, sea, sums, sea_marks, sea_low, sea_high, in_hbm(ocn_mix.reshape(1, cells)), in_hbm(force_weight.T),
+        recv, sea, sums, sea_marks, sea_first, sea_second, in_hbm(ocn_mix.reshape(1, cells)), in_hbm(force_weight.T),
         sea_pre,
     )
     mapped = mapped.reshape(1, 1, ret_fields, columns)

time: 52.6 us -> 49.8 us (0.947)
  starting transfers between devices: 28.6 us -> 25.2 us
  Pallas kernels: 10.7 us -> 11.7 us
    all_to_all x1, starting transfers between devices: 16.3 us -> 12.9 us  [on_device(): lax.all_to_all(payload, 'grp', split_axis=0, concat_axis=0, tiled=True)]
    pallas_call x1 -> x2, Pallas kernels: 4.82 us -> 5.77 us  [the longest x1 3.58 us: on_device(): pl.pallas_call(functools.partial(mid_kernel, atm_groups, amount_air), out...]
  transfers between devices with their start and end apart: 5 -> 5, of which waited for: 2 -> 2; matrix products, arithmetic and copies ran while one was open for 0% -> 0% of each run, Pallas kernels for 4% -> 8%
where the time goes in v4:
time: 49.8 us; the launch traced here: 49.3 us
  starting transfers between devices  25.2 us (51%)
  waiting for transfers between devices  11.8 us (24%)
  Pallas kernels  11.7 us (23%)
  between operations  0.72 us (1%)
    all_to_all x1, starting transfers between devices, on_device(): lax.all_to_all(payload, 'grp', split_axis=0, concat_axis=0, tiled=True)  12.9 us
    ppermute x4, starting transfers between devices, swapped(): return lax.ppermute(value, ('grp', 'dev'), pairs)  12.3 us
    all_to_all x1, waiting for transfers between devices, on_device(): lax.all_to_all(payload, 'grp', split_axis=0, concat_axis=0, tiled=True)  11.2 us
    pallas_call x1, Pallas kernels, on_device(): pl.pallas_call(functools.partial(mid_kernel, atm_groups, amount_air), out...  3.58 us
    pallas_call x1, Pallas kernels, on_device(): pl.pallas_call(functools.partial(last_kernel, atm_groups, amount_sea), ou...  2.6 us
    pallas_call x1, Pallas kernels, on_device(): pl.pallas_call(functools.partial(air_own_kernel, atm_groups), out_shape=[...  2.19 us
    pallas_call x1, Pallas kernels, on_device(): pl.pallas_call(functools.partial(sea_own_kernel, atm_groups), out_shape=[...  1.97 us
    pallas_call x1, Pallas kernels, on_device(): pl.pallas_call(functools.partial(air_pack_kernel, atm_groups), out_shape=...  1.33 us
  transfers between devices with their start and end apart: 5, of which 2 were waited for; matrix products, arithmetic and copies ran while one was open for 0% of the time, Pallas kernels for 8%

profile of v4, /device:TPU:1, one launch (start us, length us, event | category | flops | bytes accessed | tf_op | source)
XLA Modules:
  0.0 49.3 jit_solution(15371495855681368837)
XLA Ops:
  0.6 1.3 %air_pack.1 = (bf16[128,128]{1,0:T(8,128)(2,1)S(1)}, bf16[128,128]{1,0:T(8,128)(2,1)S(1)}) custom-call(f32[128,1024]{1,0:T(8,128)} %bitcast.21, s32[1,256]{1,0:T(1,128)} %bitcast.37), custom_call_target="tpu_custom_call" | custom-call | tf_op jit(solution)/shard_map/air_pack/pallas_call | solution.py:514
  2.0 9.0 %collective-permute-start = (bf16[128,128]{1,0:T(8,128)(2,1)S(1)}, bf16[128,128]{1,0:T(8,128)(2,1)S(1)}, u32[]{:S(2)}, u32[]{:S(2)}) collective-permute-start(bf16[128,128]{1,0:T(8,128)(2,1)S(1)} %get-tuple-element.16), channel_id=1, source_target_pairs={{0,63},{1,2},{2,1},{3,4},{4,3},{5,6},{6,5},{7,8},{8,7},{9,10},{10,... | collective-permute-start | bytes 98312 | tf_op jit(solution)/shard_map/ppermute | solution.py:512
  11.0 1.9 %collective-permute-start.1 = (bf16[128,128]{1,0:T(8,128)(2,1)S(1)}, bf16[128,128]{1,0:T(8,128)(2,1)S(1)}, u32[]{:S(2)}, u32[]{:S(2)}) collective-permute-start(bf16[128,128]{1,0:T(8,128)(2,1)S(1)} %get-tuple-element.17.after), channel_id=1, source_target_pairs={{0,1},{1,0},{2,3},{3,2},{4,5},{5,4},{6,7},{7,6},{8,9},{9,8},{10,11... | collective-permute-start | bytes 98312 | tf_op jit(solution)/shard_map/ppermute | solution.py:512
  12.9 2.2 %air_own.1 = (f32[128,1024]{1,0:T(8,128)S(1)}, bf16[256,1024]{1,0:T(8,128)(2,1)S(1)}) custom-call(bf16[128,128]{1,0:T(8,128)(2,1)S(1)} %get-tuple-element.17.after, f32[128,1024]{1,0:T(8,128)} %bitcast.22, s32[4,1024]{1,0:T(4,128)} %bitcast.42, f32[1,1024]{1,0:T(1,128)} %bitcast.33), custom_call_target="tpu_custom_call" | custom-call | flops 4000000000 | bytes 10000000 | tf_op jit(solution)/shard_map/air_own/pallas_call | solution.py:526
  15.1 0.0 collective-permute-done.first
  15.1 0.5 %collective-permute-done.1.second = bf16[128,128]{1,0:T(8,128)(2,1)S(1)} collective-permute-done((bf16[128,128]{1,0:T(8,128)(2,1)S(1)}, bf16[128,128]{1,0:T(8,128)(2,1)S(1)}, u32[]{:S(2)}, u32[]{:S(2)}) %collective-permute-start.1) | collective-permute-done | bytes 32800 | tf_op jit(solution)/shard_map/ppermute | solution.py:512
  15.7 3.6 %mid.1 = (bf16[16,4,24,128]{3,2,1,0:T(8,128)(2,1)}, f32[128,1024]{1,0:T(8,128)}, bf16[80,128]{1,0:T(8,128)(2,1)S(1)}, bf16[80,128]{1,0:T(8,128)(2,1)S(1)}) custom-call(bf16[128,128]{1,0:T(8,128)(2,1)S(1)} %collective-permute-done.first, bf16[128,128]{1,0:T(8,128)(2,1)S(1)} %collective-permute-done.1.second, f32[128,1024]{1,0:T(8,128)S(1)} %get-tuple-element.18.part, ...), custom_call_target="tpu_custom_call" | custom-call | tf_op jit(solution)/shard_map/mid/pallas_call | solution.py:542
  19.3 12.9 %all-to-all-start = ((bf16[16,4,24,128]{3,2,1,0:T(8,128)(2,1)}), bf16[16,4,24,128]{3,2,1,0:T(8,128)(2,1)S(1)}, u32[]{:S(2)}, u32[]{:S(2)}) async-start(bf16[16,4,24,128]{3,2,1,0:T(8,128)(2,1)} %get-tuple-element.21.after), calls=%async_computation | async-start | bytes 786432 | tf_op jit(solution)/shard_map/all_to_all | solution.py:575
  32.2 0.7 %collective-permute-start.2 = (bf16[80,128]{1,0:T(8,128)(2,1)S(1)}, bf16[80,128]{1,0:T(8,128)(2,1)S(1)}, u32[]{:S(2)}, u32[]{:S(2)}) collective-permute-start(bf16[80,128]{1,0:T(8,128)(2,1)S(1)} %get-tuple-element.24), channel_id=1, source_target_pairs={{512,575},{513,514},{514,513},{515,516},{516,515},{517,518},{518,5... | collective-permute-start | bytes 61448 | tf_op jit(solution)/shard_map/ppermute | solution.py:512
  32.9 0.7 %collective-permute-start.3 = (bf16[80,128]{1,0:T(8,128)(2,1)S(1)}, bf16[80,128]{1,0:T(8,128)(2,1)S(1)}, u32[]{:S(2)}, u32[]{:S(2)}) collective-permute-start(bf16[80,128]{1,0:T(8,128)(2,1)S(1)} %get-tuple-element.25), channel_id=1, source_target_pairs={{512,513},{513,512},{514,515},{515,514},{516,517},{517,516},{518,5... | collective-permute-start | bytes 61448 | tf_op jit(solution)/shard_map/ppermute | solution.py:512
  33.5 2.0 %sea_own.1 = (f32[80,2048]{1,0:T(8,128)S(1)}, bf16[256,2048]{1,0:T(8,128)(2,1)S(1)}, f32[80,2048]{1,0:T(8,128)}) custom-call(bf16[16,4,24,128]{3,2,1,0:T(8,128)(2,1)} %get-tuple-element.21.after, f32[80,2048]{1,0:T(8,128)} %bitcast.19, s32[6,1,2048]{2,1,0:T(1,128)} %bitcast.40), custom_call_target="tpu_custom_call" | custom-call | flops 8000000000 | bytes 10000000 | tf_op jit(solution)/shard_map/sea_own/pallas_call | solution.py:579
  35.5 0.0 collective-permute-done.2.first
  35.5 0.0 collective-permute-done.3.second
  35.5 11.2 %all-to-all-done.arrived = bf16[16,4,24,128]{3,2,1,0:T(8,128)(2,1)S(1)} async-done(((bf16[16,4,24,128]{3,2,1,0:T(8,128)(2,1)}), bf16[16,4,24,128]{3,2,1,0:T(8,128)(2,1)S(1)}, u32[]{:S(2)}, u32[]{:S(2)}) %all-to-all-start) | async-done | bytes 393248 | tf_op jit(solution)/shard_map/all_to_all | solution.py:575
  46.7 2.6 %last.1 = (f32[80,2048]{1,0:T(8,128)}, f32[12,1,1024]{2,1,0:T(1,128)}) custom-call(bf16[16,4,24,128]{3,2,1,0:T(8,128)(2,1)S(1)} %all-to-all-done.arrived, s32[8,128]{1,0:T(8,128)} %bitcast.30, f32[1,1536]{1,0:T(1,128)} %bitcast.28, s32[1,12]{1,0:T(1,128)} %bitcast.36, s32[8,4,128]{2,1,0:T(4,128)} %bitcast.26, ...), custom_call_target="tpu_custom_call", output_to_operand_aliasing={{0}: (12, {})} | custom-call | tf_op jit(solution)/shard_map/last/pallas_call | solution.py:597
Async XLA Ops:
  2.0 13.2 %collective-permute-start = (bf16[128,128]{1,0:T(8,128)(2,1)S(1)}, bf16[128,128]{1,0:T(8,128)(2,1)S(1)}, u32[]{:S(2)}, u32[]{:S(2)}) collective-permute-start(bf16[128,128]{1,0:T(8,128)(2,1)S(1)} %get-tuple-element.16), channel_id=1, source_target_pairs={{0,63},{1,2},{2,1},{3,4},{4,3},{5,6},{6,5},{7,8},{8,7},{9,10},{10,... | collective-permute-start | bytes 98312 | tf_op jit(solution)/shard_map/ppermute | solution.py:512
  11.0 4.7 %collective-permute-start.1 = (bf16[128,128]{1,0:T(8,128)(2,1)S(1)}, bf16[128,128]{1,0:T(8,128)(2,1)S(1)}, u32[]{:S(2)}, u32[]{:S(2)}) collective-permute-start(bf16[128,128]{1,0:T(8,128)(2,1)S(1)} %get-tuple-element.17.after), channel_id=1, source_target_pairs={{0,1},{1,0},{2,3},{3,2},{4,5},{5,4},{6,7},{7,6},{8,9},{9,8},{10,11... | collective-permute-start | bytes 98312 | tf_op jit(solution)/shard_map/ppermute | solution.py:512
  19.3 27.5 %all-to-all-start = ((bf16[16,4,24,128]{3,2,1,0:T(8,128)(2,1)}), bf16[16,4,24,128]{3,2,1,0:T(8,128)(2,1)S(1)}, u32[]{:S(2)}, u32[]{:S(2)}) async-start(bf16[16,4,24,128]{3,2,1,0:T(8,128)(2,1)} %get-tuple-element.21.after), calls=%async_computation | async-start | bytes 786432 | tf_op jit(solution)/shard_map/all_to_all | solution.py:575
  32.2 3.3 %collective-permute-start.2 = (bf16[80,128]{1,0:T(8,128)(2,1)S(1)}, bf16[80,128]{1,0:T(8,128)(2,1)S(1)}, u32[]{:S(2)}, u32[]{:S(2)}) collective-permute-start(bf16[80,128]{1,0:T(8,128)(2,1)S(1)} %get-tuple-element.24), channel_id=1, source_target_pairs={{512,575},{513,514},{514,513},{515,516},{516,515},{517,518},{518,5... | collective-permute-start | bytes 61448 | tf_op jit(solution)/shard_map/ppermute | solution.py:512
  32.9 2.7 %collective-permute-start.3 = (bf16[80,128]{1,0:T(8,128)(2,1)S(1)}, bf16[80,128]{1,0:T(8,128)(2,1)S(1)}, u32[]{:S(2)}, u32[]{:S(2)}) collective-permute-start(bf16[80,128]{1,0:T(8,128)(2,1)S(1)} %get-tuple-element.25), channel_id=1, source_target_pairs={{512,513},{513,512},{514,515},{515,514},{516,517},{517,516},{518,5... | collective-permute-start | bytes 61448 | tf_op jit(solution)/shard_map/ppermute | solution.py:512

commit v5 on v4

--- a/solution.py
+++ b/solution.py
@@ -151,39 +151,45 @@
         begins_at[at, :] = jnp.broadcast_to(begin[:, j : j + 1], (lanes, lanes)).astype(I16)
 
 
-def spread_rows(values, begins_at, ends_at, tile):
+def spans(columns):
+    reach = (columns // 2) // TILE
+    amount = columns // TILE
+    return [
+        (p, list(range(max(0, p - reach), min(p, amount - 1) + 1))) for p in range(amount + reach)
+    ]
+
+
+def fill_spread(begins_at, ends_at, tiles):
     columns, lanes = ends_at.shape
-    reach = (columns // 2) // TILE
     lane = lax.broadcasted_iota(I32, (TILE, lanes), 1)
-    total = None
-    for t in range(max(0, tile - reach), min(tile, columns // TILE - 1) + 1):
-        at = slice(t * TILE, (t + 1) * TILE)
-        sides = []
-        for side in range(TILE // lanes):
-            order = (lane + (tile * TILE + side * lanes)).astype(I16)
-            sides.append(interval(order, begins_at[at, :], ends_at[at, :]))
-        part = dot(values[:, at], jnp.concatenate(sides, axis=1))
-        total = part if total is None else total + part
-    return total
-
-
-def gather_rows(values, counts, ends, tile):
+    i = 0
+    for p, near in spans(columns):
+        for t in near:
+            at = slice(t * TILE, (t + 1) * TILE)
+            for side in range(0, TILE, lanes):
+                order = (lane + (p * TILE + side)).astype(I16)
+                tiles[i * TILE : (i + 1) * TILE, side : side + lanes] = interval(
+                    order, begins_at[at, :], ends_at[at, :]
+                )
+            i += 1
+
+
+def fill_gather(counts, ends, tiles):
     blocks, lanes = counts.shape
-    reach = (blocks * lanes // 2) // TILE
     each = TILE // lanes
-    end = jnp.concatenate([ends[tile * each + i : tile * each + i + 1, :] for i in range(each)], axis=1)
-    count = jnp.concatenate(
-        [counts[tile * each + i : tile * each + i + 1, :] for i in range(each)], axis=1
-    )
-    begin = (end - count).astype(I16)
-    end = end.astype(I16)
+    limits = []
+    for t in range(blocks // each):
+        lines = range(t * each, (t + 1) * each)
+        end = jnp.concatenate([ends[i : i + 1, :] for i in lines], axis=1)
+        count = jnp.concatenate([counts[i : i + 1, :] for i in lines], axis=1)
+        limits.append(((end - count).astype(I16), end.astype(I16)))
     rows = row_iota(TILE, TILE)
-    total = None
-    for t in range(tile, tile + reach + 1):
-        mark = interval((rows + t * TILE).astype(I16), begin, end)
-        part = dot(values[:, t * TILE : (t + 1) * TILE], mark)
-        total = part if total is None else total + part
-    return total
+    i = 0
+    for p, near in spans(blocks * lanes):
+        order = (rows + p * TILE).astype(I16)
+        for t in near:
+            tiles[i * TILE : (i + 1) * TILE, :] = interval(order, *limits[t])
+            i += 1
 
 
 def slots_of(owner, seen, visit):
@@ -222,34 +228,49 @@
 
 
 def air_own_kernel(
-    atm_groups, after, air_ref, air_nbrs_ref, air_mix_ref, part, marks, air, air_nbrs, air_mix, pool, sems
+    atm_groups,
+    after, air_ref, air_nbrs_ref, air_mix_ref, counts_ref, flux_weight_ref, weights_ref,
+    part, marks, tiles, air_mix, flux_weight, weights,
+    air, air_nbrs, counts, ends, begins_at, ends_at, pool, sems,
 ):
     @pl.when(lax.axis_index("grp") < atm_groups)
     def _():
-        near, *rest = fetch_all(
-            [(air_nbrs_ref, air_nbrs), (air_ref, air), (air_mix_ref, air_mix)], sems
+        many, near, whole, mixed, *rest = fetch_all(
+            [
+                (counts_ref, counts),
+                (air_nbrs_ref, air_nbrs),
+                (air_ref, air),
+                (air_mix_ref, air_mix),
+                (flux_weight_ref, flux_weight),
+                (weights_ref, weights),
+            ],
+            sems,
         )
         amount, columns = air_nbrs.shape
         nbrs = [air_nbrs.at[k : k + 1, :] for k in range(amount)]
+        many.wait()
+        fill_ends(counts, ends)
+        fill_limits(counts, ends, begins_at, ends_at)
+        fill_spread(begins_at, ends_at, tiles)
         near.wait()
         for at in range(0, columns, TILE):
             marks[:, at : at + TILE] = rim_marks(nbrs, at, TILE, columns)
-        wait_all(rest)
+        wait_all([whole, mixed])
         pool[...] = air[...].astype(BF16)
         for at in range(0, columns, TILE):
             total = sums_of(pool, nbrs, at, TILE)
             own = air[:, at : at + TILE]
             mix = air_mix[:, at : at + TILE]
             part[:, at : at + TILE] = own + mix * (total * (1.0 / amount) - own)
+        wait_all(rest)
 
 
 def mid_kernel(
     atm_groups, amount,
-    first, second, part, marks, air_ref, air_mix_ref, counts_ref, flux_weight_ref, weights_ref, owner,
+    first, second, part, marks, tiles, air_mix, flux_weight, weights, air_ref, owner_ref,
     sea_ref, sea_send_ref, ret_weight_ref, recv_ref,
     payload, air_out, sea_down_ref, sea_up_ref,
-    air, air_mix, counts, flux_weight, weights,
-    ends, begins_at, ends_at, values, sent, seen,
+    air, values, sent, owner, seen,
     sea, sea_send, ret_weight, recv, returned, down, up, sems, out_sems,
 ):
     here = lax.axis_index("grp") < atm_groups
@@ -257,22 +278,10 @@
 
     @pl.when(here)
     def _():
-        many, *rest = fetch_all(
-            [
-                (counts_ref, counts),
-                (air_mix_ref, air_mix),
-                (flux_weight_ref, flux_weight),
-                (weights_ref, weights),
-            ],
-            sems,
-        )
+        owned = fetch(owner_ref, owner, sems.at[0])
         sent[...] = jnp.zeros(sent.shape, BF16)
         values[...] = jnp.zeros(values.shape, BF16)
         rim = rims(first, second)
-        many.wait()
-        fill_ends(counts, ends)
-        fill_limits(counts, ends, begins_at, ends_at)
-        wait_all(rest)
         columns = air.shape[1]
         fields = flux_weight.shape[0]
         for at in range(0, columns, TILE):
@@ -285,16 +294,23 @@
         stored = fetch(air, air_out, out_sems.at[0])
         block = sent.shape[3]
         each = TILE // block
-        tiles = []
-        for t in range(weights.shape[1] // TILE):
-            both = spread_rows(values, begins_at, ends_at, t)
-            tile = (both[0:fields] + both[32 : 32 + fields]) * weights[:, t * TILE : (t + 1) * TILE]
-            tiles.append(tile.astype(BF16))
+        made = []
+        i = 0
+        for p, near in spans(columns):
+            both = None
+            for t in near:
+                one = values[:, t * TILE : (t + 1) * TILE]
+                more = dot(one, tiles[i * TILE : (i + 1) * TILE, :])
+                both = more if both is None else both + more
+                i += 1
+            tile = (both[0:fields] + both[32 : 32 + fields]) * weights[:, p * TILE : (p + 1) * TILE]
+            made.append(tile.astype(BF16))
 
         def visit(b, o, k):
             i = b % each
-            sent[o, k] = tiles[b // each][:, i * block : (i + 1) * block]
-
+            sent[o, k] = made[b // each][:, i * block : (i + 1) * block]
+
+        owned.wait()
         slots_of(owner, seen, visit)
         done = fetch(sent, payload.at[pl.ds(atm_groups, count_groups)], out_sems.at[1])
         wait_all([stored, done])
@@ -325,16 +341,23 @@
 
 def sea_own_kernel(
     atm_groups,
-    after, sea_ref, sea_nbrs_ref,
-    sums_ref, marks_ref, sea_out,
-    sea, sea_nbrs, sums, marks, pool, sems, out_sems,
+    after, sea_ref, sea_nbrs_ref, counts_ref, weights_ref,
+    sums_ref, marks_ref, sea_out, tiles, weights,
+    sea, sea_nbrs, sums, marks, pool, counts, ends, sems, out_sems,
 ):
     here = lax.axis_index("grp") < atm_groups
 
     @pl.when(here)
     def _():
-        fetch(sea_ref, sea, sems.at[0]).wait()
-        fetch(sea, sea_out, out_sems.at[0]).wait()
+        whole, many, given = fetch_all(
+            [(sea_ref, sea), (counts_ref, counts), (weights_ref, weights)], sems
+        )
+        whole.wait()
+        keep = fetch(sea, sea_out, out_sems.at[0])
+        many.wait()
+        fill_ends(counts, ends)
+        fill_gather(counts, ends, tiles)
+        wait_all([given, keep])
 
     @pl.when(jnp.logical_not(here))
     def _():
@@ -360,10 +383,10 @@
 
 def last_kernel(
     atm_groups, amount,
-    arrived, counts_ref, weights_ref, owner,
+    arrived, tiles, weights, owner_ref,
     recv_ref, sea_ref, sums_ref, marks_ref, first, second, sea_mix_ref, force_weight_ref, sea_in,
     sea_out, mapped_ref,
-    counts, ends, weights, mine, mapped, seen,
+    mine, mapped, owner, seen,
     recv, sea, sums, marks, sea_mix, force_weight, sems, out_sems,
 ):
     here = lax.axis_index("grp") < atm_groups
@@ -371,24 +394,28 @@
 
     @pl.when(here)
     def _():
-        many, given = fetch_all([(counts_ref, counts), (weights_ref, weights)], sems)
+        owned = fetch(owner_ref, owner, sems.at[0])
         block = arrived.shape[3]
 
         def visit(b, o, k):
             mine[:, b * block : (b + 1) * block] = arrived[atm_groups + o, k].astype(F32)
 
+        owned.wait()
         slots_of(owner, seen, visit)
-        many.wait()
-        fill_ends(counts, ends)
-        given.wait()
         w = weights[...]
         scaled = mine[0:16, :] * w
         order = row_iota(16, scaled.shape[1])
         scaled = jnp.where(order < fields, scaled, jnp.where(order == fields, w, 0.0))
         hi, lo = split(scaled)
         both_in = jnp.concatenate([hi, lo], axis=0)
-        for t in range(columns // TILE):
-            both = gather_rows(both_in, counts, ends, t)
+        sums_in = [None] * (columns // TILE)
+        i = 0
+        for p, near in spans(columns):
+            for t in near:
+                more = dot(both_in[:, p * TILE : (p + 1) * TILE], tiles[i * TILE : (i + 1) * TILE, :])
+                sums_in[t] = more if sums_in[t] is None else sums_in[t] + more
+                i += 1
+        for t, both in enumerate(sums_in):
             both = both[0:16] + both[16:32]
             mean = both[0:fields] / both[fields : fields + 1]
             for f in range(fields):
@@ -440,10 +467,6 @@
     return pl.BlockSpec(memory_space=pltpu.VMEM)
 
 
-def smem():
-    return pl.BlockSpec(memory_space=pltpu.SMEM)
-
-
 def anywhere():
     return pl.BlockSpec(memory_space=pl.ANY)
 
@@ -488,6 +511,9 @@
     payload_shape = shape((groups, capacity, fields, block), BF16)
     sent_shape = (capacity, fields, block)
     dma = pltpu.SemaphoreType.DMA
+    tile_count = sum(len(near) for _, near in spans(columns))
+    tiles_shape = shape((tile_count * TILE, TILE), BF16)
+    owner_in = pltpu.SMEM((1, blocks_here), I32)
 
     def scratch(*dims, dtype=F32):
         return pltpu.VMEM(dims, dtype)
@@ -499,8 +525,6 @@
     sea_half = scratch(levels_sea, half, dtype=BF16)
     pair_in = scratch(1, pair, dtype=I32)
     recv_in = scratch(atm_groups, capacity, block, dtype=I32)
-    weights_in = scratch(1, row_count)
-    air_row = scratch(1, columns)
     params = pltpu.CompilerParams(vmem_limit_bytes=24 * 2**20)
 
     def swapped(value, first, last, odd):
@@ -523,38 +547,45 @@
     first = swapped(to_first, 0, atm_groups, 1)
     second = swapped(to_second, 0, atm_groups, 0)
 
-    part, marks = pl.pallas_call(
+    part, marks, tiles, mix, flux_in, weights_here = pl.pallas_call(
         functools.partial(air_own_kernel, atm_groups),
-        out_shape=[air_shape, shape((pair, columns), BF16)],
-        in_specs=[anywhere()] * 4,
-        out_specs=[vmem()] * 2,
+        out_shape=[
+            air_shape,
+            shape((pair, columns), BF16),
+            tiles_shape,
+            shape((1, columns), F32),
+            shape((fields, levels_air), F32),
+            shape((1, row_count), F32),
+        ],
+        in_specs=[anywhere()] * 7,
+        out_specs=[vmem()] * 6,
         scratch_shapes=[
             air_scratch,
             scratch(amount_air, columns, dtype=I32),
-            air_row,
+            counts_in,
+            counts_in,
+            scratch(columns, 128, dtype=I16),
+            scratch(columns, 128, dtype=I16),
             scratch(levels_air, columns, dtype=BF16),
-            dma((3,)),
+            dma((6,)),
         ],
         compiler_params=params,
         cost_estimate=pl.CostEstimate(flops=4 * 10**9, bytes_accessed=10**7, transcendentals=0),
         name="air_own",
-    )(to_second, air, in_hbm(atm_nbrs.reshape(amount_air, columns)), air_mix)
+    )(
+        to_second, air, in_hbm(atm_nbrs.reshape(amount_air, columns)), air_mix, counts,
+        in_hbm(flux_weight), weights,
+    )
     payload, air_next, sea_to_first, sea_to_second = pl.pallas_call(
         functools.partial(mid_kernel, atm_groups, amount_air),
         out_shape=[payload_shape, air_shape, sea_rim, sea_rim],
-        in_specs=[vmem()] * 4 + [anywhere()] * 5 + [smem()] + [anywhere()] * 4,
+        in_specs=[vmem()] * 8 + [anywhere()] * 6,
         out_specs=[anywhere()] * 4,
         scratch_shapes=[
             air_scratch,
-            air_row,
-            counts_in,
-            scratch(fields, levels_air),
-            weights_in,
-            counts_in,
-            scratch(columns, 128, dtype=I16),
-            scratch(columns, 128, dtype=I16),
             scratch(64, columns, dtype=BF16),
             scratch(atm_groups, *sent_shape, dtype=BF16),
+            owner_in,
             pltpu.SMEM((groups - atm_groups,), I32),
             sea_scratch,
             pair_in,
@@ -569,42 +600,47 @@
         compiler_params=params,
         name="mid",
     )(
-        first, second, part, marks, air, air_mix, counts, in_hbm(flux_weight),
-        weights, owner, sea, in_hbm(ocn_send.reshape(1, pair)), in_hbm(ret_weight), recv,
+        first, second, part, marks, tiles, mix, flux_in, weights_here, air, owner, sea, in_hbm(ocn_send.reshape(1, pair)), in_hbm(ret_weight), recv,
     )
     arrived = lax.all_to_all(payload, "grp", split_axis=0, concat_axis=0, tiled=True)
     sea_first = swapped(sea_to_first, atm_groups, groups, 1)
     sea_second = swapped(sea_to_second, atm_groups, groups, 0)
 
-    sums, sea_marks, sea_pre = pl.pallas_call(
+    sums, sea_marks, sea_pre, back_tiles, weights_back = pl.pallas_call(
         functools.partial(sea_own_kernel, atm_groups),
-        out_shape=[sea_shape, shape((pair, cells), BF16), sea_shape],
-        in_specs=[anywhere()] * 3,
-        out_specs=[anywhere()] * 3,
+        out_shape=[
+            sea_shape,
+            shape((pair, cells), BF16),
+            sea_shape,
+            tiles_shape,
+            shape((1, row_count), F32),
+        ],
+        in_specs=[anywhere()] * 5,
+        out_specs=[pl.BlockSpec(memory_space=pltpu.HBM)] + [anywhere()] * 2 + [vmem()] * 2,
         scratch_shapes=[
             sea_scratch,
             scratch(amount_sea, 1, cells, dtype=I32),
             sea_scratch,
             sea_marks_in,
             scratch(levels_sea, cells, dtype=BF16),
-            dma((2,)),
+            counts_in,
+            counts_in,
+            dma((3,)),
             dma((2,)),
         ],
         compiler_params=params,
         cost_estimate=pl.CostEstimate(flops=8 * 10**9, bytes_accessed=10**7, transcendentals=0),
         name="sea_own",
-    )(payload, sea, in_hbm(ocn_nbrs.reshape(amount_sea, 1, cells)))
+    )(payload, sea, in_hbm(ocn_nbrs.reshape(amount_sea, 1, cells)), counts, weights)
     sea_next, mapped = pl.pallas_call(
         functools.partial(last_kernel, atm_groups, amount_sea),
         out_shape=[sea_shape, shape((ret_fields, 1, columns), F32)],
-        in_specs=[vmem()] + [anywhere()] * 2 + [smem()] + [anywhere()] * 4 + [vmem()] * 2 + [anywhere()] * 3,
+        in_specs=[vmem()] * 3 + [anywhere()] * 5 + [vmem()] * 2 + [anywhere()] * 3,
         out_specs=[anywhere()] * 2,
         scratch_shapes=[
-            counts_in,
-            counts_in,
-            weights_in,
             scratch(fields, row_count),
             scratch(ret_fields, 1, columns),
+            owner_in,
             pltpu.SMEM((groups - atm_groups,), I32),
             recv_in,
             sea_scratch,
@@ -619,8 +655,8 @@
         compiler_params=params,
         name="last",
     )(
-        arrived, counts, weights, owner,
-        recv, sea, sums, sea_marks, sea_first, sea_second, in_hbm(ocn_mix.reshape(1, cells)), in_hbm(force_weight.T),
+        arrived, back_tiles, weights_back, owner,
+        recv, sea, in_hbm(sums), sea_marks, sea_first, sea_second, in_hbm(ocn_mix.reshape(1, cells)), in_hbm(force_weight.T),
         sea_pre,
     )
     mapped = mapped.reshape(1, 1, ret_fields, columns)

time: 49.8 us -> 46.8 us (0.940)
  Pallas kernels: 11.7 us -> 9.54 us
  waiting for transfers between devices: 11.8 us -> 10.4 us
  local copies, waits for them, and re-layouts: 0 us -> 0.84 us
    pallas_call x1, Pallas kernels: 3.58 us -> 1.6 us  [on_device(): pl.pallas_call(functools.partial(mid_kernel, atm_groups, amount_air), out...]
    pallas_call x1, Pallas kernels: 2.6 us -> 1.72 us  [on_device(): pl.pallas_call(functools.partial(last_kernel, atm_groups, amount_sea), ou...]
    all_to_all x1, waiting for transfers between devices: 11.2 us -> 10.4 us  [on_device(): lax.all_to_all(payload, 'grp', split_axis=0, concat_axis=0, tiled=True)]
    unnamed x0 -> x2, local copies, waits for them, and re-layouts: none -> 0.84 us
    pallas_call x1, Pallas kernels: 2.19 us -> 2.91 us  [on_device(): pl.pallas_call(functools.partial(air_own_kernel, atm_groups), out_shape=[...]
    ppermute x4, waiting for transfers between devices: 0.53 us -> 0.01 us  [swapped(): return lax.ppermute(value, ('grp', 'dev'), pairs)]
  transfers between devices with their start and end apart: 5 -> 5, of which waited for: 2 -> 1; matrix products, arithmetic and copies ran while one was open for 0% -> 0% of each run, Pallas kernels for 8% -> 11%
where the time goes in v5:
time: 46.8 us; the launch traced here: 46.5 us
  starting transfers between devices  25 us (53%)
  waiting for transfers between devices  10.4 us (22%)
  Pallas kernels  9.54 us (20%)
  local copies, waits for them, and re-layouts  0.84 us (2%)
  between operations  0.72 us (2%)
    all_to_all x1, starting transfers between devices, on_device(): lax.all_to_all(payload, 'grp', split_axis=0, concat_axis=0, tiled=True)  12.7 us
    ppermute x4, starting transfers between devices, swapped(): return lax.ppermute(value, ('grp', 'dev'), pairs)  12.3 us
    all_to_all x1, waiting for transfers between devices, on_device(): lax.all_to_all(payload, 'grp', split_axis=0, concat_axis=0, tiled=True)  10.4 us
    pallas_call x1, Pallas kernels, on_device(): pl.pallas_call(functools.partial(air_own_kernel, atm_groups), out_shape=[...  2.91 us
    pallas_call x1, Pallas kernels, on_device(): pl.pallas_call(functools.partial(sea_own_kernel, atm_groups), out_shape=[...  1.98 us
    pallas_call x1, Pallas kernels, on_device(): pl.pallas_call(functools.partial(last_kernel, atm_groups, amount_sea), ou...  1.72 us
    pallas_call x1, Pallas kernels, on_device(): pl.pallas_call(functools.partial(mid_kernel, atm_groups, amount_air), out...  1.6 us
    pallas_call x1, Pallas kernels, on_device(): pl.pallas_call(functools.partial(air_pack_kernel, atm_groups), out_shape=...  1.33 us
  transfers between devices with their start and end apart: 5, of which 1 were waited for; matrix products, arithmetic and copies ran while one was open for 0% of the time, Pallas kernels for 11%

profile of v5, /device:TPU:1, one launch (start us, length us, event | category | flops | bytes accessed | tf_op | source)
XLA Modules:
  0.0 46.5 jit_solution(4081699505582874159)
XLA Ops:
  0.6 1.3 %air_pack.1 = (bf16[128,128]{1,0:T(8,128)(2,1)S(1)}, bf16[128,128]{1,0:T(8,128)(2,1)S(1)}) custom-call(f32[128,1024]{1,0:T(8,128)} %bitcast.21, s32[1,256]{1,0:T(1,128)} %bitcast.31), custom_call_target="tpu_custom_call" | custom-call | tf_op jit(solution)/shard_map/air_pack/pallas_call | solution.py:538
  2.0 9.0 %collective-permute-start = (bf16[128,128]{1,0:T(8,128)(2,1)S(1)}, bf16[128,128]{1,0:T(8,128)(2,1)S(1)}, u32[]{:S(2)}, u32[]{:S(2)}) collective-permute-start(bf16[128,128]{1,0:T(8,128)(2,1)S(1)} %get-tuple-element.22), channel_id=1, source_target_pairs={{0,63},{1,2},{2,1},{3,4},{4,3},{5,6},{6,5},{7,8},{8,7},{9,10},{10,... | collective-permute-start | bytes 98312 | tf_op jit(solution)/shard_map/ppermute | solution.py:536
  11.0 1.9 %collective-permute-start.1 = (bf16[128,128]{1,0:T(8,128)(2,1)S(1)}, bf16[128,128]{1,0:T(8,128)(2,1)S(1)}, u32[]{:S(2)}, u32[]{:S(2)}) collective-permute-start(bf16[128,128]{1,0:T(8,128)(2,1)S(1)} %get-tuple-element.23.after), channel_id=1, source_target_pairs={{0,1},{1,0},{2,3},{3,2},{4,5},{5,4},{6,7},{7,6},{8,9},{9,8},{10,11... | collective-permute-start | bytes 98312 | tf_op jit(solution)/shard_map/ppermute | solution.py:536
  12.9 2.9 %air_own.1 = (f32[128,1024]{1,0:T(8,128)S(1)}, bf16[256,1024]{1,0:T(8,128)(2,1)S(1)}, bf16[3072,256]{1,0:T(8,128)(2,1)S(1)}, f32[1,1024]{1,0:T(1,128)S(1)}, f32[...) custom-call(bf16[128,128]{1,0:T(8,128)(2,1)S(1)} %get-tuple-element.23.after, f32[128,1024]{1,0:T(8,128)} %bitcast.22, ...), custom_call_target="tpu_custom_call" | custom-call | flops 4000000000 | bytes 10000000 | tf_op jit(solution)/shard_map/air_own/pallas_call | solution.py:550
  15.9 0.0 collective-permute-done.first
  15.9 0.0 collective-permute-done.1.second
  15.9 1.6 %mid.1 = (bf16[16,4,24,128]{3,2,1,0:T(8,128)(2,1)}, f32[128,1024]{1,0:T(8,128)}, bf16[80,128]{1,0:T(8,128)(2,1)S(1)}, bf16[80,128]{1,0:T(8,128)(2,1)S(1)}) custom-call(bf16[128,128]{1,0:T(8,128)(2,1)S(1)} %collective-permute-done.first, bf16[128,128]{1,0:T(8,128)(2,1)S(1)} %collective-permute-done.1.second, f32[128,1024]{1,0:T(8,128)S(1)} %get-tuple-element.24.part, ...), custom_call_target="tpu_custom_call" | custom-call | tf_op jit(solution)/shard_map/mid/pallas_call | solution.py:579
  17.5 12.7 %all-to-all-start = ((bf16[16,4,24,128]{3,2,1,0:T(8,128)(2,1)}), bf16[16,4,24,128]{3,2,1,0:T(8,128)(2,1)S(1)}, u32[]{:S(2)}, u32[]{:S(2)}) async-start(bf16[16,4,24,128]{3,2,1,0:T(8,128)(2,1)} %get-tuple-element.31.after), calls=%async_computation | async-start | bytes 786432 | tf_op jit(solution)/shard_map/all_to_all | solution.py:605
  30.2 0.7 %collective-permute-start.2 = (bf16[80,128]{1,0:T(8,128)(2,1)S(1)}, bf16[80,128]{1,0:T(8,128)(2,1)S(1)}, u32[]{:S(2)}, u32[]{:S(2)}) collective-permute-start(bf16[80,128]{1,0:T(8,128)(2,1)S(1)} %get-tuple-element.36), channel_id=1, source_target_pairs={{512,575},{513,514},{514,513},{515,516},{516,515},{517,518},{518,5... | collective-permute-start | bytes 61448 | tf_op jit(solution)/shard_map/ppermute | solution.py:536
  30.9 0.7 %collective-permute-start.3 = (bf16[80,128]{1,0:T(8,128)(2,1)S(1)}, bf16[80,128]{1,0:T(8,128)(2,1)S(1)}, u32[]{:S(2)}, u32[]{:S(2)}) collective-permute-start(bf16[80,128]{1,0:T(8,128)(2,1)S(1)} %get-tuple-element.37), channel_id=1, source_target_pairs={{512,513},{513,512},{514,515},{515,514},{516,517},{517,516},{518,5... | collective-permute-start | bytes 61448 | tf_op jit(solution)/shard_map/ppermute | solution.py:536
  31.5 2.0 %sea_own.1 = (f32[80,2048]{1,0:T(8,128)S(1)}, bf16[256,2048]{1,0:T(8,128)(2,1)S(1)}, f32[80,2048]{1,0:T(8,128)}, bf16[3072,256]{1,0:T(8,128)(2,1)S(1)}, f32[1,1536]{1,0:T(1,128)S(1)}) custom-call(bf16[16,4,24,128]{3,2,1,0:T(8,128)(2,1)} %get-tuple-element.31.after, f32[80,2048]{1,0:T(8,128)} %bitcast.19, s32[6,1,2048]{2,1,0:T(1,128)} %bitcast.34, ...), custom_call_target="tpu_custom_call" | custom-call | flops 8000000000 | bytes 10000000 | tf_op jit(solution)/shard_map/sea_own/pallas_call | solution.py:609
  33.5 0.0 copy-start
  33.5 0.8 %copy-done = f32[80,2048]{1,0:T(8,128)} copy-done((f32[80,2048]{1,0:T(8,128)}, f32[80,2048]{1,0:T(8,128)S(1)}, u32[]{:S(2)}) %copy-start) | copy-done | bytes 655384
  34.4 0.0 collective-permute-done.2.first
  34.4 0.0 collective-permute-done.3.second
  34.4 10.4 %all-to-all-done.arrived = bf16[16,4,24,128]{3,2,1,0:T(8,128)(2,1)S(1)} async-done(((bf16[16,4,24,128]{3,2,1,0:T(8,128)(2,1)}), bf16[16,4,24,128]{3,2,1,0:T(8,128)(2,1)S(1)}, u32[]{:S(2)}, u32[]{:S(2)}) %all-to-all-start) | async-done | bytes 393248 | tf_op jit(solution)/shard_map/all_to_all | solution.py:605
  44.7 1.7 %last.1 = (f32[80,2048]{1,0:T(8,128)}, f32[12,1,1024]{2,1,0:T(1,128)}) custom-call(bf16[16,4,24,128]{3,2,1,0:T(8,128)(2,1)S(1)} %all-to-all-done.arrived, bf16[3072,256]{1,0:T(8,128)(2,1)S(1)} %get-tuple-element.32.tiles, f32[1,1536]{1,0:T(1,128)S(1)} %get-tuple-element.33.weights, s32[1,12]{1,0:T(1,128)} %bitcast.30, ...), custom_call_target="tpu_custom_call", output_to_operand_aliasing={{0}: (12, {})} | custom-call | tf_op jit(solution)/shard_map/last/pallas_call | solution.py:635
Async XLA Ops:
  2.0 13.9 %collective-permute-start = (bf16[128,128]{1,0:T(8,128)(2,1)S(1)}, bf16[128,128]{1,0:T(8,128)(2,1)S(1)}, u32[]{:S(2)}, u32[]{:S(2)}) collective-permute-start(bf16[128,128]{1,0:T(8,128)(2,1)S(1)} %get-tuple-element.22), channel_id=1, source_target_pairs={{0,63},{1,2},{2,1},{3,4},{4,3},{5,6},{6,5},{7,8},{8,7},{9,10},{10,... | collective-permute-start | bytes 98312 | tf_op jit(solution)/shard_map/ppermute | solution.py:536
  11.0 4.9 %collective-permute-start.1 = (bf16[128,128]{1,0:T(8,128)(2,1)S(1)}, bf16[128,128]{1,0:T(8,128)(2,1)S(1)}, u32[]{:S(2)}, u32[]{:S(2)}) collective-permute-start(bf16[128,128]{1,0:T(8,128)(2,1)S(1)} %get-tuple-element.23.after), channel_id=1, source_target_pairs={{0,1},{1,0},{2,3},{3,2},{4,5},{5,4},{6,7},{7,6},{8,9},{9,8},{10,11... | collective-permute-start | bytes 98312 | tf_op jit(solution)/shard_map/ppermute | solution.py:536
  17.5 27.3 %all-to-all-start = ((bf16[16,4,24,128]{3,2,1,0:T(8,128)(2,1)}), bf16[16,4,24,128]{3,2,1,0:T(8,128)(2,1)S(1)}, u32[]{:S(2)}, u32[]{:S(2)}) async-start(bf16[16,4,24,128]{3,2,1,0:T(8,128)(2,1)} %get-tuple-element.31.after), calls=%async_computation | async-start | bytes 786432 | tf_op jit(solution)/shard_map/all_to_all | solution.py:605
  30.2 4.2 %collective-permute-start.2 = (bf16[80,128]{1,0:T(8,128)(2,1)S(1)}, bf16[80,128]{1,0:T(8,128)(2,1)S(1)}, u32[]{:S(2)}, u32[]{:S(2)}) collective-permute-start(bf16[80,128]{1,0:T(8,128)(2,1)S(1)} %get-tuple-element.36), channel_id=1, source_target_pairs={{512,575},{513,514},{514,513},{515,516},{516,515},{517,518},{518,5... | collective-permute-start | bytes 61448 | tf_op jit(solution)/shard_map/ppermute | solution.py:536
  30.9 3.5 %collective-permute-start.3 = (bf16[80,128]{1,0:T(8,128)(2,1)S(1)}, bf16[80,128]{1,0:T(8,128)(2,1)S(1)}, u32[]{:S(2)}, u32[]{:S(2)}) collective-permute-start(bf16[80,128]{1,0:T(8,128)(2,1)S(1)} %get-tuple-element.37), channel_id=1, source_target_pairs={{512,513},{513,512},{514,515},{515,514},{516,517},{517,516},{518,5... | collective-permute-start | bytes 61448 | tf_op jit(solution)/shard_map/ppermute | solution.py:536
  33.5 0.8 %copy-start = (f32[80,2048]{1,0:T(8,128)}, f32[80,2048]{1,0:T(8,128)S(1)}, u32[]{:S(2)}) copy-start(f32[80,2048]{1,0:T(8,128)S(1)} %get-tuple-element.34.sums_ref) | copy-start | bytes 1966084

commit v6 on v5

--- a/solution.py
+++ b/solution.py
@@ -230,8 +230,8 @@
 def air_own_kernel(
     atm_groups,
     after, air_ref, air_nbrs_ref, air_mix_ref, counts_ref, flux_weight_ref, weights_ref,
-    part, marks, tiles, air_mix, flux_weight, weights,
-    air, air_nbrs, counts, ends, begins_at, ends_at, pool, sems,
+    part_ref, marks_ref, rows_own, rim_rows, air_mix, flux_weight, weights,
+    part, marks, air, air_nbrs, counts, ends, begins_at, ends_at, tiles, pool, values, scaled, sems, out_sems,
 ):
     @pl.when(lax.axis_index("grp") < atm_groups)
     def _():
@@ -262,12 +262,38 @@
             own = air[:, at : at + TILE]
             mix = air_mix[:, at : at + TILE]
             part[:, at : at + TILE] = own + mix * (total * (1.0 / amount) - own)
+            scaled[:, at : at + TILE] = (
+                marks[:, at : at + TILE].astype(F32) * (mix * (1.0 / amount))
+            ).astype(BF16)
+        kept = fetch_all([(part, part_ref), (marks, marks_ref)], out_sems)
         wait_all(rest)
+        fields = flux_weight.shape[0]
+        values[...] = jnp.zeros(values.shape, BF16)
+        for at in range(0, columns, TILE):
+            hi, lo = split(exact(flux_weight[...], part[:, at : at + TILE]))
+            values[0:fields, at : at + TILE] = hi
+            values[32 : 32 + fields, at : at + TILE] = lo
+        i = 0
+        for p, near_by in spans(columns):
+            both = None
+            rim = None
+            for t in near_by:
+                at = slice(t * TILE, (t + 1) * TILE)
+                mark = tiles[i * TILE : (i + 1) * TILE, :]
+                more = dot(values[:, at], mark)
+                more_rim = dot(scaled[:, at], mark)
+                both = more if both is None else both + more
+                rim = more_rim if rim is None else rim + more_rim
+                i += 1
+            at = slice(p * TILE, (p + 1) * TILE)
+            rows_own[:, at] = both[0:fields] + both[32 : 32 + fields]
+            rim_rows[:, at] = rim.astype(BF16)
+        wait_all(kept)
 
 
 def mid_kernel(
-    atm_groups, amount,
-    first, second, part, marks, tiles, air_mix, flux_weight, weights, air_ref, owner_ref,
+    atm_groups,
+    first, second, rows_own, rim_rows, flux_weight, weights, air_ref, owner_ref,
     sea_ref, sea_send_ref, ret_weight_ref, recv_ref,
     payload, air_out, sea_down_ref, sea_up_ref,
     air, values, sent, owner, seen,
@@ -282,28 +308,18 @@
         sent[...] = jnp.zeros(sent.shape, BF16)
         values[...] = jnp.zeros(values.shape, BF16)
         rim = rims(first, second)
-        columns = air.shape[1]
         fields = flux_weight.shape[0]
-        for at in range(0, columns, TILE):
-            total = dot(rim, marks[:, at : at + TILE])
-            new = part[:, at : at + TILE] + air_mix[:, at : at + TILE] * (total * (1.0 / amount))
-            air[:, at : at + TILE] = new
-            hi, lo = split(exact(flux_weight[...], new))
-            values[0:fields, at : at + TILE] = hi
-            values[32 : 32 + fields, at : at + TILE] = lo
-        stored = fetch(air, air_out, out_sems.at[0])
+        high, rest = split(flux_weight[...])
+        hi, lo = split(dot(high, rim) + dot(rest, rim))
+        values[0:fields, :] = hi
+        values[32 : 32 + fields, :] = lo
         block = sent.shape[3]
         each = TILE // block
         made = []
-        i = 0
-        for p, near in spans(columns):
-            both = None
-            for t in near:
-                one = values[:, t * TILE : (t + 1) * TILE]
-                more = dot(one, tiles[i * TILE : (i + 1) * TILE, :])
-                both = more if both is None else both + more
-                i += 1
-            tile = (both[0:fields] + both[32 : 32 + fields]) * weights[:, p * TILE : (p + 1) * TILE]
+        for p in range(weights.shape[1] // TILE):
+            at = slice(p * TILE, (p + 1) * TILE)
+            both = dot(values[...], rim_rows[:, at])
+            tile = (rows_own[:, at] + (both[0:fields] + both[32 : 32 + fields])) * weights[:, at]
             made.append(tile.astype(BF16))
 
         def visit(b, o, k):
@@ -313,7 +329,7 @@
         owned.wait()
         slots_of(owner, seen, visit)
         done = fetch(sent, payload.at[pl.ds(atm_groups, count_groups)], out_sems.at[1])
-        wait_all([stored, done])
+        done.wait()
 
     @pl.when(jnp.logical_not(here))
     def _():
@@ -340,24 +356,39 @@
 
 
 def sea_own_kernel(
-    atm_groups,
-    after, sea_ref, sea_nbrs_ref, counts_ref, weights_ref,
-    sums_ref, marks_ref, sea_out, tiles, weights,
-    sea, sea_nbrs, sums, marks, pool, counts, ends, sems, out_sems,
+    atm_groups, amount_air,
+    after, sea_ref, sea_nbrs_ref, counts_ref, weights_ref, first, second, part_ref, air_marks_ref, air_mix, air_in, sea_first_in, sea_second_in,
+    sums_ref, marks_ref, sea_out, tiles, weights, air_out, sea_first, sea_second,
+    sea, sea_nbrs, sums, marks, pool, counts, ends, air, part, air_marks, sems, out_sems,
 ):
     here = lax.axis_index("grp") < atm_groups
 
     @pl.when(here)
     def _():
-        whole, many, given = fetch_all(
-            [(sea_ref, sea), (counts_ref, counts), (weights_ref, weights)], sems
+        near, parted, whole, many, given = fetch_all(
+            [
+                (air_marks_ref, air_marks),
+                (part_ref, part),
+                (sea_ref, sea),
+                (counts_ref, counts),
+                (weights_ref, weights),
+            ],
+            sems,
         )
+        wait_all([near, parted])
+        rim = rims(first, second)
+        for at in range(0, air.shape[1], TILE):
+            total = dot(rim, air_marks[:, at : at + TILE])
+            air[:, at : at + TILE] = part[:, at : at + TILE] + air_mix[:, at : at + TILE] * (
+                total * (1.0 / amount_air)
+            )
+        stored = fetch(air, air_out, out_sems.at[1])
         whole.wait()
         keep = fetch(sea, sea_out, out_sems.at[0])
         many.wait()
         fill_ends(counts, ends)
         fill_gather(counts, ends, tiles)
-        wait_all([given, keep])
+        wait_all([given, keep, stored])
 
     @pl.when(jnp.logical_not(here))
     def _():
@@ -526,6 +557,7 @@
     pair_in = scratch(1, pair, dtype=I32)
     recv_in = scratch(atm_groups, capacity, block, dtype=I32)
     params = pltpu.CompilerParams(vmem_limit_bytes=24 * 2**20)
+    wide = pltpu.CompilerParams(vmem_limit_bytes=24 * 2**20)
 
     def swapped(value, first, last, odd):
         pairs = [
@@ -547,43 +579,50 @@
     first = swapped(to_first, 0, atm_groups, 1)
     second = swapped(to_second, 0, atm_groups, 0)
 
-    part, marks, tiles, mix, flux_in, weights_here = pl.pallas_call(
+    part, marks, rows_own, rim_rows, mix, flux_in, weights_here = pl.pallas_call(
         functools.partial(air_own_kernel, atm_groups),
         out_shape=[
             air_shape,
             shape((pair, columns), BF16),
-            tiles_shape,
+            shape((fields, row_count), F32),
+            shape((pair, row_count), BF16),
             shape((1, columns), F32),
             shape((fields, levels_air), F32),
             shape((1, row_count), F32),
         ],
         in_specs=[anywhere()] * 7,
-        out_specs=[vmem()] * 6,
+        out_specs=[anywhere()] * 2 + [vmem()] * 5,
         scratch_shapes=[
+            air_scratch,
+            scratch(pair, columns, dtype=BF16),
             air_scratch,
             scratch(amount_air, columns, dtype=I32),
             counts_in,
             counts_in,
             scratch(columns, 128, dtype=I16),
             scratch(columns, 128, dtype=I16),
+            scratch(tile_count * TILE, TILE, dtype=BF16),
             scratch(levels_air, columns, dtype=BF16),
+            scratch(64, columns, dtype=BF16),
+            scratch(pair, columns, dtype=BF16),
             dma((6,)),
+            dma((2,)),
         ],
-        compiler_params=params,
+        compiler_params=wide,
         cost_estimate=pl.CostEstimate(flops=4 * 10**9, bytes_accessed=10**7, transcendentals=0),
         name="air_own",
     )(
-        to_second, air, in_hbm(atm_nbrs.reshape(amount_air, columns)), air_mix, counts,
+        to_first, air, in_hbm(atm_nbrs.reshape(amount_air, columns)), air_mix, counts,
         in_hbm(flux_weight), weights,
     )
-    payload, air_next, sea_to_first, sea_to_second = pl.pallas_call(
-        functools.partial(mid_kernel, atm_groups, amount_air),
+    payload, air_pre, sea_to_first, sea_to_second = pl.pallas_call(
+        functools.partial(mid_kernel, atm_groups),
         out_shape=[payload_shape, air_shape, sea_rim, sea_rim],
-        in_specs=[vmem()] * 8 + [anywhere()] * 6,
+        in_specs=[vmem()] * 6 + [anywhere()] * 6,
         out_specs=[anywhere()] * 4,
         scratch_shapes=[
             air_scratch,
-            scratch(64, columns, dtype=BF16),
+            scratch(64, pair, dtype=BF16),
             scratch(atm_groups, *sent_shape, dtype=BF16),
             owner_in,
             pltpu.SMEM((groups - atm_groups,), I32),
@@ -600,23 +639,28 @@
         compiler_params=params,
         name="mid",
     )(
-        first, second, part, marks, tiles, mix, flux_in, weights_here, air, owner, sea, in_hbm(ocn_send.reshape(1, pair)), in_hbm(ret_weight), recv,
+        first, second, rows_own, rim_rows, flux_in, weights_here, air, owner, sea, in_hbm(ocn_send.reshape(1, pair)), in_hbm(ret_weight), recv,
     )
     arrived = lax.all_to_all(payload, "grp", split_axis=0, concat_axis=0, tiled=True)
-    sea_first = swapped(sea_to_first, atm_groups, groups, 1)
-    sea_second = swapped(sea_to_second, atm_groups, groups, 0)
-
-    sums, sea_marks, sea_pre, back_tiles, weights_back = pl.pallas_call(
-        functools.partial(sea_own_kernel, atm_groups),
+
+    sums, sea_marks, sea_pre, back_tiles, weights_back, air_next, *sea_sent = pl.pallas_call(
+        functools.partial(sea_own_kernel, atm_groups, amount_air),
         out_shape=[
             sea_shape,
             shape((pair, cells), BF16),
             sea_shape,
             tiles_shape,
             shape((1, row_count), F32),
+            air_shape,
+            sea_rim,
+            sea_rim,
         ],
-        in_specs=[anywhere()] * 5,
-        out_specs=[pl.BlockSpec(memory_space=pltpu.HBM)] + [anywhere()] * 2 + [vmem()] * 2,
+        in_specs=[anywhere()] * 5 + [vmem()] * 2 + [anywhere()] * 2 + [vmem()] + [anywhere()] * 3,
+        out_specs=[pl.BlockSpec(memory_space=pltpu.HBM)]
+        + [anywhere()] * 2
+        + [vmem()] * 2
+        + [anywhere()] * 3,
+        input_output_aliases={10: 5, 11: 6, 12: 7},
         scratch_shapes=[
             sea_scratch,
             scratch(amount_sea, 1, cells, dtype=I32),
@@ -625,13 +669,22 @@
             scratch(levels_sea, cells, dtype=BF16),
             counts_in,
             counts_in,
-            dma((3,)),
+            air_scratch,
+            air_scratch,
+            scratch(pair, columns, dtype=BF16),
+            dma((5,)),
             dma((2,)),
         ],
         compiler_params=params,
         cost_estimate=pl.CostEstimate(flops=8 * 10**9, bytes_accessed=10**7, transcendentals=0),
         name="sea_own",
-    )(payload, sea, in_hbm(ocn_nbrs.reshape(amount_sea, 1, cells)), counts, weights)
+    )(
+        payload, sea, in_hbm(ocn_nbrs.reshape(amount_sea, 1, cells)), counts, weights,
+        first, second, in_hbm(part), in_hbm(marks), mix, air_pre,
+        sea_to_first, sea_to_second,
+    )
+    sea_first = swapped(sea_sent[0], atm_groups, groups, 1)
+    sea_second = swapped(sea_sent[1], atm_groups, groups, 0)
     sea_next, mapped = pl.pallas_call(
         functools.partial(last_kernel, atm_groups, amount_sea),
         out_shape=[sea_shape, shape((ret_fields, 1, columns), F32)],

time: 46.8 us -> 47.8 us (1.021)
  the two profiles are of different devices: /device:TPU:1 before, /device:TPU:512 now
where the time goes in v6:
time: 47.8 us; the launch traced here: 47.4 us
  starting transfers between devices  26.1 us (55%)
  Pallas kernels  15.3 us (32%)
  waiting for transfers between devices  3.76 us (8%)
  local copies, waits for them, and re-layouts  1.63 us (3%)
  between operations  0.72 us (2%)
    all_to_all x1, starting transfers between devices, on_device(): lax.all_to_all(payload, 'grp', split_axis=0, concat_axis=0, tiled=True)  16.1 us
    ppermute x4, starting transfers between devices, swapped(): return lax.ppermute(value, ('grp', 'dev'), pairs)  9.94 us
    pallas_call x1, Pallas kernels, on_device(): pl.pallas_call(functools.partial(sea_own_kernel, atm_groups, amount_air),...  8.19 us
    pallas_call x1, Pallas kernels, on_device(): pl.pallas_call(functools.partial(last_kernel, atm_groups, amount_sea), ou...  3.77 us
    ppermute x4, waiting for transfers between devices, swapped(): return lax.ppermute(value, ('grp', 'dev'), pairs)  3.75 us
    pallas_call x1, Pallas kernels, on_device(): pl.pallas_call(functools.partial(mid_kernel, atm_groups), out_shape=[payl...  3.18 us
    unnamed x6, local copies, waits for them, and re-layouts  1.63 us
  transfers between devices with their start and end apart: 5, of which 2 were waited for; matrix products, arithmetic and copies ran while one was open for 0% of the time, Pallas kernels for 17%

profile of v6, /device:TPU:512, one launch (start us, length us, event | category | flops | bytes accessed | tf_op | source)
XLA Modules:
  0.0 47.4 jit_solution(12044207719773101979)
XLA Ops:
  0.7 0.7 %collective-permute-start = (bf16[128,128]{1,0:T(8,128)(2,1)S(1)}, bf16[128,128]{1,0:T(8,128)(2,1)S(1)}, u32[]{:S(2)}, u32[]{:S(2)}) collective-permute-start(bf16[128,128]{1,0:T(8,128)(2,1)S(1)} %get-tuple-element.26.after), channel_id=1, source_target_pairs={{0,63},{1,2},{2,1},{3,4},{4,3},{5,6},{6,5},{7,8},{8,7},{9,10},{10,... | collective-permute-start | bytes 98312 | tf_op jit(solution)/shard_map/ppermute | solution.py:568
  1.3 0.7 %collective-permute-start.1 = (bf16[128,128]{1,0:T(8,128)(2,1)S(1)}, bf16[128,128]{1,0:T(8,128)(2,1)S(1)}, u32[]{:S(2)}, u32[]{:S(2)}) collective-permute-start(bf16[128,128]{1,0:T(8,128)(2,1)S(1)} %get-tuple-element.27), channel_id=1, source_target_pairs={{0,1},{1,0},{2,3},{3,2},{4,5},{5,4},{6,7},{7,6},{8,9},{9,8},{10,11... | collective-permute-start | bytes 98312 | tf_op jit(solution)/shard_map/ppermute | solution.py:568
  2.0 0.1 air_own.1
  2.1 0.0 copy-start.2
  2.1 0.8 %copy-done.2 = bf16[256,1024]{1,0:T(8,128)(2,1)} copy-done((bf16[256,1024]{1,0:T(8,128)(2,1)}, bf16[256,1024]{1,0:T(8,128)(2,1)S(1)}, u32[]{:S(2)}) %copy-start.2) | copy-done | bytes 524312
  2.9 0.0 copy-start.1
  2.9 0.0 collective-permute-done.first
  2.9 0.0 collective-permute-done.1.second
  2.9 3.2 %mid.1 = (bf16[16,4,24,128]{3,2,1,0:T(8,128)(2,1)}, f32[128,1024]{1,0:T(8,128)}, bf16[80,128]{1,0:T(8,128)(2,1)S(1)}, bf16[80,128]{1,0:T(8,128)(2,1)S(1)}) custom-call(bf16[128,128]{1,0:T(8,128)(2,1)S(1)} %collective-permute-done.first, bf16[128,128]{1,0:T(8,128)(2,1)S(1)} %collective-permute-done.1.second, f32[24,1536]{1,0:T(8,128)S(1)} %get-tuple-element.28.rows_own, ...), custom_call_target="tpu_custom_call" | custom-call | tf_op jit(solution)/shard_map/mid/pallas_call | solution.py:618
  6.1 0.0 copy-done.1
  6.1 16.1 %all-to-all-start = ((bf16[16,4,24,128]{3,2,1,0:T(8,128)(2,1)}), bf16[16,4,24,128]{3,2,1,0:T(8,128)(2,1)S(1)}, u32[]{:S(2)}, u32[]{:S(2)}) async-start(bf16[16,4,24,128]{3,2,1,0:T(8,128)(2,1)} %get-tuple-element.32.after), calls=%async_computation | async-start | bytes 786432 | tf_op jit(solution)/shard_map/all_to_all | solution.py:644
  22.2 8.2 %sea_own.1 = (f32[80,2048]{1,0:T(8,128)S(1)}, bf16[256,2048]{1,0:T(8,128)(2,1)S(1)}, f32[80,2048]{1,0:T(8,128)}, bf16[3072,256]{1,0:T(8,128)(2,1)S(1)}, f32[1,15...) custom-call(bf16[16,4,24,128]{3,2,1,0:T(8,128)(2,1)} %get-tuple-elem, ...), custom_call_target="tpu_custom_call", output_to_operand_aliasing={{5}: (10, {}), {6}: (11, {}), {7}: (12, {})} | custom-call | flops 8000000000 | bytes 10000000 | tf_op jit(solution)/shard_map/sea_own/pallas_call | solution.py:646
  30.4 0.0 copy-start
  30.4 0.8 %copy-done = f32[80,2048]{1,0:T(8,128)} copy-done((f32[80,2048]{1,0:T(8,128)}, f32[80,2048]{1,0:T(8,128)S(1)}, u32[]{:S(2)}) %copy-start) | copy-done | bytes 655384
  31.3 6.7 %collective-permute-start.2 = (bf16[80,128]{1,0:T(8,128)(2,1)S(1)}, bf16[80,128]{1,0:T(8,128)(2,1)S(1)}, u32[]{:S(2)}, u32[]{:S(2)}) collective-permute-start(bf16[80,128]{1,0:T(8,128)(2,1)S(1)} %get-tuple-element.44), channel_id=1, source_target_pairs={{512,575},{513,514},{514,513},{515,516},{516,515},{517,518},{518,5... | collective-permute-start | bytes 61448 | tf_op jit(solution)/shard_map/ppermute | solution.py:568
  38.0 1.9 %collective-permute-start.3 = (bf16[80,128]{1,0:T(8,128)(2,1)S(1)}, bf16[80,128]{1,0:T(8,128)(2,1)S(1)}, u32[]{:S(2)}, u32[]{:S(2)}) collective-permute-start(bf16[80,128]{1,0:T(8,128)(2,1)S(1)} %get-tuple-element.45), channel_id=1, source_target_pairs={{512,513},{513,512},{514,515},{515,514},{516,517},{517,516},{518,5... | collective-permute-start | bytes 61448 | tf_op jit(solution)/shard_map/ppermute | solution.py:568
  39.9 0.4 collective-permute-done.2.first
  40.3 3.4 %collective-permute-done.3.second = bf16[80,128]{1,0:T(8,128)(2,1)S(1)} collective-permute-done((bf16[80,128]{1,0:T(8,128)(2,1)S(1)}, bf16[80,128]{1,0:T(8,128)(2,1)S(1)}, u32[]{:S(2)}, u32[]{:S(2)}) %collective-permute-start.3) | collective-permute-done | bytes 20512 | tf_op jit(solution)/shard_map/ppermute | solution.py:568
  43.7 0.0 all-to-all-done.arrived
  43.7 3.8 %last.1 = (f32[80,2048]{1,0:T(8,128)}, f32[12,1,1024]{2,1,0:T(1,128)}) custom-call(bf16[16,4,24,128]{3,2,1,0:T(8,128)(2,1)S(1)} %all-to-all-done.arrived, bf16[3072,256]{1,0:T(8,128)(2,1)S(1)} %get-tuple-element.40.tiles, f32[1,1536]{1,0:T(1,128)S(1)} %get-tuple-element.41.weights, s32[1,12]{1,0:T(1,128)} %bitcast.30, ...), custom_call_target="tpu_custom_call", output_to_operand_aliasing={{0}: (12, {})} | custom-call | tf_op jit(solution)/shard_map/last/pallas_call | solution.py:688
  (1 shorter events, 0.0 us)
Async XLA Ops:
  0.7 2.2 %collective-permute-start = (bf16[128,128]{1,0:T(8,128)(2,1)S(1)}, bf16[128,128]{1,0:T(8,128)(2,1)S(1)}, u32[]{:S(2)}, u32[]{:S(2)}) collective-permute-start(bf16[128,128]{1,0:T(8,128)(2,1)S(1)} %get-tuple-element.26.after), channel_id=1, source_target_pairs={{0,63},{1,2},{2,1},{3,4},{4,3},{5,6},{6,5},{7,8},{8,7},{9,10},{10,... | collective-permute-start | bytes 98312 | tf_op jit(solution)/shard_map/ppermute | solution.py:568
  1.3 1.6 %collective-permute-start.1 = (bf16[128,128]{1,0:T(8,128)(2,1)S(1)}, bf16[128,128]{1,0:T(8,128)(2,1)S(1)}, u32[]{:S(2)}, u32[]{:S(2)}) collective-permute-start(bf16[128,128]{1,0:T(8,128)(2,1)S(1)} %get-tuple-element.27), channel_id=1, source_target_pairs={{0,1},{1,0},{2,3},{3,2},{4,5},{5,4},{6,7},{7,6},{8,9},{9,8},{10,11... | collective-permute-start | bytes 98312 | tf_op jit(solution)/shard_map/ppermute | solution.py:568
  2.1 0.8 %copy-start.2 = (bf16[256,1024]{1,0:T(8,128)(2,1)}, bf16[256,1024]{1,0:T(8,128)(2,1)S(1)}, u32[]{:S(2)}) copy-start(bf16[256,1024]{1,0:T(8,128)(2,1)S(1)} %get-tuple-element.34.air_marks_ref) | copy-start | bytes 1572868
  2.9 3.2 %copy-start.1 = (f32[128,1024]{1,0:T(8,128)}, f32[128,1024]{1,0:T(8,128)S(1)}, u32[]{:S(2)}) copy-start(f32[128,1024]{1,0:T(8,128)S(1)} %get-tuple-element.33.part_ref) | copy-start | bytes 1572868
  6.1 37.6 %all-to-all-start = ((bf16[16,4,24,128]{3,2,1,0:T(8,128)(2,1)}), bf16[16,4,24,128]{3,2,1,0:T(8,128)(2,1)S(1)}, u32[]{:S(2)}, u32[]{:S(2)}) async-start(bf16[16,4,24,128]{3,2,1,0:T(8,128)(2,1)} %get-tuple-element.32.after), calls=%async_computation | async-start | bytes 786432 | tf_op jit(solution)/shard_map/all_to_all | solution.py:644
  30.4 0.9 %copy-start = (f32[80,2048]{1,0:T(8,128)}, f32[80,2048]{1,0:T(8,128)S(1)}, u32[]{:S(2)}) copy-start(f32[80,2048]{1,0:T(8,128)S(1)} %get-tuple-element.42.sums_ref) | copy-start | bytes 1966084
  31.3 9.0 %collective-permute-start.2 = (bf16[80,128]{1,0:T(8,128)(2,1)S(1)}, bf16[80,128]{1,0:T(8,128)(2,1)S(1)}, u32[]{:S(2)}, u32[]{:S(2)}) collective-permute-start(bf16[80,128]{1,0:T(8,128)(2,1)S(1)} %get-tuple-element.44), channel_id=1, source_target_pairs={{512,575},{513,514},{514,513},{515,516},{516,515},{517,518},{518,5... | collective-permute-start | bytes 61448 | tf_op jit(solution)/shard_map/ppermute | solution.py:568
  38.0 5.7 %collective-permute-start.3 = (bf16[80,128]{1,0:T(8,128)(2,1)S(1)}, bf16[80,128]{1,0:T(8,128)(2,1)S(1)}, u32[]{:S(2)}, u32[]{:S(2)}) collective-permute-start(bf16[80,128]{1,0:T(8,128)(2,1)S(1)} %get-tuple-element.45), channel_id=1, source_target_pairs={{512,513},{513,512},{514,515},{515,514},{516,517},{517,516},{518,5... | collective-permute-start | bytes 61448 | tf_op jit(solution)/shard_map/ppermute | solution.py:568

commit v7 on v5

--- a/solution.py
+++ b/solution.py
@@ -63,13 +63,16 @@
     return lax.rem(lax.axis_index("dev"), 2) == 0
 
 
-def pack_into(state, send, first, second):
+def pack_into(state, send, first, second, parts=()):
     half = first.shape[1]
     rows = row_marks(TILE, 2 * half)
     index = send[...]
     total = None
     for base in range(0, state.shape[1], TILE):
-        part = dot(state[:, base : base + TILE].astype(BF16), marks_at([index], base, rows))
+        marks = marks_at([index], base, rows)
+        if parts:
+            parts[base // TILE].wait()
+        part = dot(state[:, base : base + TILE].astype(BF16), marks)
         total = part if total is None else total + part
     down = total[:, :half]
     up = total[:, half:]
@@ -104,8 +107,12 @@
 def air_pack_kernel(atm_groups, air_ref, send_ref, down, up, air, send, sems):
     @pl.when(lax.axis_index("grp") < atm_groups)
     def _():
-        wait_all(fetch_all([(send_ref, send), (air_ref, air)], sems))
-        pack_into(air, send, down, up)
+        pieces = [slice(at, at + TILE) for at in range(0, air.shape[1], TILE)]
+        listed, *parts = fetch_all(
+            [(send_ref, send)] + [(air_ref.at[:, at], air.at[:, at]) for at in pieces], sems
+        )
+        listed.wait()
+        pack_into(air, send, down, up, parts)
 
 
 def sums_of(pool, nbrs, at, width):
@@ -230,8 +237,8 @@
 def air_own_kernel(
     atm_groups,
     after, air_ref, air_nbrs_ref, air_mix_ref, counts_ref, flux_weight_ref, weights_ref,
-    part, marks, tiles, air_mix, flux_weight, weights,
-    air, air_nbrs, counts, ends, begins_at, ends_at, pool, sems,
+    part, marks, tiles, air_mix, flux_weight, weights, payload,
+    air, air_nbrs, counts, ends, begins_at, ends_at, pool, none, sems, out_sem,
 ):
     @pl.when(lax.axis_index("grp") < atm_groups)
     def _():
@@ -246,6 +253,8 @@
             ],
             sems,
         )
+        none[...] = jnp.zeros(none.shape, BF16)
+        cleared = fetch(none, payload.at[pl.ds(atm_groups, none.shape[0])], out_sem)
         amount, columns = air_nbrs.shape
         nbrs = [air_nbrs.at[k : k + 1, :] for k in range(amount)]
         many.wait()
@@ -262,24 +271,22 @@
             own = air[:, at : at + TILE]
             mix = air_mix[:, at : at + TILE]
             part[:, at : at + TILE] = own + mix * (total * (1.0 / amount) - own)
-        wait_all(rest)
+        wait_all([*rest, cleared])
 
 
 def mid_kernel(
     atm_groups, amount,
     first, second, part, marks, tiles, air_mix, flux_weight, weights, air_ref, owner_ref,
-    sea_ref, sea_send_ref, ret_weight_ref, recv_ref,
+    sea_ref, sea_send_ref, ret_weight_ref, recv_ref, payload_in,
     payload, air_out, sea_down_ref, sea_up_ref,
-    air, values, sent, owner, seen,
-    sea, sea_send, ret_weight, recv, returned, down, up, sems, out_sems,
+    air, values, sent, blocks, owner, seen,
+    sea, sea_send, ret_weight, recv, returned, down, up, sems, out_sems, block_sems,
 ):
     here = lax.axis_index("grp") < atm_groups
-    count_groups = sent.shape[0]
 
     @pl.when(here)
     def _():
         owned = fetch(owner_ref, owner, sems.at[0])
-        sent[...] = jnp.zeros(sent.shape, BF16)
         values[...] = jnp.zeros(values.shape, BF16)
         rim = rims(first, second)
         columns = air.shape[1]
@@ -294,7 +301,10 @@
         stored = fetch(air, air_out, out_sems.at[0])
         block = sent.shape[3]
         each = TILE // block
-        made = []
+        owned.wait()
+        places = []
+        slots_of(owner, seen, lambda b, o, k: places.append((o, k)))
+        copies = [stored]
         i = 0
         for p, near in spans(columns):
             both = None
@@ -304,16 +314,13 @@
                 both = more if both is None else both + more
                 i += 1
             tile = (both[0:fields] + both[32 : 32 + fields]) * weights[:, p * TILE : (p + 1) * TILE]
-            made.append(tile.astype(BF16))
-
-        def visit(b, o, k):
-            i = b % each
-            sent[o, k] = made[b // each][:, i * block : (i + 1) * block]
-
-        owned.wait()
-        slots_of(owner, seen, visit)
-        done = fetch(sent, payload.at[pl.ds(atm_groups, count_groups)], out_sems.at[1])
-        wait_all([stored, done])
+            tile = tile.astype(BF16)
+            for side in range(each):
+                b = p * each + side
+                o, k = places[b]
+                blocks[b] = tile[:, side * block : (side + 1) * block]
+                copies.append(fetch(blocks.at[b], payload.at[atm_groups + o, k], block_sems.at[b]))
+        wait_all(copies)
 
     @pl.when(jnp.logical_not(here))
     def _():
@@ -540,14 +547,14 @@
         out_shape=[air_rim] * 2,
         in_specs=[anywhere()] * 2,
         out_specs=[vmem(), vmem()],
-        scratch_shapes=[air_scratch, pair_in, dma((2,))],
+        scratch_shapes=[air_scratch, pair_in, dma((1 + columns // TILE,))],
         compiler_params=params,
         name="air_pack",
     )(air, in_hbm(atm_send.reshape(1, pair)))
     first = swapped(to_first, 0, atm_groups, 1)
     second = swapped(to_second, 0, atm_groups, 0)
 
-    part, marks, tiles, mix, flux_in, weights_here = pl.pallas_call(
+    part, marks, tiles, mix, flux_in, weights_here, payload_in = pl.pallas_call(
         functools.partial(air_own_kernel, atm_groups),
         out_shape=[
             air_shape,
@@ -556,9 +563,10 @@
             shape((1, columns), F32),
             shape((fields, levels_air), F32),
             shape((1, row_count), F32),
+            payload_shape,
         ],
         in_specs=[anywhere()] * 7,
-        out_specs=[vmem()] * 6,
+        out_specs=[vmem()] * 6 + [anywhere()],
         scratch_shapes=[
             air_scratch,
             scratch(amount_air, columns, dtype=I32),
@@ -567,7 +575,9 @@
             scratch(columns, 128, dtype=I16),
             scratch(columns, 128, dtype=I16),
             scratch(levels_air, columns, dtype=BF16),
+            scratch(groups - atm_groups, *sent_shape, dtype=BF16),
             dma((6,)),
+            dma,
         ],
         compiler_params=params,
         cost_estimate=pl.CostEstimate(flops=4 * 10**9, bytes_accessed=10**7, transcendentals=0),
@@ -579,12 +589,14 @@
     payload, air_next, sea_to_first, sea_to_second = pl.pallas_call(
         functools.partial(mid_kernel, atm_groups, amount_air),
         out_shape=[payload_shape, air_shape, sea_rim, sea_rim],
-        in_specs=[vmem()] * 8 + [anywhere()] * 6,
+        in_specs=[vmem()] * 8 + [anywhere()] * 7,
         out_specs=[anywhere()] * 4,
+        input_output_aliases={14: 0},
         scratch_shapes=[
             air_scratch,
             scratch(64, columns, dtype=BF16),
             scratch(atm_groups, *sent_shape, dtype=BF16),
+            scratch(blocks_here, fields, block, dtype=BF16),
             owner_in,
             pltpu.SMEM((groups - atm_groups,), I32),
             sea_scratch,
@@ -596,11 +608,12 @@
             sea_half,
             dma((5,)),
             dma((4,)),
+            dma((blocks_here,)),
         ],
         compiler_params=params,
         name="mid",
     )(
-        first, second, part, marks, tiles, mix, flux_in, weights_here, air, owner, sea, in_hbm(ocn_send.reshape(1, pair)), in_hbm(ret_weight), recv,
+        first, second, part, marks, tiles, mix, flux_in, weights_here, air, owner, sea, in_hbm(ocn_send.reshape(1, pair)), in_hbm(ret_weight), recv, payload_in,
     )
     arrived = lax.all_to_all(payload, "grp", split_axis=0, concat_axis=0, tiled=True)
     sea_first = swapped(sea_to_first, atm_groups, groups, 1)

time: 46.8 us -> 47.3 us (1.011)
  transfers between devices with their start and end apart: 5 -> 5, of which waited for: 1 -> 1; matrix products, arithmetic and copies ran while one was open for 0% -> 0% of each run, Pallas kernels for 11% -> 10%
where the time goes in v7:
time: 47.3 us; the launch traced here: 46.9 us
  starting transfers between devices  25 us (53%)
  waiting for transfers between devices  10.4 us (22%)
  Pallas kernels  10 us (21%)
  local copies, waits for them, and re-layouts  0.84 us (2%)
  between operations  0.72 us (2%)
    all_to_all x1, starting transfers between devices, on_device(): lax.all_to_all(payload, 'grp', split_axis=0, concat_axis=0, tiled=True)  12.7 us
    ppermute x4, starting transfers between devices, swapped(): return lax.ppermute(value, ('grp', 'dev'), pairs)  12.3 us
    all_to_all x1, waiting for transfers between devices, on_device(): lax.all_to_all(payload, 'grp', split_axis=0, concat_axis=0, tiled=True)  10.4 us
    pallas_call x1, Pallas kernels, on_device(): pl.pallas_call(functools.partial(air_own_kernel, atm_groups), out_shape=[...  2.92 us
    pallas_call x1, Pallas kernels, on_device(): pl.pallas_call(functools.partial(sea_own_kernel, atm_groups), out_shape=[...  1.98 us
    pallas_call x1, Pallas kernels, on_device(): pl.pallas_call(functools.partial(mid_kernel, atm_groups, amount_air), out...  1.89 us
    pallas_call x1, Pallas kernels, on_device(): pl.pallas_call(functools.partial(last_kernel, atm_groups, amount_sea), ou...  1.73 us
    pallas_call x1, Pallas kernels, on_device(): pl.pallas_call(functools.partial(air_pack_kernel, atm_groups), out_shape=...  1.5 us
  transfers between devices with their start and end apart: 5, of which 1 were waited for; matrix products, arithmetic and copies ran while one was open for 0% of the time, Pallas kernels for 10%

profile of v7, /device:TPU:1, one launch (start us, length us, event | category | flops | bytes accessed | tf_op | source)
XLA Modules:
  0.0 46.9 jit_solution(7256957783305039781)
XLA Ops:
  0.6 1.5 %air_pack.1 = (bf16[128,128]{1,0:T(8,128)(2,1)S(1)}, bf16[128,128]{1,0:T(8,128)(2,1)S(1)}) custom-call(f32[128,1024]{1,0:T(8,128)} %bitcast.21, s32[1,256]{1,0:T(1,128)} %bitcast.31), custom_call_target="tpu_custom_call" | custom-call | tf_op jit(solution)/shard_map/air_pack/pallas_call | solution.py:545
  2.1 9.0 %collective-permute-start = (bf16[128,128]{1,0:T(8,128)(2,1)S(1)}, bf16[128,128]{1,0:T(8,128)(2,1)S(1)}, u32[]{:S(2)}, u32[]{:S(2)}) collective-permute-start(bf16[128,128]{1,0:T(8,128)(2,1)S(1)} %get-tuple-element.23), channel_id=1, source_target_pairs={{0,63},{1,2},{2,1},{3,4},{4,3},{5,6},{6,5},{7,8},{8,7},{9,10},{10,... | collective-permute-start | bytes 98312 | tf_op jit(solution)/shard_map/ppermute | solution.py:543
  11.2 1.9 %collective-permute-start.1 = (bf16[128,128]{1,0:T(8,128)(2,1)S(1)}, bf16[128,128]{1,0:T(8,128)(2,1)S(1)}, u32[]{:S(2)}, u32[]{:S(2)}) collective-permute-start(bf16[128,128]{1,0:T(8,128)(2,1)S(1)} %get-tuple-element.24.after), channel_id=1, source_target_pairs={{0,1},{1,0},{2,3},{3,2},{4,5},{5,4},{6,7},{7,6},{8,9},{9,8},{10,11... | collective-permute-start | bytes 98312 | tf_op jit(solution)/shard_map/ppermute | solution.py:543
  13.1 2.9 %air_own.1 = (f32[128,1024]{1,0:T(8,128)S(1)}, bf16[256,1024]{1,0:T(8,128)(2,1)S(1)}, bf16[3072,256]{1,0:T(8,128)(2,1)S(1)}, f32[1,1024]{1,0:T(1,128)S(1)}, f32[...) custom-call(bf16[128,128]{1,0:T(8,128)(2,1)S(1)} %get-tuple-element.24.after, ...), custom_call_target="tpu_custom_call" | custom-call | flops 4000000000 | bytes 10000000 | tf_op jit(solution)/shard_map/air_own/pallas_call | solution.py:557
  16.0 0.0 collective-permute-done.first
  16.0 0.0 collective-permute-done.1.second
  16.1 1.9 %mid.1 = (bf16[16,4,24,128]{3,2,1,0:T(8,128)(2,1)}, f32[128,1024]{1,0:T(8,128)}, bf16[80,128]{1,0:T(8,128)(2,1)S(1)}, bf16[80,128]{1,0:T(8,128)(2,1)S(1)}) custom-call(bf16[128,128]{1,0:T(8,128)(2,1)S(1)} %collective-permute-done.first, bf16[128,128]{1,0:T(8,128)(2,1)S(1)} %collective-permute-done.1.second, ...), custom_call_target="tpu_custom_call", output_to_operand_aliasing={{0}: (14, {})} | custom-call | tf_op jit(solution)/shard_map/mid/pallas_call | solution.py:589
  18.0 12.7 %all-to-all-start = ((bf16[16,4,24,128]{3,2,1,0:T(8,128)(2,1)}), bf16[16,4,24,128]{3,2,1,0:T(8,128)(2,1)S(1)}, u32[]{:S(2)}, u32[]{:S(2)}) async-start(bf16[16,4,24,128]{3,2,1,0:T(8,128)(2,1)} %get-tuple-element.33.after), calls=%async_computation | async-start | bytes 786432 | tf_op jit(solution)/shard_map/all_to_all | solution.py:618
  30.7 0.7 %collective-permute-start.2 = (bf16[80,128]{1,0:T(8,128)(2,1)S(1)}, bf16[80,128]{1,0:T(8,128)(2,1)S(1)}, u32[]{:S(2)}, u32[]{:S(2)}) collective-permute-start(bf16[80,128]{1,0:T(8,128)(2,1)S(1)} %get-tuple-element.38), channel_id=1, source_target_pairs={{512,575},{513,514},{514,513},{515,516},{516,515},{517,518},{518,5... | collective-permute-start | bytes 61448 | tf_op jit(solution)/shard_map/ppermute | solution.py:543
  31.3 0.7 %collective-permute-start.3 = (bf16[80,128]{1,0:T(8,128)(2,1)S(1)}, bf16[80,128]{1,0:T(8,128)(2,1)S(1)}, u32[]{:S(2)}, u32[]{:S(2)}) collective-permute-start(bf16[80,128]{1,0:T(8,128)(2,1)S(1)} %get-tuple-element.39), channel_id=1, source_target_pairs={{512,513},{513,512},{514,515},{515,514},{516,517},{517,516},{518,5... | collective-permute-start | bytes 61448 | tf_op jit(solution)/shard_map/ppermute | solution.py:543
  32.0 2.0 %sea_own.1 = (f32[80,2048]{1,0:T(8,128)S(1)}, bf16[256,2048]{1,0:T(8,128)(2,1)S(1)}, f32[80,2048]{1,0:T(8,128)}, bf16[3072,256]{1,0:T(8,128)(2,1)S(1)}, f32[1,1536]{1,0:T(1,128)S(1)}) custom-call(bf16[16,4,24,128]{3,2,1,0:T(8,128)(2,1)} %get-tuple-element.33.after, f32[80,2048]{1,0:T(8,128)} %bitcast.19, s32[6,1,2048]{2,1,0:T(1,128)} %bitcast.34, ...), custom_call_target="tpu_custom_call" | custom-call | flops 8000000000 | bytes 10000000 | tf_op jit(solution)/shard_map/sea_own/pallas_call | solution.py:622
  34.0 0.0 copy-start
  34.0 0.8 %copy-done = f32[80,2048]{1,0:T(8,128)} copy-done((f32[80,2048]{1,0:T(8,128)}, f32[80,2048]{1,0:T(8,128)S(1)}, u32[]{:S(2)}) %copy-start) | copy-done | bytes 655384
  34.8 0.0 collective-permute-done.2.first
  34.8 0.0 collective-permute-done.3.second
  34.8 10.4 %all-to-all-done.arrived = bf16[16,4,24,128]{3,2,1,0:T(8,128)(2,1)S(1)} async-done(((bf16[16,4,24,128]{3,2,1,0:T(8,128)(2,1)}), bf16[16,4,24,128]{3,2,1,0:T(8,128)(2,1)S(1)}, u32[]{:S(2)}, u32[]{:S(2)}) %all-to-all-start) | async-done | bytes 393248 | tf_op jit(solution)/shard_map/all_to_all | solution.py:618
  45.2 1.7 %last.1 = (f32[80,2048]{1,0:T(8,128)}, f32[12,1,1024]{2,1,0:T(1,128)}) custom-call(bf16[16,4,24,128]{3,2,1,0:T(8,128)(2,1)S(1)} %all-to-all-done.arrived, bf16[3072,256]{1,0:T(8,128)(2,1)S(1)} %get-tuple-element.34.tiles, f32[1,1536]{1,0:T(1,128)S(1)} %get-tuple-element.35.weights, s32[1,12]{1,0:T(1,128)} %bitcast.30, ...), custom_call_target="tpu_custom_call", output_to_operand_aliasing={{0}: (12, {})} | custom-call | tf_op jit(solution)/shard_map/last/pallas_call | solution.py:648
Async XLA Ops:
  2.1 13.9 %collective-permute-start = (bf16[128,128]{1,0:T(8,128)(2,1)S(1)}, bf16[128,128]{1,0:T(8,128)(2,1)S(1)}, u32[]{:S(2)}, u32[]{:S(2)}) collective-permute-start(bf16[128,128]{1,0:T(8,128)(2,1)S(1)} %get-tuple-element.23), channel_id=1, source_target_pairs={{0,63},{1,2},{2,1},{3,4},{4,3},{5,6},{6,5},{7,8},{8,7},{9,10},{10,... | collective-permute-start | bytes 98312 | tf_op jit(solution)/shard_map/ppermute | solution.py:543
  11.2 4.9 %collective-permute-start.1 = (bf16[128,128]{1,0:T(8,128)(2,1)S(1)}, bf16[128,128]{1,0:T(8,128)(2,1)S(1)}, u32[]{:S(2)}, u32[]{:S(2)}) collective-permute-start(bf16[128,128]{1,0:T(8,128)(2,1)S(1)} %get-tuple-element.24.after), channel_id=1, source_target_pairs={{0,1},{1,0},{2,3},{3,2},{4,5},{5,4},{6,7},{7,6},{8,9},{9,8},{10,11... | collective-permute-start | bytes 98312 | tf_op jit(solution)/shard_map/ppermute | solution.py:543
  18.0 27.3 %all-to-all-start = ((bf16[16,4,24,128]{3,2,1,0:T(8,128)(2,1)}), bf16[16,4,24,128]{3,2,1,0:T(8,128)(2,1)S(1)}, u32[]{:S(2)}, u32[]{:S(2)}) async-start(bf16[16,4,24,128]{3,2,1,0:T(8,128)(2,1)} %get-tuple-element.33.after), calls=%async_computation | async-start | bytes 786432 | tf_op jit(solution)/shard_map/all_to_all | solution.py:618
  30.7 4.2 %collective-permute-start.2 = (bf16[80,128]{1,0:T(8,128)(2,1)S(1)}, bf16[80,128]{1,0:T(8,128)(2,1)S(1)}, u32[]{:S(2)}, u32[]{:S(2)}) collective-permute-start(bf16[80,128]{1,0:T(8,128)(2,1)S(1)} %get-tuple-element.38), channel_id=1, source_target_pairs={{512,575},{513,514},{514,513},{515,516},{516,515},{517,518},{518,5... | collective-permute-start | bytes 61448 | tf_op jit(solution)/shard_map/ppermute | solution.py:543
  31.3 3.5 %collective-permute-start.3 = (bf16[80,128]{1,0:T(8,128)(2,1)S(1)}, bf16[80,128]{1,0:T(8,128)(2,1)S(1)}, u32[]{:S(2)}, u32[]{:S(2)}) collective-permute-start(bf16[80,128]{1,0:T(8,128)(2,1)S(1)} %get-tuple-element.39), channel_id=1, source_target_pairs={{512,513},{513,512},{514,515},{515,514},{516,517},{517,516},{518,5... | collective-permute-start | bytes 61448 | tf_op jit(solution)/shard_map/ppermute | solution.py:543
  34.0 0.8 %copy-start = (f32[80,2048]{1,0:T(8,128)}, f32[80,2048]{1,0:T(8,128)S(1)}, u32[]{:S(2)}) copy-start(f32[80,2048]{1,0:T(8,128)S(1)} %get-tuple-element.36.sums_ref) | copy-start | bytes 1966084
